TPU v7x, 32 devices: a whole 2x2x4 slice. The times are simulated.
32 devices in a mesh: fsdp: 4 (over y, core), dp: 2 (over x), seq: 4 (over z).
Axes of the slice: x: 2, y: 2, z: 4, core: 2. Of those that a mesh axis runs over, the one named last changes fastest.
Arguments:
- tokens: bfloat16 [8, 2560, 1024], P(('fsdp', 'dp'), 'seq'), may hold values from -6 to 6
- qkv_weight: bfloat16 [1024, 3072], P('fsdp'), may hold values from -0.1875 to 0.1875
- out_weight: bfloat16 [1024, 1024], P('fsdp'), may hold values from -0.1875 to 0.1875
- up_weight: bfloat16 [1024, 4096], P('fsdp'), may hold values from -0.1875 to 0.1875
- down_weight: bfloat16 [4096, 1024], P('fsdp'), may hold values from -0.09375 to 0.09375
- norm_gain: float32 [4, 1024], replicated, may hold values from 0.5 to 1.5
- norm_bias: float32 [4, 1024], replicated, may hold values from -1.75 to 1.75
- caption_len: int32 [8, 2], P(('fsdp', 'dp')), may hold values from 5 to 64, as said below
- item_start: int32 [8, 2], P(('fsdp', 'dp')), may hold values from 0 to 1531, as said below
- grad_out: bfloat16 [8, 2560, 1024], P(('fsdp', 'dp'), 'seq'), may hold values from -6 to 6
Outputs:
- block_out: bfloat16 [8, 2560, 1024], P(('fsdp', 'dp'), 'seq')
- grad_in: bfloat16 [8, 2560, 1024], P(('fsdp', 'dp'), 'seq')
- grad_qkv: float32 [1024, 3072], P('fsdp')
- grad_proj: float32 [1024, 1024], P('fsdp')
- grad_up: float32 [1024, 4096], P('fsdp')
- grad_down: float32 [4096, 1024], P('fsdp')
- grad_gain: float32 [4, 1024], replicated
- grad_bias: float32 [4, 1024], replicated
Inputs may be any that keep to these rules, and one draw needn't show every extreme that they name: `caption_len`: caption tokens of each item; item j of a row covers positions item_start[j] to item_start[j] + caption_len[j] + 1023 of that row. `item_start`: item j of a row starts at or after j * 1280 and ends before (j + 1) * 1280; positions outside every item are padding.
All inputs are finite; a program needn't handle non-finite values.
Results may differ from a plain program's by a relative error of at most 0.018.
Values may be sent and summed in bfloat16 or wider, within the bound.
A program may use at most 192 MiB of HBM per device.

v0:
```python
import jax
import jax.numpy as jnp
from jax import lax
from jax.sharding import PartitionSpec as P

H = 16
HD = 64
IMAGE = 1024


def layer_norm(values, gain_row, bias_row):
    middle = jnp.mean(values, axis=-1, keepdims=True)
    centred = values - middle
    spread = jnp.mean(centred * centred, axis=-1, keepdims=True)
    return centred * lax.rsqrt(spread + 1e-05) * gain_row + bias_row


def tanh_gelu(values):
    return jax.nn.gelu(values, approximate=True)


def segment_ids(positions, captions, starts):
    finish = starts + captions + IMAGE
    inside = (positions[:, None] >= starts[None, :]) & (positions[:, None] < finish[None, :])
    labels = jnp.arange(1, captions.shape[0] + 1, dtype=jnp.int32)
    return jnp.sum(jnp.where(inside, labels[None, :], 0), axis=-1)


def split_heads(matrix):
    return matrix.reshape(matrix.shape[0], H, HD).transpose(1, 0, 2)


def join_heads(stacked):
    return stacked.transpose(1, 0, 2).reshape(stacked.shape[1], H * HD)


def head_scores(query_head, key_head, allowed):
    raw_scores = jnp.einsum(
        "qd,kd->qk", query_head / 32, key_head, preferred_element_type=jnp.float32
    )
    return jnp.where(allowed, raw_scores / 8.0, -1e30)


def head_forward(pieces, allowed):
    query_head, key_head, value_head = pieces
    scaled = head_scores(query_head, key_head, allowed)
    row_max = jnp.max(scaled, axis=-1)
    weights = jnp.exp((scaled - row_max[:, None]) * 32.0)
    row_sum = jnp.sum(weights, axis=-1)
    attn_probs = (weights / row_sum[:, None]).astype(jnp.bfloat16)
    mixed_head = jnp.dot(attn_probs, value_head, preferred_element_type=jnp.float32)
    return (mixed_head, row_max, row_sum)


def head_backward(pieces, allowed):
    query_head, key_head, value_head, grad_head, row_max, row_sum = pieces
    scaled = head_scores(query_head, key_head, allowed)
    attn_probs = jnp.exp((scaled - row_max[:, None]) * 32.0) / row_sum[:, None]
    grad_probs = jnp.einsum("qd,kd->qk", grad_head, value_head, preferred_element_type=jnp.float32)
    inner_sum = jnp.sum(attn_probs * grad_probs, axis=-1, keepdims=True)
    grad_raw = (4.0 * attn_probs * (grad_probs - inner_sum)).astype(jnp.bfloat16)
    grad_query = jnp.dot(grad_raw, key_head, preferred_element_type=jnp.float32) / 32.0
    grad_key = jnp.einsum(
        "qk,qd->kd", grad_raw, query_head / 32, preferred_element_type=jnp.float32
    )
    grad_value = jnp.einsum(
        "qk,qd->kd", attn_probs.astype(jnp.bfloat16), grad_head, preferred_element_type=jnp.float32
    )
    return (grad_query, grad_key, grad_value)


def local(
    tokens,
    qkv_weight,
    out_weight,
    up_weight,
    down_weight,
    norm_gain,
    norm_bias,
    caption_len,
    item_start,
    grad_out,
):
    inputs = tokens[0].astype(jnp.float32)
    local_rows = inputs.shape[0]
    model_width = inputs.shape[1]
    row_length = local_rows * lax.axis_size("seq")
    seq_index = lax.axis_index("seq")
    query_pos = seq_index * local_rows + jnp.arange(local_rows, dtype=jnp.int32)
    key_pos = jnp.arange(row_length, dtype=jnp.int32)
    query_seg = segment_ids(query_pos, caption_len[0], item_start[0])
    key_seg = segment_ids(key_pos, caption_len[0], item_start[0])
    allowed = (query_seg[:, None] == key_seg[None, :]) & (key_pos[None, :] <= query_pos[:, None])
    qkv_full, out_full, up_full, down_full = (
        lax.all_gather(qkv_weight, "fsdp", axis=0, tiled=True),
        lax.all_gather(out_weight, "fsdp", axis=0, tiled=True),
        lax.all_gather(up_weight, "fsdp", axis=0, tiled=True),
        lax.all_gather(down_weight, "fsdp", axis=0, tiled=True),
    )
    normed_one = layer_norm(inputs, norm_gain[0], norm_bias[0]).astype(jnp.bfloat16)
    projected = jnp.dot(normed_one, qkv_full, preferred_element_type=jnp.float32)
    queries = projected[:, :model_width].astype(jnp.bfloat16)
    key_rows = projected[:, model_width : 2 * model_width].astype(jnp.bfloat16)
    value_rows = projected[:, 2 * model_width :].astype(jnp.bfloat16)
    keys_all, values_all = (
        lax.all_gather(key_rows, "seq", axis=0, tiled=True),
        lax.all_gather(value_rows, "seq", axis=0, tiled=True),
    )
    query_heads = split_heads(queries)
    key_heads = split_heads(keys_all)
    value_heads = split_heads(values_all)
    mixed_heads, row_max, row_sum = lax.map(
        lambda pieces: head_forward(pieces, allowed), (query_heads, key_heads, value_heads)
    )
    attended = join_heads(mixed_heads).astype(jnp.bfloat16)
    branch = jnp.dot(attended, out_full, preferred_element_type=jnp.float32)
    middle = inputs + layer_norm(branch, norm_gain[1], norm_bias[1])
    normed_two = layer_norm(middle, norm_gain[2], norm_bias[2]).astype(jnp.bfloat16)
    hidden = jnp.dot(normed_two, up_full, preferred_element_type=jnp.float32)
    activated = tanh_gelu(hidden).astype(jnp.bfloat16)
    feed_out = jnp.dot(activated, down_full, preferred_element_type=jnp.float32)
    block_out = middle + layer_norm(feed_out, norm_gain[3], norm_bias[3])
    upstream = grad_out[0].astype(jnp.float32)
    unused_four, back_four = jax.vjp(layer_norm, feed_out, norm_gain[3], norm_bias[3])
    grad_feed, gain_four, bias_four = back_four(upstream)
    grad_feed = grad_feed.astype(jnp.bfloat16)
    qkv_back, out_back, up_back, down_back = (
        lax.all_gather(qkv_weight, "fsdp", axis=0, tiled=True),
        lax.all_gather(out_weight, "fsdp", axis=0, tiled=True),
        lax.all_gather(up_weight, "fsdp", axis=0, tiled=True),
        lax.all_gather(down_weight, "fsdp", axis=0, tiled=True),
    )
    grad_act = jnp.einsum("rd,fd->rf", grad_feed, down_back, preferred_element_type=jnp.float32)
    grad_down = jnp.einsum("rf,rd->fd", activated, grad_feed, preferred_element_type=jnp.float32)
    unused_gelu, gelu_back = jax.vjp(tanh_gelu, hidden)
    grad_hidden = gelu_back(grad_act)[0].astype(jnp.bfloat16)
    grad_normed_two = jnp.einsum(
        "rf,df->rd", grad_hidden, up_back, preferred_element_type=jnp.float32
    )
    grad_up = jnp.einsum("rd,rf->df", normed_two, grad_hidden, preferred_element_type=jnp.float32)
    unused_three, back_three = jax.vjp(layer_norm, middle, norm_gain[2], norm_bias[2])
    grad_mid_part, gain_three, bias_three = back_three(grad_normed_two)
    grad_middle = upstream + grad_mid_part
    unused_two, back_two = jax.vjp(layer_norm, branch, norm_gain[1], norm_bias[1])
    grad_branch, gain_two, bias_two = back_two(grad_middle)
    grad_branch = grad_branch.astype(jnp.bfloat16)
    grad_attended = jnp.einsum(
        "rj,ij->ri", grad_branch, out_back, preferred_element_type=jnp.float32
    ).astype(jnp.bfloat16)
    grad_proj = jnp.einsum("ri,rj->ij", attended, grad_branch, preferred_element_type=jnp.float32)
    grad_query, grad_key, grad_value = lax.map(
        lambda pieces: head_backward(pieces, allowed),
        (query_heads, key_heads, value_heads, split_heads(grad_attended), row_max, row_sum),
    )
    grad_keys_all = join_heads(grad_key)
    grad_values_all = join_heads(grad_value)
    key_part, value_part = (
        lax.psum_scatter(
            grad_keys_all.astype(jnp.bfloat16), "seq", scatter_dimension=0, tiled=True
        ).astype(jnp.float32),
        lax.psum_scatter(
            grad_values_all.astype(jnp.bfloat16), "seq", scatter_dimension=0, tiled=True
        ).astype(jnp.float32),
    )
    grad_projected = jnp.concatenate(
        [
            join_heads(grad_query).astype(jnp.bfloat16),
            key_part.astype(jnp.bfloat16),
            value_part.astype(jnp.bfloat16),
        ],
        axis=1,
    )
    grad_normed_one = jnp.einsum(
        "rc,dc->rd", grad_projected, qkv_back, preferred_element_type=jnp.float32
    )
    grad_qkv = jnp.einsum(
        "rd,rc->dc", normed_one, grad_projected, preferred_element_type=jnp.float32
    )
    unused_one, back_one = jax.vjp(layer_norm, inputs, norm_gain[0], norm_bias[0])
    grad_inputs, gain_one, bias_one = back_one(grad_normed_one)
    grad_in = grad_middle + grad_inputs
    shards = (
        lax.psum_scatter(
            grad_qkv.astype(jnp.bfloat16), "fsdp", scatter_dimension=0, tiled=True
        ).astype(jnp.float32),
        lax.psum_scatter(
            grad_proj.astype(jnp.bfloat16), "fsdp", scatter_dimension=0, tiled=True
        ).astype(jnp.float32),
        lax.psum_scatter(
            grad_up.astype(jnp.bfloat16), "fsdp", scatter_dimension=0, tiled=True
        ).astype(jnp.float32),
        lax.psum_scatter(
            grad_down.astype(jnp.bfloat16), "fsdp", scatter_dimension=0, tiled=True
        ).astype(jnp.float32),
    )
    reduced = (
        lax.psum(shards[0].astype(jnp.bfloat16), ("dp", "seq")).astype(jnp.float32),
        lax.psum(shards[1].astype(jnp.bfloat16), ("dp", "seq")).astype(jnp.float32),
        lax.psum(shards[2].astype(jnp.bfloat16), ("dp", "seq")).astype(jnp.float32),
        lax.psum(shards[3].astype(jnp.bfloat16), ("dp", "seq")).astype(jnp.float32),
    )
    gain_stack = jnp.stack([gain_one, gain_two, gain_three, gain_four])
    bias_stack = jnp.stack([bias_one, bias_two, bias_three, bias_four])
    gain_total, bias_total = lax.psum((gain_stack, bias_stack), ("fsdp", "dp", "seq"))
    return (
        block_out.astype(jnp.bfloat16)[None],
        grad_in.astype(jnp.bfloat16)[None],
        reduced[0],
        reduced[1],
        reduced[2],
        reduced[3],
        gain_total,
        bias_total,
    )


def solution(mesh):
    return jax.shard_map(
        local,
        mesh=mesh,
        in_specs=(
            P(("fsdp", "dp"), "seq", None),
            P("fsdp", None),
            P("fsdp", None),
            P("fsdp", None),
            P("fsdp", None),
            P(),
            P(),
            P(("fsdp", "dp"), None),
            P(("fsdp", "dp"), None),
            P(("fsdp", "dp"), "seq", None),
        ),
        out_specs=(
            P(("fsdp", "dp"), "seq", None),
            P(("fsdp", "dp"), "seq", None),
            P("fsdp", None),
            P("fsdp", None),
            P("fsdp", None),
            P("fsdp", None),
            P(),
            P(),
        ),
        check_vma=False,
    )
```

profile of v0, /device:TPU:0, one launch (start us, length us, event | category | flops | bytes accessed | tf_op | source)
XLA Modules:
  0.0 1379.7 jit_solution(4149271503799129467)
XLA Ops:
  10.7 48.0 %all-gather.7.cloned.1.call-done = bf16[1024,3072]{1,0:T(8,128)(2,1)} async-done(((bf16[256,3072]{1,0:T(8,128)(2,1)}), bf16[1024,3072]{1,0:T(8,128)(2,1)}) %all-gather.7.cloned.1.call-update) | async-done | bytes 6291472 | tf_op jit(solution)/shard_map/all_gather | solution.py:95
  58.7 7.5 convolution_convert_fusion.3
  74.7 91.7 %all-gather.9.cloned.1.call-done = bf16[2560,1024]{1,0:T(8,128)(2,1)} async-done(((bf16[640,1024]{1,0:T(8,128)(2,1)}), bf16[2560,1024]{1,0:T(8,128)(2,1)}) %all-gather.9.cloned.1.call-update) | async-done | bytes 5242896 | tf_op jit(solution)/shard_map/all_gather | solution.py:106
  166.4 7.7 copy.45
  174.1 10.3 copy.48
  184.4 80.6 %all-gather.11.cloned.1.call-done = bf16[2560,1024]{1,0:T(8,128)(2,1)} async-done(((bf16[640,1024]{1,0:T(8,128)(2,1)}), bf16[2560,1024]{1,0:T(8,128)(2,1)}) %all-gather.11.cloned.1.call-update) | async-done | bytes 5242896 | tf_op jit(solution)/shard_map/all_gather | solution.py:107
  265.0 7.8 copy.46
  272.8 10.2 copy.49
  283.2 115.8 %while.30 = (s32[]{:T(128)}, bf16[16,640,64]{1,2,0:T(8,128)(2,1)S(1)}, f32[16,640]{1,0:T(8,128)S(1)}, f32[16,640]{1,0:T(8,128)S(1)}, bf16[16,640,64]{2,1,0:T(8,1...) while((s32[]{:T(128)}, ...), condition=%wide.region_7.8_spmd.clone, body=%wide.region_4.7_spmd.clone.sunk | while | flops 440769280 | bytes 21353092 | solution.py:112
  283.2 3.1 fusion.137
  290.4 3.1 fusion.137
  297.7 3.2 fusion.137
  305.1 3.1 fusion.137
  312.3 3.1 fusion.137
  319.5 3.1 fusion.137
  326.8 3.0 fusion.137
  334.0 3.1 fusion.137
  341.2 3.1 fusion.137
  348.4 3.1 fusion.137
  355.6 3.2 fusion.137
  362.9 3.1 fusion.137
  370.1 3.1 fusion.137
  377.3 3.1 fusion.137
  384.5 3.1 fusion.137
  391.8 3.1 fusion.137
  400.0 3.7 fusion.104
  407.9 11.6 fusion.91
  419.5 13.1 fusion.105
  439.2 16.5 %fusion.55 = bf16[640,4096]{1,0:T(8,128)(2,1)} fusion(f32[640,4096]{1,0:T(8,128)} %fusion.91, bf16[4096,1024]{1,0:T(8,128)(2,1)} %all-gather.17.cloned.1.call-done, f32[640,1024]{1,0:T(8,128)S(1)} %get-tuple-element.312, f32[640]{0:T(1024)S(1)} %negate_multiply_fusion.3), kind=kOutput, calls=%fused_computation.69 | convolution fusion | flops 5422448640 | bytes 26741248 | tf_op jit(solution)/shard_map/rd,fd->rf/dot_general | solution.py:133
  455.7 11.2 multiply_reduce_fusion.1
  476.1 226.0 %while.31 = (s32[]{:T(128)}, bf16[16,640,64]{1,2,0:T(8,128)(2,1)}, bf16[16,2560,64]{1,2,0:T(8,128)(2,1)}, bf16[16,2560,64]{1,2,0:T(8,128)(2,1)}, bf16[16,640,64]...) while((s32[]{:T(128)}, bf16[16,640,64]{1,2,0:T(8,128)(2,1)}, ...), condition=%wide.region_22.23_spmd.clone, body=%wide.region_20.22_spmd.clone.sunk | while | flops 1073274240 | bytes 53125264 | solution.py:151
  478.4 4.4 multiply_reduce_fusion.9
  492.5 4.4 multiply_reduce_fusion.9
  506.6 4.4 multiply_reduce_fusion.9
  520.7 4.4 multiply_reduce_fusion.9
  534.8 4.4 multiply_reduce_fusion.9
  549.0 4.4 multiply_reduce_fusion.9
  563.1 4.4 multiply_reduce_fusion.9
  577.2 4.4 multiply_reduce_fusion.9
  591.3 4.4 multiply_reduce_fusion.9
  605.4 4.4 multiply_reduce_fusion.9
  619.5 4.4 multiply_reduce_fusion.9
  626.2 2.9 fusion.149
  633.6 4.4 multiply_reduce_fusion.9
  647.7 4.4 multiply_reduce_fusion.9
  661.8 4.4 multiply_reduce_fusion.9
  676.0 4.4 multiply_reduce_fusion.9
  690.1 4.4 multiply_reduce_fusion.9
  702.0 8.0 copy.57
  710.1 8.0 copy.55
  719.3 4.9 convolution_convert_fusion.4
  724.4 13.8 convolution_convert_fusion.1
  739.9 11.7 convolution_convert_fusion
  751.7 50.6 %reduce-scatter.21.cloned.1.call-done = bf16[640,1024]{1,0:T(8,128)(2,1)} async-done(((bf16[2560,1024]{1,0:T(8,128)(2,1)}), bf16[640,1024]{1,0:T(8,128)(2,1)}) %reduce-scatter.21.cloned.1.call-update) | async-done | bytes 1310736
  804.3 94.6 %reduce-scatter.19.cloned.1.call-done = bf16[640,1024]{1,0:T(8,128)(2,1)} async-done(((bf16[2560,1024]{1,0:T(8,128)(2,1)}), bf16[640,1024]{1,0:T(8,128)(2,1)}) %reduce-scatter.19.cloned.1.call-update) | async-done | bytes 1310736
  901.3 9.9 convolution_convert_fusion.2
  911.6 22.4 %reduce-scatter.13.cloned.1.call-done = bf16[256,1024]{1,0:T(8,128)(2,1)} async-done(((bf16[1024,1024]{1,0:T(8,128)(2,1)}), bf16[256,1024]{1,0:T(8,128)(2,1)}) %reduce-scatter.13.cloned.1.call-update) | async-done | bytes 524304 | tf_op jit(solution)/shard_map/reduce_scatter | solution.py:186
  934.0 74.3 %reduce-scatter.17.cloned.1.call-done = bf16[1024,1024]{1,0:T(8,128)(2,1)} async-done(((bf16[4096,1024]{1,0:T(8,128)(2,1)}), bf16[1024,1024]{1,0:T(8,128)(2,1)}) %reduce-scatter.17.cloned.1.call-update) | async-done | bytes 2097168 | tf_op jit(solution)/shard_map/reduce_scatter | solution.py:192
  1008.3 74.3 %reduce-scatter.15.cloned.1.call-done = bf16[256,4096]{1,0:T(8,128)(2,1)} async-done(((bf16[1024,4096]{1,0:T(8,128)(2,1)}), bf16[256,4096]{1,0:T(8,128)(2,1)}) %reduce-scatter.15.cloned.1.call-update) | async-done | bytes 2097168 | tf_op jit(solution)/shard_map/reduce_scatter | solution.py:189
  1082.6 61.0 %reduce-scatter.11.cloned.1.call-done = bf16[256,3072]{1,0:T(8,128)(2,1)} async-done(((bf16[1024,3072]{1,0:T(8,128)(2,1)}), bf16[256,3072]{1,0:T(8,128)(2,1)}) %reduce-scatter.11.cloned.1.call-update) | async-done | bytes 1572880 | tf_op jit(solution)/shard_map/reduce_scatter | solution.py:183
  1145.2 8.8 fusion.93
  1156.7 43.0 %all-reduce = (f32[4,1024]{1,0:T(4,128)}, f32[4,1024]{1,0:T(4,128)}) all-reduce(f32[4,1024]{1,0:T(4,128)S(1)} %get-tuple-element.339, f32[4,1024]{1,0:T(4,128)S(1)} %get-tuple-element.340), channel_id=1, replica_groups=mesh['fsdp'=4,'dp'=2,'seq'=4] {'fsdp','dp','seq'}, use_global_device_ids=true, to_apply=%region_39.40 | all-reduce | flops 8192 | bytes 65536 | tf_op jit(solution)/shard_map/psum | solution.py:204
  1199.7 3.8 fusion.78
  1203.6 159.9 %all-reduce.4.cloned.1.call-done = (bf16[256,3072]{1,0:T(8,128)(2,1)}, bf16[256,1024]{1,0:T(8,128)(2,1)}, bf16[256,4096]{1,0:T(8,128)(2,1)}, bf16[1024,1024]{1,0:T(8,128)(2,1)}) async-done(((bf16[256,3072]{1,0:T(8,128)(2,1)}, bf16[256,1024]{1,0:T(8,128)(2,1)}, bf16[256,4096]{1,0:T(8,128)(2,1)}, bf16[1024,1024]{1,0:T(8,128)(2,1)}), (bf16[256,3072]{1,0:T(8,128)(2,1)}, bf16[256,1024]{1,0:T(8,128)(2,1)}, ...) | async-done | bytes 6291472 | tf_op jit(solution)/shard_map/psum | solution.py:197
  (370 shorter events, 271.9 us)
Async XLA Ops:
  7.2 2.4 copy-start.3
  7.2 3.5 copy-start.36
  7.2 3.5 copy-start.37
  7.2 51.5 %all-gather.7.cloned.1.call-start = ((), (), s32[]{:S(2)}) async-start(), calls=%async_computation.6 | async-start | bytes 7864320 | tf_op jit(solution)/shard_map/all_gather | solution.py:95
  7.9 158.5 %all-gather.9.cloned.1.call-start = ((), (), s32[]{:S(2)}) async-start(), calls=%async_computation.7 | async-start | bytes 6553600 | tf_op jit(solution)/shard_map/all_gather | solution.py:106
  9.6 49.2 %copy-start.19 = (f32[640]{0:T(1024)}, f32[640]{0:T(1024)S(1)}, u32[]{:S(2)}) copy-start(f32[640]{0:T(1024)S(1)} %broadcast_multiply_fusion.3) | copy-start | bytes 7684
  10.0 0.6 copy-start.27
  10.6 48.1 %copy-start.23 = (f32[640]{0:T(1024)}, f32[640]{0:T(1024)S(1)}, u32[]{:S(2)}) copy-start(f32[640]{0:T(1024)S(1)} %fusion.81) | copy-start | bytes 7684
  10.7 48.0 %copy-start.25 = (f32[1,1024]{1,0:T(1,128)}, f32[1,1024]{1,0:T(1,128)S(1)}, u32[]{:S(2)}) copy-start(f32[1,1024]{1,0:T(1,128)S(1)} %get-tuple-element.327) | copy-start | bytes 12292
  10.7 456.2 %copy-start.33 = (f32[1,1024]{1,0:T(1,128)}, f32[1,1024]{1,0:T(1,128)S(1)}, u32[]{:S(2)}) copy-start(f32[1,1024]{1,0:T(1,128)S(1)} %get-tuple-element.328) | copy-start | bytes 12292
  10.7 55.5 %copy-start.42 = (f32[1,1024]{1,0:T(1,128)}, f32[1,1024]{1,0:T(1,128)S(1)}, u32[]{:S(2)}) copy-start(f32[1,1024]{1,0:T(1,128)S(1)} %get-tuple-element.331) | copy-start | bytes 12292
  10.7 397.1 %copy-start.44 = (f32[1,1024]{1,0:T(1,128)}, f32[1,1024]{1,0:T(1,128)S(1)}, u32[]{:S(2)}) copy-start(f32[1,1024]{1,0:T(1,128)S(1)} %get-tuple-element.332) | copy-start | bytes 12292
  68.2 196.8 %all-gather.11.cloned.1.call-start = ((), (), s32[]{:S(2)}) async-start(), calls=%async_computation.8 | async-start | bytes 6553600 | tf_op jit(solution)/shard_map/all_gather | solution.py:107
  68.9 2.1 copy-start.46
  68.9 2.1 copy-start.47
  68.9 330.1 %all-gather.13.cloned.1.call-start = ((), (), s32[]{:S(2)}) async-start(), calls=%async_computation.9 | async-start | bytes 2621440 | tf_op jit(solution)/shard_map/all_gather | solution.py:96
  69.5 338.3 %all-gather.15.cloned.1.call-start = ((), (), s32[]{:S(2)}) async-start(), calls=%async_computation.10 | async-start | bytes 10485760 | tf_op jit(solution)/shard_map/all_gather | solution.py:97
  70.1 349.4 %all-gather.17.cloned.1.call-start = ((), (), s32[]{:S(2)}) async-start(), calls=%async_computation.11 | async-start | bytes 10485760 | tf_op jit(solution)/shard_map/all_gather | solution.py:98
  70.7 731.6 %reduce-scatter.21.cloned.1.call-start = ((), (), s32[]{:S(2)}) async-start(), calls=%async_computation.17 | async-start | bytes 6553600
  399.0 1.1 copy-start.10
  403.7 1.3 copy-start.4
  405.9 1.5 copy-start
  405.9 61.0 %copy-start.21 = (f32[640]{0:T(1024)}, f32[640]{0:T(1024)S(1)}, u32[]{:S(2)}) copy-start(f32[640]{0:T(1024)S(1)} %broadcast_multiply_fusion.1) | copy-start | bytes 7684
  407.8 59.1 %copy-start.31 = (f32[640]{0:T(1024)}, f32[640]{0:T(1024)S(1)}, u32[]{:S(2)}) copy-start(f32[640]{0:T(1024)S(1)} %fusion.83) | copy-start | bytes 7684
  432.6 1.3 copy-start.7
  433.0 2.4 copy-start.1
  437.7 1.5 copy-start.13
  437.7 18.0 %copy-start.40 = (f32[640]{0:T(1024)}, f32[640]{0:T(1024)S(1)}, u32[]{:S(2)}) copy-start(f32[640]{0:T(1024)S(1)} %negate_multiply_fusion.3) | copy-start | bytes 7684
  469.6 1.5 copy-start.6
  469.6 3.0 copy-start.16
  471.1 1.5 copy-start.12
  710.0 188.9 %reduce-scatter.19.cloned.1.call-start = ((), (), s32[]{:S(2)}) async-start(), calls=%async_computation.16 | async-start | bytes 6553600
  718.0 1.3 copy-start.11
  718.1 6.3 copy-start.41
  718.1 215.9 %reduce-scatter.13.cloned.1.call-start = ((), (), s32[]{:S(2)}) async-start(), calls=%async_computation.13 | async-start | bytes 2621440 | tf_op jit(solution)/shard_map/reduce_scatter | solution.py:186
  724.3 284.0 %reduce-scatter.17.cloned.1.call-start = ((), (), s32[]{:S(2)}) async-start(), calls=%async_computation.15 | async-start | bytes 10485760 | tf_op jit(solution)/shard_map/reduce_scatter | solution.py:192
  738.1 1.8 copy-start.2
  738.1 1.8 copy-start.22
  738.1 1.8 copy-start.32
  738.1 1.8 copy-start.34
  738.1 1.8 copy-start.45
  738.2 344.5 %reduce-scatter.15.cloned.1.call-start = ((), (), s32[]{:S(2)}) async-start(), calls=%async_computation.14 | async-start | bytes 10485760 | tf_op jit(solution)/shard_map/reduce_scatter | solution.py:189
  751.6 149.7 %copy-start.5 = (bf16[1,640,1024]{2,1,0:T(8,128)(2,1)S(1)}, bf16[1,640,1024]{2,1,0:T(8,128)(2,1)}, u32[]{:S(2)}) copy-start(bf16[1,640,1024]{2,1,0:T(8,128)(2,1)} %param.14) | copy-start | bytes 3932164
  751.7 149.7 %copy-start.20 = (f32[640]{0:T(1024)S(1)}, f32[640]{0:T(1024)}, u32[]{:S(2)}) copy-start(f32[640]{0:T(1024)} %copy-done.19) | copy-start | bytes 7684
  751.7 149.7 %copy-start.24 = (f32[640]{0:T(1024)S(1)}, f32[640]{0:T(1024)}, u32[]{:S(2)}) copy-start(f32[640]{0:T(1024)} %copy-done.23) | copy-start | bytes 7684
  751.7 149.7 %copy-start.26 = (f32[1,1024]{1,0:T(1,128)S(1)}, f32[1,1024]{1,0:T(1,128)}, u32[]{:S(2)}) copy-start(f32[1,1024]{1,0:T(1,128)} %copy-done.25) | copy-start | bytes 12292
  751.7 149.7 %copy-start.43 = (f32[1,1024]{1,0:T(1,128)S(1)}, f32[1,1024]{1,0:T(1,128)}, u32[]{:S(2)}) copy-start(f32[1,1024]{1,0:T(1,128)} %copy-done.42) | copy-start | bytes 12292
  751.7 391.9 %reduce-scatter.11.cloned.1.call-start = ((), (), s32[]{:S(2)}) async-start(), calls=%async_computation.12 | async-start | bytes 7864320 | tf_op jit(solution)/shard_map/reduce_scatter | solution.py:183
  804.2 107.0 %copy-start.18 = (bf16[640,1024]{0,1:T(8,128)(2,1)}, bf16[640,1024]{0,1:T(8,128)(2,1)S(1)}, u32[]{:S(2)}) copy-start(bf16[640,1024]{0,1:T(8,128)(2,1)S(1)} %copy.58) | copy-start | bytes 3932164
  911.3 452.2 %all-reduce.4.cloned.1.call-start = ((), (), s32[]{:S(2)}) async-start(), calls=%async_computation.18 | async-start | bytes 12582912 | tf_op jit(solution)/shard_map/psum | solution.py:197
  1143.6 1.3 copy-start.8
  1145.2 8.8 copy-start.28
  1153.9 1.5 copy-start.9
  1153.9 2.7 copy-start.29
  1153.9 2.7 copy-start.30
  1153.9 2.7 copy-start.35
  1154.0 2.7 copy-start.38
  1154.0 2.7 copy-start.39
  1363.5 2.3 copy-start.17
  1365.7 2.2 copy-start.15
  1367.9 2.5 copy-start.14
Sparse Core Ops, SparseCore 0:
  9.6 49.0 all-gather.6
  68.3 98.0 all-gather.8
  168.5 96.4 all-gather.10
  266.4 20.9 all-gather.12
  288.8 58.2 all-gather.14
  348.6 58.2 all-gather.16
  710.1 92.1 reduce-scatter.20
  804.6 94.2 reduce-scatter.18
  902.0 31.9 reduce-scatter.12
  936.6 71.6 reduce-scatter.16
  1010.9 71.6 reduce-scatter.14
  1085.2 58.3 reduce-scatter.10
  1148.1 215.3 all-reduce.3
where the time goes:
time: 1390 us; the launch traced here: 1380 us
  waiting for transfers between devices  760 us (55%)
  matrix products  419 us (30%)
  local copies, waits for them, and re-layouts  81.3 us (6%)
  other arithmetic  58.5 us (4%)
  blocking collectives  43 us (3%)
  between operations  14.9 us (1%)
    psum x1, waiting for transfers between devices, local(): lax.psum(shards[0].astype(jnp.bfloat16), ('dp', 'seq')).astype(jnp.float32)  160 us
    unnamed x15, waiting for transfers between devices  148 us
    dot_general x32, matrix products, head_scores(): jnp.einsum('qd,kd->qk', query_head / 32, key_head, preferred_element_type...  120 us
    all_gather x1, waiting for transfers between devices, local(): lax.all_gather(key_rows, 'seq', axis=0, tiled=True)  91.7 us
    all_gather x1, waiting for transfers between devices, local(): lax.all_gather(value_rows, 'seq', axis=0, tiled=True)  80.6 us
    reduce_scatter x1, waiting for transfers between devices, local(): lax.psum_scatter(grad_down.astype(jnp.bfloat16), 'fsdp', scatter_dimensio...  74.3 us
    reduce_scatter x1, waiting for transfers between devices, local(): lax.psum_scatter(grad_up.astype(jnp.bfloat16), 'fsdp', scatter_dimension=...  74.3 us
    reduce_scatter x1, waiting for transfers between devices, local(): lax.psum_scatter(grad_qkv.astype(jnp.bfloat16), 'fsdp', scatter_dimension...  61 us
  transfers between devices with their start and end apart: 13, of which 10 were waited for; matrix products, arithmetic and copies ran while one was open for 17% of the time, Pallas kernels for 0%

commit v1 on v0

v1 whole, which is shorter than its diff:
```python
import functools

import jax
import jax.numpy as jnp
from jax import lax
from jax.experimental import pallas as pl
from jax.experimental.pallas import tpu as pltpu
from jax.sharding import PartitionSpec as P

HD = 64
IMAGE = 1024
SLOT = 1280
BLK = 256
LOG2E = 1.4426950408889634
SCALE = LOG2E / 8.0
NEG = -1e30
F32 = jnp.float32
BF16 = jnp.bfloat16
VMEM_LIMIT = 60 * 1024 * 1024
GROUPS = 2


def nn(a, b):
    return lax.dot_general(a, b, (((1,), (0,)), ((), ())), preferred_element_type=F32)


def nt(a, b):
    return lax.dot_general(a, b, (((1,), (1,)), ((), ())), preferred_element_type=F32)


def tn(a, b):
    return lax.dot_general(a, b, (((0,), (0,)), ((), ())), preferred_element_type=F32)


def normalise(v):
    mean = jnp.mean(v, axis=-1, keepdims=True)
    centred = v - mean
    var = jnp.mean(centred * centred, axis=-1, keepdims=True)
    rstd = lax.rsqrt(var + 1e-05)
    return centred * rstd, rstd


def norm_back(g, hat, rstd, gain):
    gg = g * gain
    return rstd * (
        gg - jnp.mean(gg, axis=-1, keepdims=True) - hat * jnp.mean(gg * hat, axis=-1, keepdims=True)
    )


def call(body, grid, prefetch, in_specs, out_specs, out_shape, scratch=(), flops=0, moved=0):
    return pl.pallas_call(
        body,
        grid_spec=pltpu.PrefetchScalarGridSpec(
            num_scalar_prefetch=prefetch,
            grid=grid,
            in_specs=in_specs,
            out_specs=out_specs,
            scratch_shapes=list(scratch),
        ),
        out_shape=out_shape,
        compiler_params=pltpu.CompilerParams(vmem_limit_bytes=VMEM_LIMIT),
        cost_estimate=pl.CostEstimate(flops=int(flops), bytes_accessed=int(moved), transcendentals=0),
    )


def full(shape):
    zeros = (0,) * len(shape)
    return pl.BlockSpec(shape, lambda *_: zeros)


def hbm():
    return pl.BlockSpec(memory_space=pl.ANY)


def shape(dims, dtype):
    return jax.ShapeDtypeStruct(dims, dtype)


def project_body(info, pos, own, head, rest, gain, bias, *refs, pieces):
    parts = refs[:pieces]
    q, k, v, n_t, w, sems = refs[pieces:]
    step = pl.program_id(0)
    half = q.shape[1]

    def copies():
        return [
            pltpu.make_async_copy(
                parts[i], w.at[pl.ds(pl.multiple_of(pos[i], 16), parts[i].shape[0])], sems.at[i]
            )
            for i in range(pieces)
        ]

    @pl.when(step == 0)
    def _():
        for c in copies():
            c.start()

    def rows(x):
        hat, _ = normalise(x.astype(F32))
        return (hat * gain[...] + bias[...]).astype(BF16)

    def emit(normed):
        n_t[...] = normed.T
        out = nn(normed, w[...])
        q[...] = out[:, :half].astype(BF16)
        k[...] = out[:, half : 2 * half].astype(BF16)
        v[...] = out[:, 2 * half :].astype(BF16)

    @pl.when(step == 0)
    def _():
        normed = rows(own[...])
        for c in copies():
            c.wait()
        emit(normed)

    @pl.when(step == 1)
    def _():
        emit(rows(jnp.concatenate([head[...], rest[...]], axis=0)))


def project(info, pos, own, head, rest, gain, bias, parts):
    local, d = own.shape
    wide = parts[0].shape[1]
    half = wide // 3
    block = lambda i, info, pos: ((info[1] + i) % 2, 0)
    return call(
        functools.partial(project_body, pieces=len(parts)),
        (2,),
        2,
        [full(own.shape), full(head.shape), full(rest.shape), full((1, d)), full((1, d))]
        + [hbm()] * len(parts),
        [pl.BlockSpec((local, half), block)] * 3
        + [
            pl.BlockSpec((d, local), lambda i, info, pos: (0, (info[1] + i) % 2)),
            full((d, wide)),
        ],
        [shape((2 * local, half), BF16)] * 3 + [shape((d, 2 * local), BF16), shape((d, wide), BF16)],
        [pltpu.SemaphoreType.DMA((len(parts),))],
        flops=4 * local * d * wide,
        moved=16e6,
    )(info, pos, own, head, rest, gain, bias, *parts)


def pad_body(x, gain, bias, w, k, v, n_t):
    hat, _ = normalise(x[...].astype(F32))
    normed = (hat * gain[...] + bias[...]).astype(BF16)
    n_t[...] = normed.T
    half = k.shape[1]
    out = nn(normed, w[:, half:])
    k[...] = out[:, :half].astype(BF16)
    v[...] = out[:, half:].astype(BF16)


def pad_project(x, gain, bias, w):
    rows, d = x.shape
    half = w.shape[1] // 3
    return call(
        pad_body,
        (1,),
        0,
        [full(x.shape), full((1, d)), full((1, d)), full(w.shape)],
        [full((rows, half)), full((rows, half)), full((d, rows))],
        [shape((rows, half), BF16)] * 2 + [shape((d, rows), BF16)],
        flops=4 * rows * d * half,
        moved=5e6,
    )(x, gain, bias, w)


def attend_body(info, q, k, v, kp, vp, o, lse):
    start, stop, pad_a, pad_b = info[2], info[3], info[4], info[5]
    lane = lax.broadcasted_iota(jnp.int32, (1, 2 * HD), 1)
    row = lax.broadcasted_iota(jnp.int32, (BLK, 1), 0)
    col = lax.broadcasted_iota(jnp.int32, (1, BLK), 1)
    causal = col <= row
    pad_col = (col < pad_a) | (col >= pad_b)
    count = SLOT // BLK
    for i in range(count):
        n = (i + 1) * BLK
        qi = q[i * BLK : n, :]
        edge = i in (0, count - 1)
        pos_q = row + i * BLK
        in_q = (pos_q >= start) & (pos_q < stop)
        masks = []
        for j in range(i + 1):
            pos_k = col + j * BLK
            mask = None
            if edge:
                in_k = (pos_k >= start) & (pos_k < stop)
                mask = (in_q & in_k) | (~in_q & ~in_k)
            elif j == 0:
                mask = jnp.broadcast_to(pos_k >= start, (BLK, BLK))
            if j == i:
                mask = causal if mask is None else mask & causal
            masks.append(mask)
        outs = []
        for h in range(2):
            qh = jnp.where(lane // HD == h, qi, jnp.zeros_like(qi))
            blocks = []
            for j in range(i + 1):
                s = nt(qh, k[j * BLK : (j + 1) * BLK, :]) * SCALE
                if masks[j] is not None:
                    s = jnp.where(masks[j], s, NEG)
                blocks.append(s)
            if edge:
                s = nt(qh, kp[...]) * SCALE
                blocks.append(jnp.where(~in_q & pad_col, s, NEG))
            top = functools.reduce(jnp.maximum, blocks)
            top = jnp.max(top, axis=1, keepdims=True)
            probs = [jnp.exp2(s - top) for s in blocks]
            total = jnp.sum(functools.reduce(jnp.add, probs), axis=1, keepdims=True)
            probs = [x.astype(BF16) for x in probs]
            mixed = nn(jnp.concatenate(probs[: i + 1], axis=1), v[0:n, :])
            if edge:
                mixed = mixed + nn(probs[-1], vp[...])
            outs.append(mixed * (1.0 / total))
            level = jnp.broadcast_to(top + jnp.log2(total), (BLK, 128))
            lse[0, h : h + 1, i * BLK : n] = level.T[0:1, :]
        o[i * BLK : n, :] = jnp.where(lane < HD, outs[0], outs[1]).astype(BF16)


def attend(info, q, k, v, kp, vp):
    rows, half = q.shape
    pairs = half // (2 * HD)
    pair = pl.BlockSpec((rows, 2 * HD), lambda i, info: (0, i))
    pad = pl.BlockSpec((kp.shape[0], 2 * HD), lambda i, info: (0, i))
    return call(
        attend_body,
        (pairs,),
        1,
        [pair, pair, pair, pad, pad],
        [pair, pl.BlockSpec((1, 2, rows), lambda i, info: (i, 0, 0))],
        [shape((rows, half), BF16), shape((pairs, 2, rows), F32)],
        flops=pairs * 34 * BLK * BLK * 256 * 4,
        moved=6e6,
    )(info, q, k, v, kp, vp)


def attend_back_body(
    info, q, k, v, kp, vp, o, lse, d_own, d_other, dq, dk, dv, dkp, dvp, do, dk_sum, dv_sum, dkp_sum, dvp_sum
):
    parity, start, stop, pad_a, pad_b = info[1], info[2], info[3], info[4], info[5]
    local = d_own.shape[0]
    do[pl.ds(pl.multiple_of(parity * local, 128), local), :] = d_own[...]
    do[pl.ds(pl.multiple_of((1 - parity) * local, 128), local), :] = d_other[...]
    lane = lax.broadcasted_iota(jnp.int32, (1, 2 * HD), 1)
    pick = (
        lax.broadcasted_iota(jnp.int32, (8, 2 * HD), 1) // HD
        == lax.broadcasted_iota(jnp.int32, (8, 2 * HD), 0)
    ).astype(F32)
    inner = lax.dot_general(
        pick,
        do[...].astype(F32) * o[...].astype(F32),
        (((1,), (1,)), ((), ())),
        precision=lax.Precision.HIGHEST,
        preferred_element_type=F32,
    )
    row = lax.broadcasted_iota(jnp.int32, (BLK, 1), 0)
    col = lax.broadcasted_iota(jnp.int32, (1, 2 * BLK), 1) % BLK
    causal = row <= col
    pad_row = (row < pad_a) | (row >= pad_b)
    dk_sum[...] = jnp.zeros_like(dk_sum)
    dv_sum[...] = jnp.zeros_like(dv_sum)
    dkp_sum[...] = jnp.zeros_like(dkp_sum)
    dvp_sum[...] = jnp.zeros_like(dvp_sum)
    count = SLOT // BLK

    def split(x):
        zero = jnp.zeros_like(x)
        return [jnp.where(lane // HD == h, x, zero) for h in range(2)]

    for i in range(count):
        rows = slice(i * BLK, (i + 1) * BLK)
        qs = jnp.concatenate(split(q[rows, :]), axis=0)
        ds = jnp.concatenate(split(do[rows, :]), axis=0)
        level = jnp.concatenate([lse[0, 0:1, rows], lse[0, 1:2, rows]], axis=1)
        inner_i = jnp.concatenate([inner[0:1, rows], inner[1:2, rows]], axis=1)
        edge = i in (0, count - 1)
        pos_q = col + i * BLK
        in_q = (pos_q >= start) & (pos_q < stop)
        dq_sum = jnp.zeros((BLK, 2 * HD), F32)

        def block(kj, vj, mask):
            s = nt(kj, qs) * SCALE - level
            if mask is not None:
                s = jnp.where(mask, s, NEG)
            p = jnp.exp2(s)
            g = p * (nt(vj, ds) - inner_i)
            p, g = p.astype(BF16), g.astype(BF16)
            halves = split(kj)
            part = tn(g[:, :BLK], halves[0]) + tn(g[:, BLK:], halves[1])
            return nn(g, qs), nn(p, ds), part

        for j in range(i + 1):
            keys = slice(j * BLK, (j + 1) * BLK)
            pos_k = row + j * BLK
            mask = None
            if edge:
                in_k = (pos_k >= start) & (pos_k < stop)
                mask = (in_q & in_k) | (~in_q & ~in_k)
            elif j == 0:
                mask = jnp.broadcast_to(pos_k >= start, (BLK, 2 * BLK))
            if j == i:
                mask = causal if mask is None else mask & causal
            gk, gv, part = block(k[keys, :], v[keys, :], mask)
            dk_sum[keys, :] += gk
            dv_sum[keys, :] += gv
            dq_sum = dq_sum + part
        if edge:
            gk, gv, part = block(kp[...], vp[...], ~in_q & pad_row)
            dkp_sum[...] += gk
            dvp_sum[...] += gv
            dq_sum = dq_sum + part
        dq[rows, :] = (dq_sum * 0.125).astype(BF16)
    dk[...] = (dk_sum[...] * 0.125).astype(BF16)
    dv[...] = dv_sum[...].astype(BF16)
    dkp[...] = (dkp_sum[...] * 0.125).astype(BF16)
    dvp[...] = dvp_sum[...].astype(BF16)


def attend_back(info, q, k, v, kp, vp, o, lse, d_own, d_other):
    rows, half = q.shape
    pads = kp.shape[0]
    pairs = half // (2 * HD)
    pick = lambda n: pl.BlockSpec((n, 2 * HD), lambda i, info: (0, i))
    pair, pad, part = pick(rows), pick(pads), pick(d_own.shape[0])
    return call(
        attend_back_body,
        (pairs,),
        1,
        [pair, pair, pair, pad, pad, pair, pl.BlockSpec((1, 2, rows), lambda i, info: (i, 0, 0)), part, part],
        [pair, pair, pair, pad, pad],
        [shape((rows, half), BF16)] * 3 + [shape((pads, half), BF16)] * 2,
        [
            pltpu.VMEM((rows, 2 * HD), BF16),
            pltpu.VMEM((rows, 2 * HD), F32),
            pltpu.VMEM((rows, 2 * HD), F32),
            pltpu.VMEM((pads, 2 * HD), F32),
            pltpu.VMEM((pads, 2 * HD), F32),
        ],
        flops=pairs * 34 * BLK * BLK * 256 * 10,
        moved=14e6,
    )(info, q, k, v, kp, vp, o, lse, d_own, d_other)


def forward_body(info, pos, own, other, x, up, gains, biases, *refs, counts):
    total = sum(counts)
    parts = refs[:total]
    (out, g_feed, act_t, slope, n_t, branch, middle, edges, wo_out, wu_out, wd_out) = refs[total : total + 11]
    wo, wu, wd, normed, feed, sems, out_sems = refs[total + 11 :]
    parity = info[1]
    step, last = pl.program_id(0), pl.num_programs(0) - 1
    local = x.shape[0]
    half = own.shape[1]
    tile = slope.shape[1]
    blocks = local // 128

    def copies(which):
        first = sum(counts[:which])
        target = (wo, wu, wd)[which]
        return [
            pltpu.make_async_copy(
                parts[i],
                target.at[pl.ds(pl.multiple_of(pos[i], 16), parts[i].shape[0])],
                sems.at[i],
            )
            for i in range(first, first + counts[which])
        ]

    def store(which):
        return pltpu.make_async_copy(
            (wo, wu, wd)[which], (wo_out, wu_out, wd_out)[which], out_sems.at[which]
        )

    @pl.when(step == 0)
    def _():
        for which in range(3):
            for c in copies(which):
                c.start()
        for c in copies(0):
            c.wait()
        store(0).start()
        w_own = wo[pl.ds(pl.multiple_of(parity * half, 128), half), :]
        w_other = wo[pl.ds(pl.multiple_of((1 - parity) * half, 128), half), :]
        branch[...] = nn(own[...], w_own) + nn(other[...], w_other)

        def rows(i, carry):
            at = pl.ds(pl.multiple_of(i * 128, 128), 128)
            hat, _ = normalise(branch[at, :])
            mid = x[at, :].astype(F32) + hat * gains[1:2, :] + biases[1:2, :]
            middle[at, :] = mid
            hat, _ = normalise(mid)
            two = (hat * gains[2:3, :] + biases[2:3, :]).astype(BF16)
            normed[at, :] = two
            n_t[:, at] = two.T
            return carry

        lax.fori_loop(0, blocks, rows, 0)
        feed[...] = jnp.zeros_like(feed)
        for which in (1, 2):
            for c in copies(which):
                c.wait()
            store(which).start()

    cols = pl.ds(pl.multiple_of(step * tile, 128), tile)
    u = nn(normed[...], wu[:, cols])
    th = jnp.tanh(0.7978845608 * (u + 0.044715 * (u * u * u)))
    act = (0.5 * u * (1.0 + th)).astype(BF16)
    slope[...] = (
        0.5 * (1.0 + th) + 0.5 * u * (1.0 - th * th) * (0.7978845608 + (3 * 0.044715 * 0.7978845608) * (u * u))
    ).astype(BF16)
    act_t[...] = act.T
    feed[...] += nn(act, wd[cols, :])

    @pl.when(step == last)
    def _():
        def rows(i, carry):
            at = pl.ds(pl.multiple_of(i * 128, 128), 128)
            g = up[at, :].astype(F32)
            hat, rstd = normalise(feed[at, :])
            gain = gains[3:4, :]
            out[at, :] = (middle[at, :] + hat * gain + biases[3:4, :]).astype(BF16)
            g_feed[at, :] = norm_back(g, hat, rstd, gain).astype(BF16)
            return (
                carry[0] + jnp.sum(g * hat, axis=0, keepdims=True),
                carry[1] + jnp.sum(g, axis=0, keepdims=True),
            )

        zero = jnp.zeros((1, x.shape[1]), F32)
        a, b = lax.fori_loop(0, blocks, rows, (zero, zero))
        edges[0:1, :] = a
        edges[1:2, :] = b
        for which in range(3):
            store(which).wait()


def forward(info, pos, own, other, x, up, gains, biases, parts, counts, ff):
    attn, half, parity = own
    local, d = x.shape
    tile = 512
    once = lambda s: pl.BlockSpec(s, lambda *_: (0,) * len(s), pipeline_mode=pl.Buffered(1))
    return call(
        functools.partial(forward_body, counts=counts),
        (ff // tile,),
        2,
        [
            pl.BlockSpec((local, half), lambda i, info, pos: (info[1], 0), pipeline_mode=pl.Buffered(1)),
            once(other.shape),
            once(x.shape),
            once(up.shape),
            once(gains.shape),
            once(biases.shape),
        ]
        + [hbm()] * len(parts),
        [
            full((local, d)),
            full((local, d)),
            pl.BlockSpec((tile, local), lambda i, info, pos: (i, 0)),
            pl.BlockSpec((local, tile), lambda i, info, pos: (0, i)),
            full((d, local)),
            full((local, d)),
            full((local, d)),
            full((2, d)),
            hbm(),
            hbm(),
            hbm(),
        ],
        [
            shape((local, d), BF16),
            shape((local, d), BF16),
            shape((ff, local), BF16),
            shape((local, ff), BF16),
            shape((d, local), BF16),
            shape((local, d), F32),
            shape((local, d), F32),
            shape((2, d), F32),
            shape((d, d), BF16),
            shape((d, ff), BF16),
            shape((ff, d), BF16),
        ],
        [
            pltpu.VMEM((d, d), BF16),
            pltpu.VMEM((d, ff), BF16),
            pltpu.VMEM((ff, d), BF16),
            pltpu.VMEM((local, d), BF16),
            pltpu.VMEM((local, d), F32),
            pltpu.SemaphoreType.DMA((len(parts),)),
            pltpu.SemaphoreType.DMA((3,)),
        ],
        flops=2 * local * d * (d + 2 * ff),
        moved=60e6,
    )(info, pos, attn, other, x, up, gains, biases, *parts)


def back_body(info, g_feed, n_t, act_t, slope, wd, wu, keep, send, g_two, *, fsdp):
    r = pl.program_id(0)
    f = info[0]
    tile = wd.shape[0]
    rows = n_t.shape[0] // fsdp
    width = keep.shape[2]
    piece = width // fsdp
    here = r ^ f
    g = g_feed[...]
    hid = (nt(g, wd[...]) * slope[...].astype(F32)).astype(BF16)
    down = nn(act_t[...], g).astype(BF16)
    even = r % 2 == 0

    @pl.when(even)
    def _():
        keep[r // 2, 0:tile, :] = down

    @pl.when(~even)
    def _():
        send[r // 2, 0:tile, :] = down

    lanes = pl.ds(pl.multiple_of(here * piece, 128), piece)
    for other in range(fsdp):
        shard = other ^ f
        up = nn(n_t[pl.ds(pl.multiple_of(shard * rows, 128), rows), :], hid).astype(BF16)
        target = (keep, send)[other % 2]
        for c in range(tile // piece):
            target[other // 2, tile + c * rows : tile + (c + 1) * rows, lanes] = up[:, c * piece : (c + 1) * piece]
    part = nt(hid, wu[...])

    @pl.when(r == 0)
    def _():
        g_two[...] = part

    @pl.when(r != 0)
    def _():
        g_two[...] += part


def back_group(info, g, g_feed, n_t, act_t, slope, wd, wu, fsdp):
    local, d = g_feed.shape
    ff = wd.shape[0]
    tile = ff // fsdp // GROUPS
    extra = (d // fsdp) * (fsdp * tile // d)
    block = lambda i, info: (i ^ info[0]) * GROUPS + g
    grads = shape((fsdp // 2, tile + extra, d), BF16)
    return call(
        functools.partial(back_body, fsdp=fsdp),
        (fsdp,),
        1,
        [
            full((local, d)),
            full((d, local)),
            pl.BlockSpec((tile, local), lambda i, info: (block(i, info), 0)),
            pl.BlockSpec((local, tile), lambda i, info: (0, block(i, info))),
            pl.BlockSpec((tile, d), lambda i, info: (block(i, info), 0)),
            pl.BlockSpec((d, tile), lambda i, info: (0, block(i, info))),
        ],
        [full(grads.shape), full(grads.shape), full((local, d))],
        [grads, grads, shape((local, d), F32)],
        flops=8 * local * d * tile * fsdp,
        moved=40e6,
    )(info, g_feed, n_t, act_t, slope, wd, wu)


def middle_body(
    info, ga, gb, middle, branch, up, gains, wo, own, other, g_mid, d_own, d_send, keep, send, edges, att, gbr, *, fsdp
):
    f, parity = info[0], info[1]
    step, last = pl.program_id(0), pl.num_programs(0) - 1
    half = own.shape[1]

    @pl.when(step == 0)
    def _():
        edges[...] = jnp.zeros_like(edges)
        att[:, pl.ds(pl.multiple_of(parity * half, 128), half)] = own[...]
        att[:, pl.ds(pl.multiple_of((1 - parity) * half, 128), half)] = other[...]

    g = ga[...] + gb[...]
    hat, rstd = normalise(middle[...])
    edges[2:3, :] += jnp.sum(g * hat, axis=0, keepdims=True)
    edges[3:4, :] += jnp.sum(g, axis=0, keepdims=True)
    gm = up[...].astype(F32) + norm_back(g, hat, rstd, gains[2:3, :])
    g_mid[...] = gm
    hat, rstd = normalise(branch[...])
    edges[0:1, :] += jnp.sum(gm * hat, axis=0, keepdims=True)
    edges[1:2, :] += jnp.sum(gm, axis=0, keepdims=True)
    gr = norm_back(gm, hat, rstd, gains[1:2, :]).astype(BF16)
    gbr[pl.ds(pl.multiple_of(step * gr.shape[0], 16), gr.shape[0]), :] = gr

    @pl.when(step == last)
    def _():
        grad = gbr[...]
        d_send[...] = nt(grad, wo[pl.ds(pl.multiple_of((1 - parity) * half, 128), half), :]).astype(BF16)
        d_own[...] = nt(grad, wo[pl.ds(pl.multiple_of(parity * half, 128), half), :]).astype(BF16)
        rows = keep.shape[1]
        for r in range(fsdp):
            cols = pl.ds(pl.multiple_of((r ^ f) * rows, 128), rows)
            (keep, send)[r % 2][r // 2] = tn(att[:, cols], grad).astype(BF16)


def middle_back(info, ga, gb, middle, branch, up, gains, wo, attn, half, other, fsdp):
    local, d = ga.shape
    rows = 128
    block = pl.BlockSpec((rows, d), lambda i, info: (i, 0))
    grads = shape((fsdp // 2, d // fsdp, d), BF16)
    return call(
        functools.partial(middle_body, fsdp=fsdp),
        (local // rows,),
        1,
        [block, block, block, block, block, full(gains.shape), full(wo.shape)]
        + [pl.BlockSpec((local, half), lambda i, info: (info[1], 0)), full(other.shape)],
        [block, full((local, half)), full((local, half)), full(grads.shape), full(grads.shape), full((4, d))],
        [shape((local, d), F32), shape((local, half), BF16), shape((local, half), BF16), grads, grads, shape((4, d), F32)],
        [pltpu.VMEM((local, d), BF16), pltpu.VMEM((local, d), BF16)],
        flops=4 * local * d * d,
        moved=22e6,
    )(info, ga, gb, middle, branch, up, gains, wo, attn, other)


def project_back_body(
    info, own, head, rest, padx, gains, dq, dk, dv, dkp, dvp, w, n_t, np_t, g_own, g_send, g_pad, keep, send, edges, *, fsdp
):
    f, parity = info[0], info[1]
    step = pl.program_id(0)
    local = own.shape[0]
    half = dq.shape[1]
    gain = gains[0:1, :]

    def through(at):
        return (
            nt(dq[at, :], w[:, 0:half])
            + nt(dk[at, :], w[:, half : 2 * half])
            + nt(dv[at, :], w[:, 2 * half :])
        )

    @pl.when(step == 0)
    def _():
        g = nt(dkp[...], w[:, half : 2 * half]) + nt(dvp[...], w[:, 2 * half :])
        g_pad[...] = g.astype(BF16)
        hat, _ = normalise(padx[...].astype(F32))
        edges[0:1, :] = jnp.sum(g * hat, axis=0, keepdims=True)
        edges[1:2, :] = jnp.sum(g, axis=0, keepdims=True)
        g = through(pl.ds(pl.multiple_of((1 - parity) * local, 128), local))
        g_send[...] = g.astype(BF16)
        hat, _ = normalise(jnp.concatenate([head[...], rest[...]], axis=0).astype(F32))
        edges[0:1, :] += jnp.sum(g * hat, axis=0, keepdims=True)
        edges[1:2, :] += jnp.sum(g, axis=0, keepdims=True)

    @pl.when(step == 1)
    def _():
        g = through(pl.ds(pl.multiple_of(parity * local, 128), local))
        g_own[...] = g
        hat, _ = normalise(own[...].astype(F32))
        edges[0:1, :] += jnp.sum(g * hat, axis=0, keepdims=True)
        edges[1:2, :] += jnp.sum(g, axis=0, keepdims=True)
        rows = keep.shape[1]
        for r in range(fsdp):
            at = pl.ds(pl.multiple_of((r ^ f) * rows, 128), rows)
            target = (keep, send)[r % 2]
            left, pads = n_t[at, :], np_t[at, :]
            target[r // 2, :, 0:half] = nn(left, dq[...]).astype(BF16)
            target[r // 2, :, half : 2 * half] = (nn(left, dk[...]) + nn(pads, dkp[...])).astype(BF16)
            target[r // 2, :, 2 * half :] = (nn(left, dv[...]) + nn(pads, dvp[...])).astype(BF16)


def project_back(info, own, head, rest, padx, gains, dq, dk, dv, dkp, dvp, w, n_t, np_t, fsdp):
    local, d = own.shape
    wide = w.shape[1]
    pads = padx.shape[0]
    grads = shape((fsdp // 2, d // fsdp, wide), BF16)
    arrays = (own, head, rest, padx, gains, dq, dk, dv, dkp, dvp, w, n_t, np_t)
    return call(
        functools.partial(project_back_body, fsdp=fsdp),
        (2,),
        1,
        [pl.BlockSpec(a.shape, lambda *_: (0, 0), pipeline_mode=pl.Buffered(1)) for a in arrays],
        [full((local, d)), full((local, d)), full((pads, d)), full(grads.shape), full(grads.shape), full((2, d))],
        [shape((local, d), F32), shape((local, d), BF16), shape((pads, d), BF16), grads, grads, shape((2, d), F32)],
        flops=8 * local * d * wide,
        moved=24e6,
    )(info, *arrays)


def finish_body(info, x, g_own, g_other, pad_a, pad_b, g_mid, gains, out, total):
    s, start, cut = info[6], info[7], info[8]
    row = lax.broadcasted_iota(jnp.int32, (pad_a.shape[0], 1), 0)
    mine = ((s == 0) & (row < start)) | ((s == 1) & (row >= cut))
    extra = jnp.where(mine, pad_a[...].astype(F32) + pad_b[...].astype(F32), 0.0)
    total[...] = g_own[...] + g_other[...].astype(F32)
    at = pl.ds(pl.multiple_of(jnp.where(s == 0, 0, total.shape[0] - pad_a.shape[0]), 128), pad_a.shape[0])
    total[at, :] += extra

    def rows(i, carry):
        at = pl.ds(pl.multiple_of(i * 128, 128), 128)
        hat, rstd = normalise(x[at, :].astype(F32))
        out[at, :] = (g_mid[at, :] + norm_back(total[at, :], hat, rstd, gains[0:1, :])).astype(BF16)
        return carry

    lax.fori_loop(0, x.shape[0] // 128, rows, 0)


def finish(info, x, g_own, g_other, pad_a, pad_b, g_mid, gains):
    arrays = (x, g_own, g_other, pad_a, pad_b, g_mid, gains)
    return call(
        finish_body,
        (1,),
        1,
        [full(a.shape) for a in arrays],
        full(x.shape),
        shape(x.shape, BF16),
        [pltpu.VMEM(x.shape, F32)],
        flops=1e7,
        moved=12e6,
    )(info, *arrays)


def hop(value, axis, mask):
    return lax.ppermute(value, axis, [(i, i ^ mask) for i in range(lax.axis_size(axis))])


def arrange(pieces, index):
    count = len(pieces)
    if count == 1:
        return list(pieces)
    half = count // 2
    low, high = arrange(pieces[:half], index), arrange(pieces[half:], index)
    bit = (index & half) != 0
    return [jnp.where(bit, b, a) for a, b in zip(low, high)] + [jnp.where(bit, a, b) for a, b in zip(low, high)]


def part_of(value, count, index):
    rows = value.shape[0] // count
    return lax.dynamic_slice_in_dim(value, index * rows, rows, 0)


def gather_weight(w, f, x):
    fsdp, dp = lax.axis_size("fsdp"), lax.axis_size("dp")
    rows = w.shape[0]
    sub = rows // dp
    pieces, places = [w, hop(w, "fsdp", 1)], [f * rows, (f ^ 1) * rows]
    mine = part_of(w, dp, x)
    for ry in range(1, fsdp // 2):
        first = hop(mine, "fsdp", 2 * ry)
        for rx in range(dp):
            got = first if rx == 0 else hop(first, "dp", rx)
            pieces += [got, hop(got, "fsdp", 1)]
            place = (x ^ rx) * sub
            places += [(f ^ (2 * ry)) * rows + place, (f ^ (2 * ry + 1)) * rows + place]
    return pieces, places


def gather_half(w, f):
    fsdp = lax.axis_size("fsdp")
    rows = w.shape[0]
    pieces, places = [], []
    for ry in range(fsdp // 2):
        got = w if ry == 0 else hop(w, "fsdp", 2 * ry)
        pieces += [got, hop(got, "fsdp", 1)]
        places += [(f ^ (2 * ry)) * rows, (f ^ (2 * ry + 1)) * rows]
    return pieces, places


def add_hop(total, value, axis, mask):
    return total + hop(value.astype(BF16), axis, mask).astype(F32)


def split_sum(value, count, axis, unit, index):
    total = part_of(value, count, index)
    for m in range(1, count):
        total = add_hop(total, part_of(value, count, index ^ m), axis, m * unit)
    return total


def join(value, count, axis, unit, index):
    pieces = [value] + [hop(value, axis, m * unit) for m in range(1, count)]
    return jnp.concatenate(arrange(pieces, index), axis=0)


def reduce_shard(keep, send, x, s, pair_done):
    got = hop(send, "fsdp", 1)
    total = keep[0].astype(F32) + got[0].astype(F32)
    for ry in range(1, keep.shape[0]):
        total = add_hop(total, keep[ry].astype(F32) + got[ry].astype(F32), "fsdp", 2 * ry)
    dp = lax.axis_size("dp")
    part = split_sum(total, dp, "dp", 1, x)
    count, unit, index = (2, 2, s // 2) if pair_done else (lax.axis_size("seq"), 1, s)
    part = split_sum(part, count, "seq", unit, index)
    part = join(part.astype(BF16), count, "seq", unit, index)
    return join(part, dp, "dp", 1, x)


def sum_all(value):
    for axis in ("fsdp", "dp", "seq"):
        m = 1
        while m < lax.axis_size(axis):
            value = value + hop(value, axis, m)
            m *= 2
    return value


def local(
    tokens, qkv_weight, out_weight, up_weight, down_weight, norm_gain, norm_bias, caption_len, item_start, grad_out
):
    x_tok, up = tokens[0], grad_out[0]
    local_rows, d = x_tok.shape
    fsdp = lax.axis_size("fsdp")
    ff = up_weight.shape[1]
    half = d // 2
    f, x, s = lax.axis_index("fsdp"), lax.axis_index("dp"), lax.axis_index("seq")
    parity, slot = s % 2, s // 2
    caps, starts = caption_len[0], item_start[0]
    start = jnp.where(slot == 0, starts[0], starts[1] - SLOT)
    stop = start + jnp.where(slot == 0, caps[0], caps[1]) + IMAGE
    pad_a = jnp.where(slot == 0, 0, starts[0])
    pad_b = jnp.where(slot == 0, BLK, starts[0] + caps[0])
    info = jnp.stack(
        [f, parity, start, stop, pad_a, pad_b, s, starts[0], starts[0] + caps[0]]
    ).astype(jnp.int32)

    head = hop(x_tok[:BLK], "seq", 1)
    rest = hop(x_tok[BLK:], "seq", 1)
    index = lax.broadcasted_iota(jnp.int32, (BLK, 1), 0)
    pads = jnp.where(index < starts[0], head, x_tok[local_rows - BLK :])
    pads = lax.ppermute(pads, "seq", [(1, 2)])
    pads = jnp.where(s == 3, lax.ppermute(pads, "seq", [(2, 3)]), pads)

    w_half = jnp.concatenate(
        [lax.dynamic_slice_in_dim(qkv_weight, c * d + parity * half, half, 1) for c in range(3)], axis=1
    )
    parts, places = gather_half(w_half, f)
    gain0, bias0 = norm_gain[0:1], norm_bias[0:1]
    q, k, v, n_t, w_qkv = project(
        info, jnp.stack(places).astype(jnp.int32), x_tok, head, rest, gain0, bias0, parts
    )
    kp, vp, np_t = pad_project(pads, gain0, bias0, w_qkv)
    mixed, lse = attend(info, q, k, v, kp, vp)
    to_send = lax.dynamic_slice_in_dim(mixed, (1 - parity) * local_rows, local_rows, 0)
    other = hop(to_send, "seq", 1)

    parts, places, counts = [], [], []
    for w in (out_weight, up_weight, down_weight):
        got, at = gather_weight(w, f, x)
        parts += got
        places += at
        counts.append(len(got))
    (out, g_feed, act_t, slope, two_t, branch, middle, edges3, wo, wu, wd) = forward(
        info,
        jnp.stack(places).astype(jnp.int32),
        (mixed, half, parity),
        other,
        x_tok,
        up,
        norm_gain,
        norm_bias,
        parts,
        tuple(counts),
        ff,
    )
    keeps, g_twos = [], []
    for g in range(GROUPS):
        keep, send, g_two = back_group(info, g, g_feed, two_t, act_t, slope, wd, wu, fsdp)
        keeps.append((keep, send))
        g_twos.append(g_two)
    g_mid, d_own, d_send, keep_o, send_o, edges12 = middle_back(
        info, g_twos[0], g_twos[1], middle, branch, up, norm_gain, wo, mixed, half, other, fsdp
    )
    d_other = hop(d_send, "seq", 1)
    dq, dk, dv, dkp, dvp = attend_back(info, q, k, v, kp, vp, mixed, lse, d_own, d_other)
    g_own, g_send, g_pad, keep_q, send_q, edges0 = project_back(
        info, x_tok, head, rest, pads, norm_gain, dq, dk, dv, dkp, dvp, w_qkv, n_t, np_t, fsdp
    )
    g_other = hop(g_send, "seq", 1)
    back_a = lax.ppermute(g_pad, "seq", [(2, 0), (3, 1)])
    back_b = lax.ppermute(g_pad, "seq", [(2, 1), (3, 0)])
    grad_in = finish(info, x_tok, g_own, g_other, back_a, back_b, g_mid, norm_gain)

    sums = sum_all(
        jnp.stack(
            [edges0[0], edges12[0], edges12[2], edges3[0], edges0[1], edges12[1], edges12[3], edges3[1]]
        )
    )

    reduced = [reduce_shard(a, b, x, s, False) for a, b in keeps]
    grad_proj = reduce_shard(keep_o, send_o, x, s, False).astype(F32)
    half_q = reduce_shard(keep_q, send_q, x, s, True)
    both = arrange([half_q, hop(half_q, "seq", 1)], parity)
    grad_qkv = jnp.concatenate(
        [both[h][:, c * half : (c + 1) * half] for c in range(3) for h in range(2)], axis=1
    ).astype(F32)
    tile = ff // fsdp // GROUPS
    rows = d // fsdp
    grad_down = jnp.concatenate([r[:tile] for r in reduced], axis=0).astype(F32)
    piece = d // fsdp
    blocks = []
    for h in range(fsdp):
        for r in reduced:
            for c in range(tile // piece):
                blocks.append(r[tile + c * rows : tile + (c + 1) * rows, h * piece : (h + 1) * piece])
    grad_up = jnp.concatenate(blocks, axis=1).astype(F32)
    return (out[None], grad_in[None], grad_qkv, grad_proj, grad_up, grad_down, sums[0:4], sums[4:8])


def solution(mesh):
    rows = P(("fsdp", "dp"), "seq", None)
    shard = P("fsdp", None)
    items = P(("fsdp", "dp"), None)
    return jax.shard_map(
        local,
        mesh=mesh,
        in_specs=(rows, shard, shard, shard, shard, P(), P(), items, items, rows),
        out_specs=(rows, rows, shard, shard, shard, shard, P(), P()),
        check_vma=False,
    )
```

time: 1390 us -> 757 us (0.54)
  matrix products: 419 us -> 0 us
  waiting for transfers between devices: 760 us -> 381 us
  Pallas kernels: 0 us -> 209 us
  starting transfers between devices: 0.99 us -> 94.3 us
  local copies, waits for them, and re-layouts: 81.3 us -> 18.4 us
  blocking collectives: 43 us -> 0 us
  other arithmetic: 58.5 us -> 38.2 us
    dot_general x124 -> x0, matrix products: 419 us -> none  [the longest x32 120 us: head_scores(): jnp.einsum('qd,kd->qk', query_head / 32, key_head, preferred_element_type...]
    ppermute x0 -> x69, waiting for transfers between devices: none -> 381 us  [the longest x65 381 us: hop(): lax.ppermute(value, axis, [(i, i ^ mask) for i in range(lax.axis_size(axi...]
    reduce_scatter x4 -> x0, waiting for transfers between devices: 232 us -> none  [the longest x1 74.3 us: local(): lax.psum_scatter(grad_down.astype(jnp.bfloat16), 'fsdp', scatter_dimensio...]
    all_gather x6 -> x0, waiting for transfers between devices: 220 us -> none  [the longest x1 91.7 us: local(): lax.all_gather(key_rows, 'seq', axis=0, tiled=True)]
    pallas_call x0 -> x10, Pallas kernels: none -> 209 us  [the longest x2 45.3 us: back_group(): call(functools.partial(back_body, fsdp=fsdp), (fsdp,), 1, [full((local, d...]
    psum x1 -> x0, waiting for transfers between devices: 160 us -> none  [local(): lax.psum(shards[0].astype(jnp.bfloat16), ('dp', 'seq')).astype(jnp.float32)]
    unnamed x15 -> x0, waiting for transfers between devices: 148 us -> none
    ppermute x0 -> x69, starting transfers between devices: none -> 94.3 us  [the longest x65 90.1 us: hop(): lax.ppermute(value, axis, [(i, i ^ mask) for i in range(lax.axis_size(axi...]
  transfers between devices with their start and end apart: 13 -> 69, of which waited for: 10 -> 28; matrix products, arithmetic and copies ran while one was open for 17% -> 6% of each run, Pallas kernels for 0% -> 6%
where the time goes in v1:
time: 757 us; the launch traced here: 747 us
  waiting for transfers between devices  381 us (50%)
  Pallas kernels  209 us (28%)
  starting transfers between devices  94.3 us (12%)
  other arithmetic  38.2 us (5%)
  local copies, waits for them, and re-layouts  18.4 us (2%)
    ppermute x65, waiting for transfers between devices, hop(): lax.ppermute(value, axis, [(i, i ^ mask) for i in range(lax.axis_size(axi...  381 us
    ppermute x65, starting transfers between devices, hop(): lax.ppermute(value, axis, [(i, i ^ mask) for i in range(lax.axis_size(axi...  90.1 us
    pallas_call x2, Pallas kernels, back_group(): call(functools.partial(back_body, fsdp=fsdp), (fsdp,), 1, [full((local, d...  45.3 us
    pallas_call x1, Pallas kernels, attend_back(): call(attend_back_body, (pairs,), 1, [pair, pair, pair, pad, pad, pair, pl...  44.9 us
    pallas_call x1, Pallas kernels, forward(): call(functools.partial(forward_body, counts=counts), (ff // tile,), 2, [p...  35.6 us
    pallas_call x1, Pallas kernels, attend(): call(attend_body, (pairs,), 1, [pair, pair, pair, pad, pad], [pair, pl.Bl...  24.3 us
    pallas_call x1, Pallas kernels, project_back(): call(functools.partial(project_back_body, fsdp=fsdp), (2,), 1, [pl.BlockS...  19.8 us
    pallas_call x1, Pallas kernels, middle_back(): call(functools.partial(middle_body, fsdp=fsdp), (local // rows,), 1, [blo...  15.2 us
  transfers between devices with their start and end apart: 69, of which 28 were waited for; matrix products, arithmetic and copies ran while one was open for 6% of the time, Pallas kernels for 6%

profile of v1, /device:TPU:0, one launch (start us, length us, event | category | flops | bytes accessed | tf_op | source)
XLA Modules:
  0.0 746.6 jit_solution(14970303711012953386)
XLA Ops:
  1.8 3.1 collective-permute-start
  5.9 1.6 collective-permute-start.9
  8.9 5.8 collective-permute-done.9.refs_2_
  14.7 1.5 collective-permute-start.11
  18.0 4.7 collective-permute-done.11.refs_4_
  26.5 1.5 collective-permute-start.14
  29.2 4.6 collective-permute-done.1.rest
  33.8 1.7 collective-permute-start.3
  37.0 54.1 %collective-permute-done.3.refs_2_ = bf16[256,1536]{1,0:T(8,128)(2,1)} collective-permute-done((bf16[256,1536]{1,0:T(8,128)(2,1)S(1)}, bf16[256,1536]{1,0:T(8,128)(2,1)}, u32[]{:S(2)}, u32[]{:S(2)}) %collective-permute-start.3) | collective-permute-done | bytes 786464 | tf_op jit(solution)/shard_map/ppermute | solution.py:712
  91.1 1.5 collective-permute-start.16
  104.2 12.2 %shard_map.161 = (bf16[1280,512]{1,0:T(8,128)(2,1)}, bf16[1280,512]{1,0:T(8,128)(2,1)}, bf16[1280,512]{1,0:T(8,128)(2,1)}, bf16[1024,1280]{1,0:T(8,128)(2,1)}, bf16[1024,1536]{1,0:T(8,128)(2,1)}) custom-call(s32[9]{0:T(128)} %stack.94.info, s32[4]{0:T(128)} %pad_add_fusion.pos, bf16[640,1024]{1,0:T(8,128)(2,1)} %bitcast.53, bf16[256,1024]{1,0:T(8,128)(2,1)} %copy-done.14, ...), custom_call_target="tpu_custom_call" | custom-call | flops 4026531840 | bytes 16000000 | tf_op jit(solution)/shard_map/pallas_call | solution.py:126
  116.4 4.0 shard_map.162
  120.9 18.6 %collective-permute-done.21.refs_16_ = bf16[512,1024]{1,0:T(8,128)(2,1)} collective-permute-done((bf16[512,1024]{1,0:T(8,128)(2,1)}, bf16[512,1024]{1,0:T(8,128)(2,1)}, u32[]{:S(2)}, u32[]{:S(2)}) %collective-permute-start.21) | collective-permute-done | bytes 1048608 | tf_op jit(solution)/shard_map/ppermute | solution.py:712
  139.5 24.3 %shard_map.163 = (bf16[1280,512]{1,0:T(8,128)(2,1)}, f32[4,2,1280]{2,1,0:T(2,128)}) custom-call(s32[9]{0:T(128)} %stack.94.info, bf16[1280,512]{1,0:T(8,128)(2,1)} %get-tuple-element.52.q, bf16[1280,512]{1,0:T(8,128)(2,1)} %get-tuple-element.53.k, bf16[1280,512]{1,0:T(8,128)(2,1)} %get-tuple-element.54.v, bf16[256,512]{1,0:T(8,128)(2,1)} %get-tuple-element.56.kp, ...), custom_call_target="tpu_custom_call" | custom-call | flops 9126805504 | bytes 6000000 | tf_op jit(solution)/shard_map/pallas_call | solution.py:226
  165.9 16.2 %collective-permute-done.7.other = bf16[640,512]{1,0:T(8,128)(2,1)S(1)} collective-permute-done((bf16[640,512]{1,0:T(8,128)(2,1)S(1)}, bf16[640,512]{1,0:T(8,128)(2,1)S(1)}, u32[]{:S(2)}, u32[]{:S(2)}) %collective-permute-start.7) | collective-permute-done | bytes 655392 | tf_op jit(solution)/shard_map/ppermute | solution.py:712
  183.0 35.6 %shard_map.164 = (bf16[640,1024]{1,0:T(8,128)(2,1)}, bf16[640,1024]{1,0:T(8,128)(2,1)}, bf16[4096,640]{1,0:T(8,128)(2,1)}, bf16[640,4096]{1,0:T(8,128)(2,1)}, bf...) custom-call(s32[9]{0:T(128)} %stack.94.info, ...), custom_call_target="tpu_custom_call" | custom-call | flops 12079595520 | bytes 60000000 | tf_op jit(solution)/shard_map/pallas_call | solution.py:441
  218.6 22.7 %shard_map.165 = (bf16[2,1024,1024]{2,1,0:T(8,128)(2,1)}, bf16[2,1024,1024]{2,1,0:T(8,128)(2,1)}, f32[640,1024]{1,0:T(8,128)}) custom-call(s32[9]{0:T(128)} %stack.94.info, bf16[640,1024]{1,0:T(8,128)(2,1)} %get-tuple-element.61.g_feed, bf16[1024,640]{1,0:T(8,128)(2,1)} %get-tuple-element.62.n_t, bf16[4096,640]{1,0:T(8,128)(2,1)} %get-tuple-element.63.act_t, ...), custom_call_target="tpu_custom_call" | custom-call | flops 10737418240 | bytes 40000000 | tf_op jit(solution)/shard_map/pallas_call | solution.py:540
  241.3 22.5 %shard_map.166 = (bf16[2,1024,1024]{2,1,0:T(8,128)(2,1)}, bf16[2,1024,1024]{2,1,0:T(8,128)(2,1)}, f32[640,1024]{1,0:T(8,128)}) custom-call(s32[9]{0:T(128)} %stack.94.info, bf16[640,1024]{1,0:T(8,128)(2,1)} %get-tuple-element.61.g_feed, bf16[1024,640]{1,0:T(8,128)(2,1)} %get-tuple-element.62.n_t, bf16[4096,640]{1,0:T(8,128)(2,1)} %get-tuple-element.63.act_t, ...), custom_call_target="tpu_custom_call" | custom-call | flops 10737418240 | bytes 40000000 | tf_op jit(solution)/shard_map/pallas_call | solution.py:540
  263.8 15.2 %shard_map.167 = (f32[640,1024]{1,0:T(8,128)}, bf16[640,512]{1,0:T(8,128)(2,1)}, bf16[640,512]{1,0:T(8,128)(2,1)}, bf16[2,256,1024]{2,1,0:T(8,128)(2,1)}, bf16[2...) custom-call(s32[9]{0:T(128)} %stack.94.info, f32[640,1024]{1,0:T(8,128)} %get-tuple-element.67.ga, ...), custom_call_target="tpu_custom_call" | custom-call | flops 2684354560 | bytes 22000000 | tf_op jit(solution)/shard_map/pallas_call | solution.py:600
  279.4 16.3 %collective-permute-done.23.d_other = bf16[640,512]{1,0:T(8,128)(2,1)S(1)} collective-permute-done((bf16[640,512]{1,0:T(8,128)(2,1)}, bf16[640,512]{1,0:T(8,128)(2,1)S(1)}, u32[]{:S(2)}, u32[]{:S(2)}) %collective-permute-start.23) | collective-permute-done | bytes 655392 | tf_op jit(solution)/shard_map/ppermute | solution.py:712
  296.5 44.9 %shard_map.168 = (bf16[1280,512]{1,0:T(8,128)(2,1)}, bf16[1280,512]{1,0:T(8,128)(2,1)}, bf16[1280,512]{1,0:T(8,128)(2,1)}, bf16[256,512]{1,0:T(8,128)(2,1)}, bf16[256,512]{1,0:T(8,128)(2,1)}) custom-call(s32[9]{0:T(128)} %stack.94.info, bf16[1280,512]{1,0:T(8,128)(2,1)} %get-tuple-element.52.q, bf16[1280,512]{1,0:T(8,128)(2,1)} %get-tuple-element.53.k, ...), custom_call_target="tpu_custom_call" | custom-call | flops 22817013760 | bytes 14000000 | tf_op jit(solution)/shard_map/pallas_call | solution.py:326
  341.4 19.8 %shard_map.169 = (f32[640,1024]{1,0:T(8,128)}, bf16[640,1024]{1,0:T(8,128)(2,1)}, bf16[256,1024]{1,0:T(8,128)(2,1)}, bf16[2,256,1536]{2,1,0:T(8,128)(2,1)}, bf16...) custom-call(s32[9]{0:T(128)} %stack.94.info, bf16[640,1024]{1,0:T(8,128)(2,1)} %bitcast.55, bf16[256,1024]{1,0:T(8,128)(2,1)} %copy-done.14, ...), custom_call_target="tpu_custom_call" | custom-call | flops 8053063680 | bytes 24000000 | tf_op jit(solution)/shard_map/pallas_call | solution.py:666
  362.3 4.2 collective-permute-done.34
  367.9 1.6 collective-permute-start.35
  371.2 11.5 %collective-permute-done.35 = bf16[256,1024]{1,0:T(8,128)(2,1)S(1)} collective-permute-done((bf16[256,1024]{1,0:T(8,128)(2,1)S(1)}, bf16[256,1024]{1,0:T(8,128)(2,1)S(1)}, u32[]{:S(2)}, u32[]{:S(2)}) %collective-permute-start.35) | collective-permute-done | bytes 524320 | tf_op jit(solution)/shard_map/ppermute | solution.py:712
  384.1 1.6 collective-permute-start.36
  387.0 1.5 collective-permute-start.65
  388.6 10.9 %collective-permute-done.65 = f32[8,1024]{1,0:T(8,128)S(1)} collective-permute-done((f32[8,1024]{1,0:T(8,128)S(1)}, f32[8,1024]{1,0:T(8,128)S(1)}, u32[]{:S(2)}, u32[]{:S(2)}) %collective-permute-start.65) | collective-permute-done | bytes 32800 | tf_op jit(solution)/shard_map/ppermute | solution.py:712
  399.5 1.5 collective-permute-start.66
  401.0 2.4 collective-permute-done.66
  403.8 1.8 bitcast_add_fusion.2
  405.7 1.7 collective-permute-start.29
  407.5 3.6 collective-permute-start.39
  411.2 4.9 collective-permute-done.68
  417.0 4.8 collective-permute-done.38
  424.8 2.4 collective-permute-start.42
  427.3 2.4 collective-permute-done.40
  431.0 17.8 %collective-permute-done.41 = bf16[32,1024]{1,0:T(8,128)(2,1)S(1)} collective-permute-done((bf16[32,1024]{1,0:T(8,128)(2,1)S(1)}, bf16[32,1024]{1,0:T(8,128)(2,1)S(1)}, u32[]{:S(2)}, u32[]{:S(2)}) %collective-permute-start.41) | collective-permute-done | bytes 65568 | tf_op jit(solution)/shard_map/ppermute | solution.py:712
  451.1 31.5 %collective-permute-done.30 = bf16[64,1536]{1,0:T(8,128)(2,1)S(1)} collective-permute-done((bf16[64,1536]{1,0:T(8,128)(2,1)S(1)}, bf16[64,1536]{1,0:T(8,128)(2,1)S(1)}, u32[]{:S(2)}, u32[]{:S(2)}) %collective-permute-start.30) | collective-permute-done | bytes 196640 | tf_op jit(solution)/shard_map/ppermute | solution.py:712
  482.7 2.7 fusion
  485.4 29.5 %collective-permute-done.31 = bf16[64,1536]{1,0:T(8,128)(2,1)S(1)} collective-permute-done((bf16[64,1536]{1,0:T(8,128)(2,1)S(1)}, bf16[64,1536]{1,0:T(8,128)(2,1)S(1)}, u32[]{:S(2)}, u32[]{:S(2)}) %collective-permute-start.31) | collective-permute-done | bytes 196640 | tf_op jit(solution)/shard_map/ppermute | solution.py:712
  515.0 1.6 collective-permute-start.45
  517.2 3.9 fusion.1
  525.5 7.8 %shard_map.170 = bf16[640,1024]{1,0:T(8,128)(2,1)} custom-call(s32[9]{0:T(128)} %stack.94.info, bf16[640,1024]{1,0:T(8,128)(2,1)} %bitcast.56, f32[640,1024]{1,0:T(8,128)} %get-tuple-element.81.g_own, bf16[640,1024]{1,0:T(8,128)(2,1)} %copy-done.8, bf16[256,1024]{1,0:T(8,128)(2,1)} %copy-done.12, bf16[256,1024]{1,0:T(8,128)(2,1)} %copy-done.13, ...), custom_call_target="tpu_custom_call" | custom-call | flops 10000000 | bytes 12000000 | tf_op jit(solution)/shard_map/pallas_call | solution.py:698
  535.4 1.7 broadcast_select_fusion.8
  537.1 1.8 collective-permute-start.33
  538.9 24.7 %collective-permute-done.45 = bf16[1024,1024]{1,0:T(8,128)(2,1)} collective-permute-done((bf16[1024,1024]{1,0:T(8,128)(2,1)S(1)}, bf16[1024,1024]{1,0:T(8,128)(2,1)}, u32[]{:S(2)}, u32[]{:S(2)}) %collective-permute-start.45) | collective-permute-done | bytes 2097184 | tf_op jit(solution)/shard_map/ppermute | solution.py:712
  563.6 3.8 bitcast_add_fusion.1
  568.7 37.7 %collective-permute-done.55 = bf16[1024,1024]{1,0:T(8,128)(2,1)} collective-permute-done((bf16[1024,1024]{1,0:T(8,128)(2,1)}, bf16[1024,1024]{1,0:T(8,128)(2,1)}, u32[]{:S(2)}, u32[]{:S(2)}) %collective-permute-start.55) | collective-permute-done | bytes 2097184 | tf_op jit(solution)/shard_map/ppermute | solution.py:712
  606.4 3.6 bitcast_add_fusion
  612.6 3.1 collective-permute-start.48
  616.5 16.8 %collective-permute-done.56 = bf16[512,1024]{1,0:T(8,128)(2,1)S(1)} collective-permute-done((bf16[512,1024]{1,0:T(8,128)(2,1)S(1)}, bf16[512,1024]{1,0:T(8,128)(2,1)S(1)}, u32[]{:S(2)}, u32[]{:S(2)}) %collective-permute-start.56) | collective-permute-done | bytes 1048608 | tf_op jit(solution)/shard_map/ppermute | solution.py:712
  633.9 3.4 collective-permute-start.58
  638.3 7.4 collective-permute-done.48
  647.2 18.3 %collective-permute-start.52 = (bf16[128,1024]{1,0:T(8,128)(2,1)S(1)}, bf16[128,1024]{1,0:T(8,128)(2,1)S(1)}, u32[]{:S(2)}, u32[]{:S(2)}) collective-permute-start(bf16[128,1024]{1,0:T(8,128)(2,1)S(1)} %add_convert_fusion.5), channel_id=1, source_target_pairs={{0,1},{1,0},{2,3},{3,2},{4,5},{5,4},{6,7},{7,6},{8,9},{9,8},{10,11... | collective-permute-start | bytes 786440 | tf_op jit(solution)/shard_map/ppermute | solution.py:712
  665.5 5.1 collective-permute-done.58
  671.5 16.6 %collective-permute-start.62 = (bf16[128,1024]{1,0:T(8,128)(2,1)S(1)}, bf16[128,1024]{1,0:T(8,128)(2,1)S(1)}, u32[]{:S(2)}, u32[]{:S(2)}) collective-permute-start(bf16[128,1024]{1,0:T(8,128)(2,1)S(1)} %add_convert_fusion.4), channel_id=1, source_target_pairs={{0,1},{1,0},{2,3},{3,2},{4,5},{5,4},{6,7},{7,6},{8,9},{9,8},{10,11... | collective-permute-start | bytes 786440 | tf_op jit(solution)/shard_map/ppermute | solution.py:712
  688.0 5.1 collective-permute-done.51
  694.4 9.8 %collective-permute-done.61 = bf16[128,1024]{1,0:T(8,128)(2,1)S(1)} collective-permute-done((bf16[128,1024]{1,0:T(8,128)(2,1)S(1)}, bf16[128,1024]{1,0:T(8,128)(2,1)S(1)}, u32[]{:S(2)}, u32[]{:S(2)}) %collective-permute-start.61) | collective-permute-done | bytes 262176 | tf_op jit(solution)/shard_map/ppermute | solution.py:712
  705.4 2.0 convert_element_type.220
  707.4 12.1 %collective-permute-done.53 = bf16[512,1024]{1,0:T(8,128)(2,1)S(1)} collective-permute-done((bf16[512,1024]{1,0:T(8,128)(2,1)S(1)}, bf16[512,1024]{1,0:T(8,128)(2,1)S(1)}, u32[]{:S(2)}, u32[]{:S(2)}) %collective-permute-start.53) | collective-permute-done | bytes 1048608 | tf_op jit(solution)/shard_map/ppermute | solution.py:712
  720.1 20.4 %collective-permute-done.63 = bf16[512,1024]{1,0:T(8,128)(2,1)S(1)} collective-permute-done((bf16[512,1024]{1,0:T(8,128)(2,1)S(1)}, bf16[512,1024]{1,0:T(8,128)(2,1)S(1)}, u32[]{:S(2)}, u32[]{:S(2)}) %collective-permute-start.63) | collective-permute-done | bytes 1048608 | tf_op jit(solution)/shard_map/ppermute | solution.py:712
  741.5 2.5 convert_element_type.270
  744.0 2.4 maximum_convert_fusion
  (224 shorter events, 58.4 us)
Async XLA Ops:
  1.8 15.8 %collective-permute-start = (bf16[256,1024]{1,0:T(8,128)(2,1)S(1)}, bf16[256,1024]{1,0:T(8,128)(2,1)S(1)}, u32[]{:S(2)}, u32[]{:S(2)}) collective-permute-start(bf16[256,1024]{1,0:T(8,128)(2,1)S(1)} %slice_bitcast_fusion.1), channel_id=1, source_target_pairs={{0,1},{1,0},{2,3},{3,2},{4,5},{5,4},{6,7},{7,6},{8,9},{9,8},{10,11... | collective-permute-start | bytes 1572872 | tf_op jit(solution)/shard_map/ppermute | solution.py:712
  4.9 21.0 %collective-permute-start.8 = (bf16[256,1024]{1,0:T(8,128)(2,1)}, bf16[256,1024]{1,0:T(8,128)(2,1)}, u32[]{:S(2)}, u32[]{:S(2)}) collective-permute-start(bf16[256,1024]{1,0:T(8,128)(2,1)} %refs_0_.1), channel_id=1, source_target_pairs={{0,8},{8,0},{16,24},{24,16},{1,9},{9,1},{17,25},{25,17},{2,10},{10... | collective-permute-start | bytes 1572872 | tf_op jit(solution)/shard_map/ppermute | solution.py:712
  5.9 8.8 %collective-permute-start.9 = (bf16[128,1024]{1,0:T(8,128)(2,1)S(1)}, bf16[128,1024]{1,0:T(8,128)(2,1)S(1)}, u32[]{:S(2)}, u32[]{:S(2)}) collective-permute-start(bf16[128,1024]{1,0:T(8,128)(2,1)S(1)} %constant_dynamic-slice_fusion.2), channel_id=1, source_target_pairs={{0,16},{8,24},{16,0},{24,8},{1,17},{9,25},{17,1},{25,9},{2,18},{10... | collective-permute-start | bytes 786440 | tf_op jit(solution)/shard_map/ppermute | solution.py:712
  8.4 25.4 %collective-permute-start.1 = (bf16[384,1024]{1,0:T(8,128)(2,1)}, bf16[384,1024]{1,0:T(8,128)(2,1)}, u32[]{:S(2)}, u32[]{:S(2)}) collective-permute-start(bf16[384,1024]{1,0:T(8,128)(2,1)} %slice_bitcast_fusion), channel_id=1, source_target_pairs={{0,1},{1,0},{2,3},{3,2},{4,5},{5,4},{6,7},{7,6},{8,9},{9,8},{10,11... | collective-permute-start | bytes 2359304 | tf_op jit(solution)/shard_map/ppermute | solution.py:712
  14.7 8.0 %collective-permute-start.11 = (bf16[128,1024]{1,0:T(8,128)(2,1)S(1)}, bf16[128,1024]{1,0:T(8,128)(2,1)}, u32[]{:S(2)}, u32[]{:S(2)}) collective-permute-start(bf16[128,1024]{1,0:T(8,128)(2,1)S(1)} %collective-permute-done.9.refs_2_), channel_id=1, source_target_pairs={{0,4},{4,0},{1,5},{5,1},{2,6},{6,2},{3,7},{7,3},{8,12},{12,8},{9,1... | collective-permute-start | bytes 786440 | tf_op jit(solution)/shard_map/ppermute | solution.py:712
  17.4 18.2 %collective-permute-start.2 = (bf16[256,1536]{1,0:T(8,128)(2,1)S(1)}, bf16[256,1536]{1,0:T(8,128)(2,1)}, u32[]{:S(2)}, u32[]{:S(2)}) collective-permute-start(bf16[256,1536]{1,0:T(8,128)(2,1)S(1)} %pad_maximum_fusion.2.refs_0_), channel_id=1, source_target_pairs={{0,8},{8,0},{16,24},{24,16},{1,9},{9,1},{17,25},{25,17},{2,10},{10... | collective-permute-start | bytes 2359304 | tf_op jit(solution)/shard_map/ppermute | solution.py:712
  17.7 8.9 %collective-permute-start.10 = (bf16[128,1024]{1,0:T(8,128)(2,1)S(1)}, bf16[128,1024]{1,0:T(8,128)(2,1)}, u32[]{:S(2)}, u32[]{:S(2)}) collective-permute-start(bf16[128,1024]{1,0:T(8,128)(2,1)S(1)} %collective-permute-done.9.refs_2_), channel_id=1, source_target_pairs={{0,8},{8,0},{16,24},{24,16},{1,9},{9,1},{17,25},{25,17},{2,10},{10... | collective-permute-start | bytes 786440 | tf_op jit(solution)/shard_map/ppermute | solution.py:712
  22.7 5.3 collective-permute-start.12
  26.0 94.4 %collective-permute-start.13 = (bf16[256,4096]{1,0:T(8,128)(2,1)}, bf16[256,4096]{1,0:T(8,128)(2,1)}, u32[]{:S(2)}, u32[]{:S(2)}) collective-permute-start(bf16[256,4096]{1,0:T(8,128)(2,1)} %refs_6_.1), channel_id=1, source_target_pairs={{0,8},{8,0},{16,24},{24,16},{1,9},{9,1},{17,25},{25,17},{2,10},{10... | collective-permute-start | bytes 6291464 | tf_op jit(solution)/shard_map/ppermute | solution.py:712
  26.5 64.6 %collective-permute-start.14 = (bf16[128,4096]{1,0:T(8,128)(2,1)S(1)}, bf16[128,4096]{1,0:T(8,128)(2,1)}, u32[]{:S(2)}, u32[]{:S(2)}) collective-permute-start(bf16[128,4096]{1,0:T(8,128)(2,1)S(1)} %constant_dynamic-slice_fusion.1), channel_id=1, source_target_pairs={{0,16},{8,24},{16,0},{24,8},{1,17},{9,25},{17,1},{25,9},{2,18},{10... | collective-permute-start | bytes 3145736 | tf_op jit(solution)/shard_map/ppermute | solution.py:712
  28.1 64.6 %collective-permute-start.19 = (bf16[512,1024]{1,0:T(8,128)(2,1)S(1)}, bf16[512,1024]{1,0:T(8,128)(2,1)}, u32[]{:S(2)}, u32[]{:S(2)}) collective-permute-start(bf16[512,1024]{1,0:T(8,128)(2,1)S(1)} %constant_dynamic-slice_fusion), channel_id=1, source_target_pairs={{0,16},{8,24},{16,0},{24,8},{1,17},{9,25},{17,1},{25,9},{2,18},{10... | collective-permute-start | bytes 3145736 | tf_op jit(solution)/shard_map/ppermute | solution.py:712
  33.8 57.3 %collective-permute-start.3 = (bf16[256,1536]{1,0:T(8,128)(2,1)S(1)}, bf16[256,1536]{1,0:T(8,128)(2,1)}, u32[]{:S(2)}, u32[]{:S(2)}) collective-permute-start(bf16[256,1536]{1,0:T(8,128)(2,1)S(1)} %pad_maximum_fusion.2.refs_0_), channel_id=1, source_target_pairs={{0,16},{8,24},{16,0},{24,8},{1,17},{9,25},{17,1},{25,9},{2,18},{10... | collective-permute-start | bytes 2359304 | tf_op jit(solution)/shard_map/ppermute | solution.py:712
  36.3 66.4 %collective-permute-start.6 = (bf16[256,1024]{1,0:T(8,128)(2,1)S(1)}, bf16[256,1024]{1,0:T(8,128)(2,1)S(1)}, u32[]{:S(2)}, u32[]{:S(2)}) collective-permute-start(bf16[256,1024]{1,0:T(8,128)(2,1)S(1)} %collective-permute-done.5), channel_id=1, source_target_pairs={{2,3},{6,7},{10,11},{14,15},{18,19},{22,23},{26,27},{30,31}} | collective-permute-start | bytes 1572872 | tf_op jit(solution)/shard_map/ppermute | solution.py:819
  91.1 12.5 %collective-permute-start.4 = (bf16[256,1536]{1,0:T(8,128)(2,1)}, bf16[256,1536]{1,0:T(8,128)(2,1)}, u32[]{:S(2)}, u32[]{:S(2)}) collective-permute-start(bf16[256,1536]{1,0:T(8,128)(2,1)} %collective-permute-done.3.refs_2_), channel_id=1, source_target_pairs={{0,8},{8,0},{16,24},{24,16},{1,9},{9,1},{17,25},{25,17},{2,10},{10... | collective-permute-start | bytes 2359304 | tf_op jit(solution)/shard_map/ppermute | solution.py:712
  91.1 29.3 %collective-permute-start.16 = (bf16[128,4096]{1,0:T(8,128)(2,1)}, bf16[128,4096]{1,0:T(8,128)(2,1)}, u32[]{:S(2)}, u32[]{:S(2)}) collective-permute-start(bf16[128,4096]{1,0:T(8,128)(2,1)} %collective-permute-done.14.refs_8_), channel_id=1, source_target_pairs={{0,4},{4,0},{1,5},{5,1},{2,6},{6,2},{3,7},{7,3},{8,12},{12,8},{9,1... | collective-permute-start | bytes 3145736 | tf_op jit(solution)/shard_map/ppermute | solution.py:712
  92.6 46.9 %collective-permute-start.21 = (bf16[512,1024]{1,0:T(8,128)(2,1)}, bf16[512,1024]{1,0:T(8,128)(2,1)}, u32[]{:S(2)}, u32[]{:S(2)}) collective-permute-start(bf16[512,1024]{1,0:T(8,128)(2,1)} %collective-permute-done.19.refs_14_), channel_id=1, source_target_pairs={{0,4},{4,0},{1,5},{5,1},{2,6},{6,2},{3,7},{7,3},{8,12},{12,8},{9,1... | collective-permute-start | bytes 3145736 | tf_op jit(solution)/shard_map/ppermute | solution.py:712
  102.8 63.2 %collective-permute-start.18 = (bf16[1024,1024]{1,0:T(8,128)(2,1)}, bf16[1024,1024]{1,0:T(8,128)(2,1)S(1)}, u32[]{:S(2)}, u32[]{:S(2)}) collective-permute-start(bf16[1024,1024]{1,0:T(8,128)(2,1)} %refs_12_.1), channel_id=1, source_target_pairs={{0,8},{8,0},{16,24},{24,16},{1,9},{9,1},{17,25},{25,17},{2,10},{10... | collective-permute-start | bytes 6291464 | tf_op jit(solution)/shard_map/ppermute | solution.py:712
  103.7 61.2 %collective-permute-start.15 = (bf16[128,4096]{1,0:T(8,128)(2,1)}, bf16[128,4096]{1,0:T(8,128)(2,1)}, u32[]{:S(2)}, u32[]{:S(2)}) collective-permute-start(bf16[128,4096]{1,0:T(8,128)(2,1)} %collective-permute-done.14.refs_8_), channel_id=1, source_target_pairs={{0,8},{8,0},{16,24},{24,16},{1,9},{9,1},{17,25},{25,17},{2,10},{10... | collective-permute-start | bytes 3145736 | tf_op jit(solution)/shard_map/ppermute | solution.py:712
  120.4 45.5 %collective-permute-start.20 = (bf16[512,1024]{1,0:T(8,128)(2,1)}, bf16[512,1024]{1,0:T(8,128)(2,1)}, u32[]{:S(2)}, u32[]{:S(2)}) collective-permute-start(bf16[512,1024]{1,0:T(8,128)(2,1)} %collective-permute-done.19.refs_14_), channel_id=1, source_target_pairs={{0,8},{8,0},{16,24},{24,16},{1,9},{9,1},{17,25},{25,17},{2,10},{10... | collective-permute-start | bytes 3145736 | tf_op jit(solution)/shard_map/ppermute | solution.py:712
  120.4 61.7 %collective-permute-start.17 = (bf16[128,4096]{1,0:T(8,128)(2,1)}, bf16[128,4096]{1,0:T(8,128)(2,1)}, u32[]{:S(2)}, u32[]{:S(2)}) collective-permute-start(bf16[128,4096]{1,0:T(8,128)(2,1)} %collective-permute-done.16.refs_10_), channel_id=1, source_target_pairs={{0,8},{8,0},{16,24},{24,16},{1,9},{9,1},{17,25},{25,17},{2,10},{10... | collective-permute-start | bytes 3145736 | tf_op jit(solution)/shard_map/ppermute | solution.py:712
  139.5 42.6 %collective-permute-start.22 = (bf16[512,1024]{1,0:T(8,128)(2,1)}, bf16[512,1024]{1,0:T(8,128)(2,1)}, u32[]{:S(2)}, u32[]{:S(2)}) collective-permute-start(bf16[512,1024]{1,0:T(8,128)(2,1)} %collective-permute-done.21.refs_16_), channel_id=1, source_target_pairs={{0,8},{8,0},{16,24},{24,16},{1,9},{9,1},{17,25},{25,17},{2,10},{10... | collective-permute-start | bytes 3145736 | tf_op jit(solution)/shard_map/ppermute | solution.py:712
  164.9 17.2 %collective-permute-start.7 = (bf16[640,512]{1,0:T(8,128)(2,1)S(1)}, bf16[640,512]{1,0:T(8,128)(2,1)S(1)}, u32[]{:S(2)}, u32[]{:S(2)}) collective-permute-start(bf16[640,512]{1,0:T(8,128)(2,1)S(1)} %constant_dynamic-slice_fusion.3), channel_id=1, source_target_pairs={{0,1},{1,0},{2,3},{3,2},{4,5},{5,4},{6,7},{7,6},{8,9},{9,8},{10,11... | collective-permute-start | bytes 1966088 | tf_op jit(solution)/shard_map/ppermute | solution.py:712
  279.0 16.6 %collective-permute-start.23 = (bf16[640,512]{1,0:T(8,128)(2,1)}, bf16[640,512]{1,0:T(8,128)(2,1)S(1)}, u32[]{:S(2)}, u32[]{:S(2)}) collective-permute-start(bf16[640,512]{1,0:T(8,128)(2,1)} %get-tuple-element.73), channel_id=1, source_target_pairs={{0,1},{1,0},{2,3},{3,2},{4,5},{5,4},{6,7},{7,6},{8,9},{9,8},{10,11... | collective-permute-start | bytes 1966088 | tf_op jit(solution)/shard_map/ppermute | solution.py:712
  361.2 8.3 %collective-permute-start.27 = (bf16[2,256,1536]{2,1,0:T(8,128)(2,1)}, bf16[2,256,1536]{2,1,0:T(8,128)(2,1)S(1)}, u32[]{:S(2)}, u32[]{:S(2)}) collective-permute-start(bf16[2,256,1536]{2,1,0:T(8,128)(2,1)} %get-tuple-element.86), channel_id=1, source_target_pairs={{0,8},{8,0},{16,24},{24,16},{1,9},{9,1},{17,25},{25,17},{2,10},{10... | collective-permute-start | bytes 4718600 | tf_op jit(solution)/shard_map/ppermute | solution.py:712
  361.3 5.2 collective-permute-start.34
  361.8 120.8 %collective-permute-start.44 = (bf16[2,1024,1024]{2,1,0:T(8,128)(2,1)}, bf16[2,1024,1024]{2,1,0:T(8,128)(2,1)}, u32[]{:S(2)}, u32[]{:S(2)}) collective-permute-start(bf16[2,1024,1024]{2,1,0:T(8,128)(2,1)} %get-tuple-element.90), channel_id=1, source_target_pairs={{0,8},{8,0},{16,24},{24,16},{1,9},{9,1},{17,25},{25,17},{2,10},{10... | collective-permute-start | bytes 12582920 | tf_op jit(solution)/shard_map/ppermute | solution.py:712
  361.9 154.7 %collective-permute-start.54 = (bf16[2,1024,1024]{2,1,0:T(8,128)(2,1)}, bf16[2,1024,1024]{2,1,0:T(8,128)(2,1)}, u32[]{:S(2)}, u32[]{:S(2)}) collective-permute-start(bf16[2,1024,1024]{2,1,0:T(8,128)(2,1)} %get-tuple-element.92), channel_id=1, source_target_pairs={{0,8},{8,0},{16,24},{24,16},{1,9},{9,1},{17,25},{25,17},{2,10},{10... | collective-permute-start | bytes 12582920 | tf_op jit(solution)/shard_map/ppermute | solution.py:712
  367.9 14.8 %collective-permute-start.35 = (bf16[256,1024]{1,0:T(8,128)(2,1)S(1)}, bf16[256,1024]{1,0:T(8,128)(2,1)S(1)}, u32[]{:S(2)}, u32[]{:S(2)}) collective-permute-start(bf16[256,1024]{1,0:T(8,128)(2,1)S(1)} %fusion.3), channel_id=1, source_target_pairs={{0,16},{8,24},{16,0},{24,8},{1,17},{9,25},{17,1},{25,9},{2,18},{10... | collective-permute-start | bytes 1572872 | tf_op jit(solution)/shard_map/ppermute | solution.py:712
  370.8 33.0 %collective-permute-start.28 = (bf16[256,1536]{1,0:T(8,128)(2,1)}, bf16[256,1536]{1,0:T(8,128)(2,1)}, u32[]{:S(2)}, u32[]{:S(2)}) collective-permute-start(bf16[256,1536]{1,0:T(8,128)(2,1)} %fusion.2), channel_id=1, source_target_pairs={{0,16},{8,24},{16,0},{24,8},{1,17},{9,25},{17,1},{25,9},{2,18},{10... | collective-permute-start | bytes 2359304 | tf_op jit(solution)/shard_map/ppermute | solution.py:712
  384.1 19.6 %collective-permute-start.36 = (bf16[128,1024]{1,0:T(8,128)(2,1)S(1)}, bf16[128,1024]{1,0:T(8,128)(2,1)S(1)}, u32[]{:S(2)}, u32[]{:S(2)}) collective-permute-start(bf16[128,1024]{1,0:T(8,128)(2,1)S(1)} %dynamic-slice_convert_fusion.9), channel_id=1, source_target_pairs={{0,4},{4,0},{1,5},{5,1},{2,6},{6,2},{3,7},{7,3},{8,12},{12,8},{9,1... | collective-permute-start | bytes 786440 | tf_op jit(solution)/shard_map/ppermute | solution.py:712
  387.0 12.5 %collective-permute-start.65 = (f32[8,1024]{1,0:T(8,128)S(1)}, f32[8,1024]{1,0:T(8,128)S(1)}, u32[]{:S(2)}, u32[]{:S(2)}) collective-permute-start(f32[8,1024]{1,0:T(8,128)S(1)} %add.287), channel_id=1, source_target_pairs={{0,16},{8,24},{16,0},{24,8},{1,17},{9,25},{17,1},{25,9},{2,18},{10... | collective-permute-start | bytes 98312 | tf_op jit(solution)/shard_map/ppermute | solution.py:712
  403.4 7.7 %collective-permute-start.67 = (f32[8,1024]{1,0:T(8,128)S(1)}, f32[8,1024]{1,0:T(8,128)S(1)}, u32[]{:S(2)}, u32[]{:S(2)}) collective-permute-start(f32[8,1024]{1,0:T(8,128)S(1)} %add.289), channel_id=1, source_target_pairs={{0,1},{1,0},{2,3},{3,2},{4,5},{5,4},{6,7},{7,6},{8,9},{9,8},{10,11... | collective-permute-start | bytes 98312 | tf_op jit(solution)/shard_map/ppermute | solution.py:712
  405.7 19.1 %collective-permute-start.29 = (bf16[128,1536]{1,0:T(8,128)(2,1)S(1)}, bf16[128,1536]{1,0:T(8,128)(2,1)S(1)}, u32[]{:S(2)}, u32[]{:S(2)}) collective-permute-start(bf16[128,1536]{1,0:T(8,128)(2,1)S(1)} %dynamic-slice_convert_fusion.2), channel_id=1, source_target_pairs={{0,4},{4,0},{1,5},{5,1},{2,6},{6,2},{3,7},{7,3},{8,12},{12,8},{9,1... | collective-permute-start | bytes 1179656 | tf_op jit(solution)/shard_map/ppermute | solution.py:712
  407.5 9.3 %collective-permute-start.39 = (bf16[32,1024]{1,0:T(8,128)(2,1)S(1)}, bf16[32,1024]{1,0:T(8,128)(2,1)S(1)}, u32[]{:S(2)}, u32[]{:S(2)}) collective-permute-start(bf16[32,1024]{1,0:T(8,128)(2,1)S(1)} %get-tuple-element.124), channel_id=1, source_target_pairs={{0,3},{1,2},{2,1},{3,0},{4,7},{5,6},{6,5},{7,4},{8,11},{9,10},{10,... | collective-permute-start | bytes 196616 | tf_op jit(solution)/shard_map/ppermute | solution.py:712
  416.1 5.6 collective-permute-start.38
  422.7 6.9 collective-permute-start.40
  423.8 25.0 %collective-permute-start.41 = (bf16[32,1024]{1,0:T(8,128)(2,1)S(1)}, bf16[32,1024]{1,0:T(8,128)(2,1)S(1)}, u32[]{:S(2)}, u32[]{:S(2)}) collective-permute-start(bf16[32,1024]{1,0:T(8,128)(2,1)S(1)} %add_convert_fusion.7), channel_id=1, source_target_pairs={{0,2},{1,3},{2,0},{3,1},{4,6},{5,7},{6,4},{7,5},{8,10},{9,11},{10,... | collective-permute-start | bytes 196616 | tf_op jit(solution)/shard_map/ppermute | solution.py:712
  424.8 25.4 %collective-permute-start.42 = (bf16[32,1024]{1,0:T(8,128)(2,1)S(1)}, bf16[32,1024]{1,0:T(8,128)(2,1)S(1)}, u32[]{:S(2)}, u32[]{:S(2)}) collective-permute-start(bf16[32,1024]{1,0:T(8,128)(2,1)S(1)} %add_convert_fusion.7), channel_id=1, source_target_pairs={{0,1},{1,0},{2,3},{3,2},{4,5},{5,4},{6,7},{7,6},{8,9},{9,8},{10,11... | collective-permute-start | bytes 196616 | tf_op jit(solution)/shard_map/ppermute | solution.py:712
  429.7 91.4 %collective-permute-start.25 = (bf16[256,1024]{1,0:T(8,128)(2,1)}, bf16[256,1024]{1,0:T(8,128)(2,1)S(1)}, u32[]{:S(2)}, u32[]{:S(2)}) collective-permute-start(bf16[256,1024]{1,0:T(8,128)(2,1)} %get-tuple-element.83), channel_id=1, source_target_pairs={{2,0},{3,1},{6,4},{7,5},{10,8},{11,9},{14,12},{15,13},{18,16},{19,... | collective-permute-start | bytes 1572872 | tf_op jit(solution)/shard_map/ppermute | solution.py:867
  448.8 74.0 %collective-permute-start.26 = (bf16[256,1024]{1,0:T(8,128)(2,1)}, bf16[256,1024]{1,0:T(8,128)(2,1)S(1)}, u32[]{:S(2)}, u32[]{:S(2)}) collective-permute-start(bf16[256,1024]{1,0:T(8,128)(2,1)} %get-tuple-element.83), channel_id=1, source_target_pairs={{2,1},{3,0},{6,5},{7,4},{10,9},{11,8},{14,13},{15,12},{18,17},{19,... | collective-permute-start | bytes 1572872 | tf_op jit(solution)/shard_map/ppermute | solution.py:868
  450.3 32.3 %collective-permute-start.30 = (bf16[64,1536]{1,0:T(8,128)(2,1)S(1)}, bf16[64,1536]{1,0:T(8,128)(2,1)S(1)}, u32[]{:S(2)}, u32[]{:S(2)}) collective-permute-start(bf16[64,1536]{1,0:T(8,128)(2,1)S(1)} %dynamic-slice_convert_fusion.10), channel_id=1, source_target_pairs={{0,2},{1,3},{2,0},{3,1},{4,6},{5,7},{6,4},{7,5},{8,10},{9,11},{10,... | collective-permute-start | bytes 589832 | tf_op jit(solution)/shard_map/ppermute | solution.py:712
  482.6 41.8 %collective-permute-start.24 = (bf16[640,1024]{1,0:T(8,128)(2,1)}, bf16[640,1024]{1,0:T(8,128)(2,1)S(1)}, u32[]{:S(2)}, u32[]{:S(2)}) collective-permute-start(bf16[640,1024]{1,0:T(8,128)(2,1)} %get-tuple-element.82), channel_id=1, source_target_pairs={{0,1},{1,0},{2,3},{3,2},{4,5},{5,4},{6,7},{7,6},{8,9},{9,8},{10,11... | collective-permute-start | bytes 3932168 | tf_op jit(solution)/shard_map/ppermute | solution.py:712
  482.6 32.3 %collective-permute-start.31 = (bf16[64,1536]{1,0:T(8,128)(2,1)S(1)}, bf16[64,1536]{1,0:T(8,128)(2,1)S(1)}, u32[]{:S(2)}, u32[]{:S(2)}) collective-permute-start(bf16[64,1536]{1,0:T(8,128)(2,1)S(1)} %add_convert_fusion.6), channel_id=1, source_target_pairs={{0,2},{1,3},{2,0},{3,1},{4,6},{5,7},{6,4},{7,5},{8,10},{9,11},{10,... | collective-permute-start | bytes 589832 | tf_op jit(solution)/shard_map/ppermute | solution.py:712
  515.0 48.7 %collective-permute-start.45 = (bf16[1024,1024]{1,0:T(8,128)(2,1)S(1)}, bf16[1024,1024]{1,0:T(8,128)(2,1)}, u32[]{:S(2)}, u32[]{:S(2)}) collective-permute-start(bf16[1024,1024]{1,0:T(8,128)(2,1)S(1)} %fusion), channel_id=1, source_target_pairs={{0,16},{8,24},{16,0},{24,8},{1,17},{9,25},{17,1},{25,9},{2,18},{10... | collective-permute-start | bytes 6291464 | tf_op jit(solution)/shard_map/ppermute | solution.py:712
  516.6 16.7 %collective-permute-start.43 = (bf16[128,1024]{1,0:T(8,128)(2,1)}, bf16[128,1024]{1,0:T(8,128)(2,1)}, u32[]{:S(2)}, u32[]{:S(2)}) collective-permute-start(bf16[128,1024]{1,0:T(8,128)(2,1)} %pad_maximum_fusion.5), channel_id=1, source_target_pairs={{0,4},{4,0},{1,5},{5,1},{2,6},{6,2},{3,7},{7,3},{8,12},{12,8},{9,1... | collective-permute-start | bytes 786440 | tf_op jit(solution)/shard_map/ppermute | solution.py:712
  521.1 85.4 %collective-permute-start.55 = (bf16[1024,1024]{1,0:T(8,128)(2,1)}, bf16[1024,1024]{1,0:T(8,128)(2,1)}, u32[]{:S(2)}, u32[]{:S(2)}) collective-permute-start(bf16[1024,1024]{1,0:T(8,128)(2,1)} %fusion.1), channel_id=1, source_target_pairs={{0,16},{8,24},{16,0},{24,8},{1,17},{9,25},{17,1},{25,9},{2,18},{10... | collective-permute-start | bytes 6291464 | tf_op jit(solution)/shard_map/ppermute | solution.py:712
  522.8 12.6 %collective-permute-start.32 = (bf16[128,1536]{1,0:T(8,128)(2,1)}, bf16[128,1536]{1,0:T(8,128)(2,1)}, u32[]{:S(2)}, u32[]{:S(2)}) collective-permute-start(bf16[128,1536]{1,0:T(8,128)(2,1)} %pad_maximum_fusion.4), channel_id=1, source_target_pairs={{0,4},{4,0},{1,5},{5,1},{2,6},{6,2},{3,7},{7,3},{8,12},{12,8},{9,1... | collective-permute-start | bytes 1179656 | tf_op jit(solution)/shard_map/ppermute | solution.py:712
  537.1 74.2 %collective-permute-start.33 = (bf16[256,1536]{1,0:T(8,128)(2,1)S(1)}, bf16[256,1536]{1,0:T(8,128)(2,1)S(1)}, u32[]{:S(2)}, u32[]{:S(2)}) collective-permute-start(bf16[256,1536]{1,0:T(8,128)(2,1)S(1)} %pad_maximum_fusion.3), channel_id=1, source_target_pairs={{0,1},{1,0},{2,3},{3,2},{4,5},{5,4},{6,7},{7,6},{8,9},{9,8},{10,11... | collective-permute-start | bytes 2359304 | tf_op jit(solution)/shard_map/ppermute | solution.py:712
  567.6 44.1 %collective-permute-start.46 = (bf16[512,1024]{1,0:T(8,128)(2,1)S(1)}, bf16[512,1024]{1,0:T(8,128)(2,1)S(1)}, u32[]{:S(2)}, u32[]{:S(2)}) collective-permute-start(bf16[512,1024]{1,0:T(8,128)(2,1)S(1)} %dynamic-slice_convert_fusion.1), channel_id=1, source_target_pairs={{0,4},{4,0},{1,5},{5,1},{2,6},{6,2},{3,7},{7,3},{8,12},{12,8},{9,1... | collective-permute-start | bytes 3145736 | tf_op jit(solution)/shard_map/ppermute | solution.py:712
  610.2 23.1 %collective-permute-start.56 = (bf16[512,1024]{1,0:T(8,128)(2,1)S(1)}, bf16[512,1024]{1,0:T(8,128)(2,1)S(1)}, u32[]{:S(2)}, u32[]{:S(2)}) collective-permute-start(bf16[512,1024]{1,0:T(8,128)(2,1)S(1)} %dynamic-slice_convert_fusion), channel_id=1, source_target_pairs={{0,4},{4,0},{1,5},{5,1},{2,6},{6,2},{3,7},{7,3},{8,12},{12,8},{9,1... | collective-permute-start | bytes 3145736 | tf_op jit(solution)/shard_map/ppermute | solution.py:712
  612.1 25.2 %collective-permute-start.49 = (bf16[128,1024]{1,0:T(8,128)(2,1)S(1)}, bf16[128,1024]{1,0:T(8,128)(2,1)S(1)}, u32[]{:S(2)}, u32[]{:S(2)}) collective-permute-start(bf16[128,1024]{1,0:T(8,128)(2,1)S(1)} %get-tuple-element.104), channel_id=1, source_target_pairs={{0,3},{1,2},{2,1},{3,0},{4,7},{5,6},{6,5},{7,4},{8,11},{9,10},{10,... | collective-permute-start | bytes 786440 | tf_op jit(solution)/shard_map/ppermute | solution.py:712
  612.6 33.2 %collective-permute-start.48 = (bf16[128,1024]{1,0:T(8,128)(2,1)S(1)}, bf16[128,1024]{1,0:T(8,128)(2,1)S(1)}, u32[]{:S(2)}, u32[]{:S(2)}) collective-permute-start(bf16[128,1024]{1,0:T(8,128)(2,1)S(1)} %get-tuple-element.105), channel_id=1, source_target_pairs={{0,2},{1,3},{2,0},{3,1},{4,6},{5,7},{6,4},{7,5},{8,10},{9,11},{10,... | collective-permute-start | bytes 786440 | tf_op jit(solution)/shard_map/ppermute | solution.py:712
  615.6 30.1 %collective-permute-start.47 = (bf16[128,1024]{1,0:T(8,128)(2,1)S(1)}, bf16[128,1024]{1,0:T(8,128)(2,1)S(1)}, u32[]{:S(2)}, u32[]{:S(2)}) collective-permute-start(bf16[128,1024]{1,0:T(8,128)(2,1)S(1)} %get-tuple-element.103), channel_id=1, source_target_pairs={{0,1},{1,0},{2,3},{3,2},{4,5},{5,4},{6,7},{7,6},{8,9},{9,8},{10,11... | collective-permute-start | bytes 786440 | tf_op jit(solution)/shard_map/ppermute | solution.py:712
  633.8 13.5 %collective-permute-start.59 = (bf16[128,1024]{1,0:T(8,128)(2,1)S(1)}, bf16[128,1024]{1,0:T(8,128)(2,1)S(1)}, u32[]{:S(2)}, u32[]{:S(2)}) collective-permute-start(bf16[128,1024]{1,0:T(8,128)(2,1)S(1)} %get-tuple-element.101), channel_id=1, source_target_pairs={{0,3},{1,2},{2,1},{3,0},{4,7},{5,6},{6,5},{7,4},{8,11},{9,10},{10,... | collective-permute-start | bytes 786440 | tf_op jit(solution)/shard_map/ppermute | solution.py:712
  633.9 36.7 %collective-permute-start.58 = (bf16[128,1024]{1,0:T(8,128)(2,1)S(1)}, bf16[128,1024]{1,0:T(8,128)(2,1)S(1)}, u32[]{:S(2)}, u32[]{:S(2)}) collective-permute-start(bf16[128,1024]{1,0:T(8,128)(2,1)S(1)} %get-tuple-element.102), channel_id=1, source_target_pairs={{0,2},{1,3},{2,0},{3,1},{4,6},{5,7},{6,4},{7,5},{8,10},{9,11},{10,... | collective-permute-start | bytes 786440 | tf_op jit(solution)/shard_map/ppermute | solution.py:712
  637.3 33.3 %collective-permute-start.57 = (bf16[128,1024]{1,0:T(8,128)(2,1)S(1)}, bf16[128,1024]{1,0:T(8,128)(2,1)S(1)}, u32[]{:S(2)}, u32[]{:S(2)}) collective-permute-start(bf16[128,1024]{1,0:T(8,128)(2,1)S(1)} %get-tuple-element.100), channel_id=1, source_target_pairs={{0,1},{1,0},{2,3},{3,2},{4,5},{5,4},{6,7},{7,6},{8,9},{9,8},{10,11... | collective-permute-start | bytes 786440 | tf_op jit(solution)/shard_map/ppermute | solution.py:712
  645.9 25.6 %collective-permute-start.50 = (bf16[128,1024]{1,0:T(8,128)(2,1)S(1)}, bf16[128,1024]{1,0:T(8,128)(2,1)S(1)}, u32[]{:S(2)}, u32[]{:S(2)}) collective-permute-start(bf16[128,1024]{1,0:T(8,128)(2,1)S(1)} %add_convert_fusion.5), channel_id=1, source_target_pairs={{0,3},{1,2},{2,1},{3,0},{4,7},{5,6},{6,5},{7,4},{8,11},{9,10},{10,... | collective-permute-start | bytes 786440 | tf_op jit(solution)/shard_map/ppermute | solution.py:712
  647.2 45.9 %collective-permute-start.51 = (bf16[128,1024]{1,0:T(8,128)(2,1)S(1)}, bf16[128,1024]{1,0:T(8,128)(2,1)S(1)}, u32[]{:S(2)}, u32[]{:S(2)}) collective-permute-start(bf16[128,1024]{1,0:T(8,128)(2,1)S(1)} %add_convert_fusion.5), channel_id=1, source_target_pairs={{0,2},{1,3},{2,0},{3,1},{4,6},{5,7},{6,4},{7,5},{8,10},{9,11},{10,... | collective-permute-start | bytes 786440 | tf_op jit(solution)/shard_map/ppermute | solution.py:712
  647.2 45.9 %collective-permute-start.52 = (bf16[128,1024]{1,0:T(8,128)(2,1)S(1)}, bf16[128,1024]{1,0:T(8,128)(2,1)S(1)}, u32[]{:S(2)}, u32[]{:S(2)}) collective-permute-start(bf16[128,1024]{1,0:T(8,128)(2,1)S(1)} %add_convert_fusion.5), channel_id=1, source_target_pairs={{0,1},{1,0},{2,3},{3,2},{4,5},{5,4},{6,7},{7,6},{8,9},{9,8},{10,11... | collective-permute-start | bytes 786440 | tf_op jit(solution)/shard_map/ppermute | solution.py:712
  670.8 23.6 %collective-permute-start.60 = (bf16[128,1024]{1,0:T(8,128)(2,1)S(1)}, bf16[128,1024]{1,0:T(8,128)(2,1)S(1)}, u32[]{:S(2)}, u32[]{:S(2)}) collective-permute-start(bf16[128,1024]{1,0:T(8,128)(2,1)S(1)} %add_convert_fusion.4), channel_id=1, source_target_pairs={{0,3},{1,2},{2,1},{3,0},{4,7},{5,6},{6,5},{7,4},{8,11},{9,10},{10,... | collective-permute-start | bytes 786440 | tf_op jit(solution)/shard_map/ppermute | solution.py:712
  671.5 32.6 %collective-permute-start.61 = (bf16[128,1024]{1,0:T(8,128)(2,1)S(1)}, bf16[128,1024]{1,0:T(8,128)(2,1)S(1)}, u32[]{:S(2)}, u32[]{:S(2)}) collective-permute-start(bf16[128,1024]{1,0:T(8,128)(2,1)S(1)} %add_convert_fusion.4), channel_id=1, source_target_pairs={{0,2},{1,3},{2,0},{3,1},{4,6},{5,7},{6,4},{7,5},{8,10},{9,11},{10,... | collective-permute-start | bytes 786440 | tf_op jit(solution)/shard_map/ppermute | solution.py:712
  671.5 32.6 %collective-permute-start.62 = (bf16[128,1024]{1,0:T(8,128)(2,1)S(1)}, bf16[128,1024]{1,0:T(8,128)(2,1)S(1)}, u32[]{:S(2)}, u32[]{:S(2)}) collective-permute-start(bf16[128,1024]{1,0:T(8,128)(2,1)S(1)} %add_convert_fusion.4), channel_id=1, source_target_pairs={{0,1},{1,0},{2,3},{3,2},{4,5},{5,4},{6,7},{7,6},{8,9},{9,8},{10,11... | collective-permute-start | bytes 786440 | tf_op jit(solution)/shard_map/ppermute | solution.py:712
  693.3 26.1 %collective-permute-start.53 = (bf16[512,1024]{1,0:T(8,128)(2,1)S(1)}, bf16[512,1024]{1,0:T(8,128)(2,1)S(1)}, u32[]{:S(2)}, u32[]{:S(2)}) collective-permute-start(bf16[512,1024]{1,0:T(8,128)(2,1)S(1)} %pad_maximum_fusion), channel_id=1, source_target_pairs={{0,4},{4,0},{1,5},{5,1},{2,6},{6,2},{3,7},{7,3},{8,12},{12,8},{9,1... | collective-permute-start | bytes 3145736 | tf_op jit(solution)/shard_map/ppermute | solution.py:712
  704.3 36.2 %collective-permute-start.63 = (bf16[512,1024]{1,0:T(8,128)(2,1)S(1)}, bf16[512,1024]{1,0:T(8,128)(2,1)S(1)}, u32[]{:S(2)}, u32[]{:S(2)}) collective-permute-start(bf16[512,1024]{1,0:T(8,128)(2,1)S(1)} %pad_maximum_fusion.1), channel_id=1, source_target_pairs={{0,4},{4,0},{1,5},{5,1},{2,6},{6,2},{3,7},{7,3},{8,12},{12,8},{9,1... | collective-permute-start | bytes 3145736 | tf_op jit(solution)/shard_map/ppermute | solution.py:712
  (29 other events, 424.8 us)

commit v2 on v1

--- a/solution.py
+++ b/solution.py
@@ -708,6 +708,268 @@
     )(info, *arrays)
 
 
+def peer(axis, mask):
+    return {axis: lax.axis_index(axis) ^ mask}
+
+
+def greet(partners):
+    barrier = pltpu.get_barrier_semaphore()
+    for p in partners:
+        pl.semaphore_signal(barrier, inc=1, device_id=p, device_id_type=pl.DeviceIdType.MESH)
+    pl.semaphore_wait(barrier, len(partners))
+
+
+def remote(src, dst, send, recv, to):
+    return pltpu.make_async_remote_copy(
+        src_ref=src, dst_ref=dst, send_sem=send, recv_sem=recv, device_id=to, device_id_type=pl.DeviceIdType.MESH
+    )
+
+
+class Lane:
+    names = ("core_s", "core_r", "y_s", "y_r", "x_s", "x_r", "z_s", "z_r", "zz_s", "zz_r", "xx_s", "xx_r", "own")
+
+    @staticmethod
+    def scratch(count, rows, cols, fsdp, dp, masks):
+        y, parts = fsdp // 2, len(masks) + 1
+        dma = pltpu.SemaphoreType.DMA
+        sems = [(count,), (count,)]
+        sems += [(count, max(y - 1, 1))] * 2 + [(count, max(dp - 1, 1))] * 2
+        sems += [(count, len(masks))] * 4 + [(count, max(dp - 1, 1))] * 2 + [(count,)]
+        return [
+            pltpu.VMEM((count, y, rows, cols), BF16),
+            pltpu.VMEM((count, max(y - 1, 1), rows, cols), BF16),
+            pltpu.VMEM((count, max(dp - 1, 1), rows // dp, cols), BF16),
+            pltpu.VMEM((count, len(masks), rows // dp, cols // parts), BF16),
+        ] + [dma(s) for s in sems]
+
+    size = 4 + 13
+
+    def __init__(self, refs, final, fsdp, dp, masks, unit):
+        self.acc, self.y_in, self.x_in, self.z_in = refs[:4]
+        self.sems = dict(zip(self.names, refs[4:]))
+        self.final = final
+        self.ys, self.dp, self.masks = fsdp // 2, dp, masks
+        self.count, _, self.rows, self.cols = self.acc.shape
+        self.x = lax.axis_index("dp")
+        self.part = self.cols // (len(masks) + 1)
+        self.unit = unit
+
+    def place(self, mask=0):
+        at = (lax.axis_index("seq") ^ mask) // self.unit % (len(self.masks) + 1)
+        return pl.ds(pl.multiple_of(at * self.part, 128), self.part)
+
+    def band(self, mask=0):
+        n = self.rows // self.dp
+        return pl.ds(pl.multiple_of((self.x ^ mask) * n, 16), n)
+
+    def core(self, u, src):
+        return remote(src, self.acc.at[u], self.sems["core_s"].at[u], self.sems["core_r"].at[u], peer("fsdp", 1))
+
+    def over_y(self, u, ry):
+        s = self.sems
+        return remote(
+            self.acc.at[u, ry], self.y_in.at[u, ry - 1], s["y_s"].at[u, ry - 1], s["y_r"].at[u, ry - 1], peer("fsdp", 2 * ry)
+        )
+
+    def over_x(self, u, rx):
+        s = self.sems
+        return remote(
+            self.acc.at[u, 0, self.band(rx)],
+            self.x_in.at[u, rx - 1],
+            s["x_s"].at[u, rx - 1],
+            s["x_r"].at[u, rx - 1],
+            peer("dp", rx),
+        )
+
+    def over_z(self, u, i):
+        s, m = self.sems, self.masks[i]
+        return remote(
+            self.acc.at[u, 0, self.band(), self.place(m)],
+            self.z_in.at[u, i],
+            s["z_s"].at[u, i],
+            s["z_r"].at[u, i],
+            peer("seq", m),
+        )
+
+    def back_z(self, u, i):
+        s, m = self.sems, self.masks[i]
+        return remote(
+            self.acc.at[u, 0, self.band(), self.place()],
+            self.final.at[u, self.band(), self.place()],
+            s["zz_s"].at[u, i],
+            s["zz_r"].at[u, i],
+            peer("seq", m),
+        )
+
+    def back_x(self, u, rx):
+        s = self.sems
+        at = self.final.at[u, self.band()]
+        return remote(at, at, s["xx_s"].at[u, rx - 1], s["xx_r"].at[u, rx - 1], peer("dp", rx))
+
+    def keep(self, u):
+        return pltpu.make_async_copy(
+            self.acc.at[u, 0, self.band(), self.place()],
+            self.final.at[u, self.band(), self.place()],
+            self.sems["own"].at[u],
+        )
+
+    def add(self, target, sources):
+        rows = target.shape[0]
+        step = 64 if rows % 64 == 0 else 16
+
+        def body(i, carry):
+            at = pl.ds(pl.multiple_of(i * step, 16), step)
+            total = target[at, :].astype(F32)
+            for src in sources:
+                total = total + src[at, :].astype(F32)
+            target[at, :] = total.astype(BF16)
+            return carry
+
+        lax.fori_loop(0, rows // step, body, 0)
+
+    def one(self, u, keep):
+        self.core(u, keep).wait_recv()
+        for ry in range(self.ys):
+            self.add(self.acc.at[u, ry], [keep.at[ry]])
+        for ry in range(1, self.ys):
+            self.over_y(u, ry).start()
+
+    def two(self, u):
+        for ry in range(1, self.ys):
+            self.over_y(u, ry).wait_recv()
+        self.add(self.acc.at[u, 0], [self.y_in.at[u, ry - 1] for ry in range(1, self.ys)])
+        for rx in range(1, self.dp):
+            self.over_x(u, rx).start()
+
+    def three(self, u):
+        for rx in range(1, self.dp):
+            self.over_x(u, rx).wait_recv()
+        self.add(self.acc.at[u, 0, self.band()], [self.x_in.at[u, rx - 1] for rx in range(1, self.dp)])
+        for i in range(len(self.masks)):
+            self.over_z(u, i).start()
+
+    def four(self, u):
+        for i in range(len(self.masks)):
+            self.over_z(u, i).wait_recv()
+        self.add(
+            self.acc.at[u, 0, self.band(), self.place()], [self.z_in.at[u, i] for i in range(len(self.masks))]
+        )
+        self.keep(u).start()
+        for i in range(len(self.masks)):
+            self.back_z(u, i).start()
+
+    def five(self, u):
+        self.keep(u).wait()
+        for i in range(len(self.masks)):
+            self.back_z(u, i).wait_recv()
+        for rx in range(1, self.dp):
+            self.back_x(u, rx).start()
+
+    def six(self, u):
+        for rx in range(1, self.dp):
+            self.back_x(u, rx).wait_recv()
+
+    def drain(self, u, src):
+        self.core(u, src).wait_send()
+        for ry in range(1, self.ys):
+            self.over_y(u, ry).wait_send()
+        for rx in range(1, self.dp):
+            self.over_x(u, rx).wait_send()
+            self.back_x(u, rx).wait_send()
+        for i in range(len(self.masks)):
+            self.over_z(u, i).wait_send()
+            self.back_z(u, i).wait_send()
+
+
+def partners(fsdp, dp):
+    return (
+        [peer("fsdp", 1)]
+        + [peer("fsdp", 2 * ry) for ry in range(1, fsdp // 2)]
+        + [peer("dp", rx) for rx in range(1, dp)]
+        + [peer("seq", m) for m in (1, 2, 3)]
+    )
+
+
+def reduce_body(*refs, fsdp, dp, layout):
+    n_in = len(layout)
+    keeps, sends = refs[:n_in], refs[n_in : 2 * n_in]
+    final_a, final_b = refs[2 * n_in : 2 * n_in + 2]
+    rest = refs[2 * n_in + 2 :]
+    held_a, held_b, load_a, load_b = rest[:4]
+    a = Lane(rest[4 : 4 + Lane.size], final_a, fsdp, dp, (1, 2, 3), 1)
+    b = Lane(rest[4 + Lane.size :], final_b, fsdp, dp, (2,), 2)
+    greet(partners(fsdp, dp))
+
+    def views(lane, held, load):
+        u = 0
+        for i, (kind, cuts) in enumerate(layout):
+            if kind != (lane is b):
+                continue
+            for cut in range(cuts):
+                if kind:
+                    at = (slice(None), slice(None), pl.ds(cut * lane.cols, lane.cols))
+                else:
+                    at = (slice(None), pl.ds(cut * lane.rows, lane.rows))
+                yield u, sends[i].at[at], functools.partial(
+                    pltpu.make_async_copy, keeps[i].at[at], held.at[u], load.at[u]
+                )
+                u += 1
+
+    lanes = ((a, held_a, load_a), (b, held_b, load_b))
+    for lane, held, load in lanes:
+        for u, src, copy in views(lane, held, load):
+            lane.core(u, src).start()
+            copy().start()
+    for lane, held, load in lanes:
+        for u, src, copy in views(lane, held, load):
+            copy().wait()
+    total = a.count + b.count
+
+    def tick(t, carry):
+        for offset, name in ((0, "one"), (2, "two"), (3, "three"), (4, "four"), (5, "five"), (6, "six")):
+            for lane, held, first in ((a, held_a, 0), (b, held_b, a.count)):
+                u = t - offset - first
+
+                @pl.when((u >= 0) & (u < lane.count))
+                def _():
+                    if name == "one":
+                        lane.one(u, held.at[u])
+                    else:
+                        getattr(lane, name)(u)
+
+        return carry
+
+    lax.fori_loop(0, total + 6, tick, 0)
+    for lane, held, load in lanes:
+        for u, src, copy in views(lane, held, load):
+            lane.drain(u, src)
+
+
+def reduce_all(pairs, fsdp, dp):
+    d = pairs[0][0].shape[2]
+    rows = d // fsdp
+    layout = tuple((False, k.shape[1] // rows) for k, _ in pairs[:-1]) + ((True, 3),)
+    n_a = sum(c for kind, c in layout if not kind)
+    wide = pairs[-1][0].shape[2] // 3
+    y = fsdp // 2
+    return pl.pallas_call(
+        functools.partial(reduce_body, fsdp=fsdp, dp=dp, layout=layout),
+        in_specs=[hbm()] * (2 * len(pairs)),
+        out_specs=[hbm(), hbm()],
+        out_shape=[shape((n_a, rows, d), BF16), shape((3, rows, wide), BF16)],
+        scratch_shapes=[
+            pltpu.VMEM((n_a, y, rows, d), BF16),
+            pltpu.VMEM((3, y, rows, wide), BF16),
+            pltpu.SemaphoreType.DMA((n_a,)),
+            pltpu.SemaphoreType.DMA((3,)),
+        ]
+        + Lane.scratch(n_a, rows, d, fsdp, dp, (1, 2, 3))
+        + Lane.scratch(3, rows, wide, fsdp, dp, (2,)),
+        compiler_params=pltpu.CompilerParams(vmem_limit_bytes=VMEM_LIMIT, collective_id=0, has_side_effects=True),
+        cost_estimate=pl.CostEstimate(flops=10**8, bytes_accessed=5 * 10**8, transcendentals=0),
+    )(*[k for k, _ in pairs], *[s for _, s in pairs])
+
+
 def hop(value, axis, mask):
     return lax.ppermute(value, axis, [(i, i ^ mask) for i in range(lax.axis_size(axis))])
 
@@ -752,35 +1014,6 @@
         pieces += [got, hop(got, "fsdp", 1)]
         places += [(f ^ (2 * ry)) * rows, (f ^ (2 * ry + 1)) * rows]
     return pieces, places
-
-
-def add_hop(total, value, axis, mask):
-    return total + hop(value.astype(BF16), axis, mask).astype(F32)
-
-
-def split_sum(value, count, axis, unit, index):
-    total = part_of(value, count, index)
-    for m in range(1, count):
-        total = add_hop(total, part_of(value, count, index ^ m), axis, m * unit)
-    return total
-
-
-def join(value, count, axis, unit, index):
-    pieces = [value] + [hop(value, axis, m * unit) for m in range(1, count)]
-    return jnp.concatenate(arrange(pieces, index), axis=0)
-
-
-def reduce_shard(keep, send, x, s, pair_done):
-    got = hop(send, "fsdp", 1)
-    total = keep[0].astype(F32) + got[0].astype(F32)
-    for ry in range(1, keep.shape[0]):
-        total = add_hop(total, keep[ry].astype(F32) + got[ry].astype(F32), "fsdp", 2 * ry)
-    dp = lax.axis_size("dp")
-    part = split_sum(total, dp, "dp", 1, x)
-    count, unit, index = (2, 2, s // 2) if pair_done else (lax.axis_size("seq"), 1, s)
-    part = split_sum(part, count, "seq", unit, index)
-    part = join(part.astype(BF16), count, "seq", unit, index)
-    return join(part, dp, "dp", 1, x)
 
 
 def sum_all(value):
@@ -874,15 +1107,18 @@
         )
     )
 
-    reduced = [reduce_shard(a, b, x, s, False) for a, b in keeps]
-    grad_proj = reduce_shard(keep_o, send_o, x, s, False).astype(F32)
-    half_q = reduce_shard(keep_q, send_q, x, s, True)
+    dp = lax.axis_size("dp")
+    done, done_q = reduce_all(keeps + [(keep_o, send_o), (keep_q, send_q)], fsdp, dp)
+    rows = d // fsdp
+    per = (done.shape[0] - 1) // GROUPS
+    reduced = [done[g * per : (g + 1) * per].reshape(per * rows, d) for g in range(GROUPS)]
+    grad_proj = done[-1].astype(F32)
+    half_q = jnp.concatenate([done_q[0], done_q[1], done_q[2]], axis=1)
     both = arrange([half_q, hop(half_q, "seq", 1)], parity)
     grad_qkv = jnp.concatenate(
         [both[h][:, c * half : (c + 1) * half] for c in range(3) for h in range(2)], axis=1
     ).astype(F32)
     tile = ff // fsdp // GROUPS
-    rows = d // fsdp
     grad_down = jnp.concatenate([r[:tile] for r in reduced], axis=0).astype(F32)
     piece = d // fsdp
     blocks = []

time: 757 us -> 601 us (0.79)
  the two profiles are of different devices: /device:TPU:0 before, /device:TPU:20 now
where the time goes in v2:
time: 601 us; the launch traced here: 591 us
  Pallas kernels  384 us (64%)
  waiting for transfers between devices  129 us (21%)
  starting transfers between devices  30.4 us (5%)
  local copies, waits for them, and re-layouts  28.2 us (5%)
  other arithmetic  12.9 us (2%)
  between operations  6.14 us (1%)
    pallas_call x1, Pallas kernels, reduce_all(): pl.pallas_call(functools.partial(reduce_body, fsdp=fsdp, dp=dp, layout=la...  175 us
    ppermute x29, waiting for transfers between devices, hop(): lax.ppermute(value, axis, [(i, i ^ mask) for i in range(lax.axis_size(axi...  129 us
    pallas_call x2, Pallas kernels, back_group(): call(functools.partial(back_body, fsdp=fsdp), (fsdp,), 1, [full((local, d...  45.5 us
    pallas_call x1, Pallas kernels, attend_back(): call(attend_back_body, (pairs,), 1, [pair, pair, pair, pad, pad, pair, pl...  44.9 us
    pallas_call x1, Pallas kernels, forward(): call(functools.partial(forward_body, counts=counts), (ff // tile,), 2, [p...  35.8 us
    pallas_call x1, Pallas kernels, attend(): call(attend_body, (pairs,), 1, [pair, pair, pair, pad, pad], [pair, pl.Bl...  24.3 us
    ppermute x29, starting transfers between devices, hop(): lax.ppermute(value, axis, [(i, i ^ mask) for i in range(lax.axis_size(axi...  20.4 us
    pallas_call x1, Pallas kernels, project_back(): call(functools.partial(project_back_body, fsdp=fsdp), (2,), 1, [pl.BlockS...  19.5 us
  transfers between devices with their start and end apart: 33, of which 11 were waited for; matrix products, arithmetic and copies ran while one was open for 7% of the time, Pallas kernels for 36%

profile of v2, /device:TPU:20, one launch (start us, length us, event | category | flops | bytes accessed | tf_op | source)
XLA Modules:
  0.0 590.7 jit_solution(1378521425816490227)
XLA Ops:
  0.7 1.1 constant_dynamic-slice_fusion.2
  2.4 1.9 slice_bitcast_fusion.1
  4.2 1.6 collective-permute-start
  6.4 1.4 constant_dynamic-slice_fusion
  7.8 2.8 collective-permute-done.9.refs_2_
  10.6 1.5 collective-permute-start.11
  12.3 6.4 %collective-permute-done.11.refs_4_ = bf16[128,1024]{1,0:T(8,128)(2,1)S(1)} collective-permute-done((bf16[128,1024]{1,0:T(8,128)(2,1)}, bf16[128,1024]{1,0:T(8,128)(2,1)S(1)}, u32[]{:S(2)}, u32[]{:S(2)}) %collective-permute-start.11) | collective-permute-done | bytes 262176 | tf_op jit(solution)/shard_map/ppermute | solution.py:974
  19.2 1.5 collective-permute-start.19
  22.1 0.6 iota_compare_fusion
  23.2 12.2 %collective-permute-done.1.rest = bf16[384,1024]{1,0:T(8,128)(2,1)} collective-permute-done((bf16[384,1024]{1,0:T(8,128)(2,1)S(1)}, bf16[384,1024]{1,0:T(8,128)(2,1)}, u32[]{:S(2)}, u32[]{:S(2)}) %collective-permute-start.1) | collective-permute-done | bytes 786464 | tf_op jit(solution)/shard_map/ppermute | solution.py:974
  35.4 1.3 collective-permute-start.5
  36.7 2.6 collective-permute-done.3.refs_2_
  39.3 22.5 %collective-permute-done.19.refs_14_ = bf16[512,1024]{1,0:T(8,128)(2,1)} collective-permute-done((bf16[512,1024]{1,0:T(8,128)(2,1)S(1)}, bf16[512,1024]{1,0:T(8,128)(2,1)}, u32[]{:S(2)}, u32[]{:S(2)}) %collective-permute-start.19) | collective-permute-done | bytes 1048608 | tf_op jit(solution)/shard_map/ppermute | solution.py:974
  61.7 1.5 collective-permute-start.21
  63.2 3.5 collective-permute-start.6
  66.8 15.1 %collective-permute-done.14.refs_8_ = bf16[128,4096]{1,0:T(8,128)(2,1)} collective-permute-done((bf16[128,4096]{1,0:T(8,128)(2,1)S(1)}, bf16[128,4096]{1,0:T(8,128)(2,1)}, u32[]{:S(2)}, u32[]{:S(2)}) %collective-permute-start.14) | collective-permute-done | bytes 1048608 | tf_op jit(solution)/shard_map/ppermute | solution.py:974
  81.9 1.6 collective-permute-start.16
  88.6 1.3 slice.187.bias
  89.9 1.3 slice.186.gain
  91.2 1.3 stack.94.info
  93.6 0.9 broadcast_select_fusion.2.x.padx
  94.8 12.2 %shard_map.161 = (bf16[1280,512]{1,0:T(8,128)(2,1)}, bf16[1280,512]{1,0:T(8,128)(2,1)}, bf16[1280,512]{1,0:T(8,128)(2,1)}, bf16[1024,1280]{1,0:T(8,128)(2,1)}, bf16[1024,1536]{1,0:T(8,128)(2,1)}) custom-call(s32[9]{0:T(128)} %stack.94.info, s32[4]{0:T(128)} %pad_add_fusion.pos, bf16[640,1024]{1,0:T(8,128)(2,1)} %bitcast.50, bf16[256,1024]{1,0:T(8,128)(2,1)} %copy-done.9, ...), custom_call_target="tpu_custom_call" | custom-call | flops 4026531840 | bytes 16000000 | tf_op jit(solution)/shard_map/pallas_call | solution.py:126
  107.0 4.0 shard_map.162
  111.4 24.3 %shard_map.163 = (bf16[1280,512]{1,0:T(8,128)(2,1)}, f32[4,2,1280]{2,1,0:T(2,128)}) custom-call(s32[9]{0:T(128)} %stack.94.info, bf16[1280,512]{1,0:T(8,128)(2,1)} %get-tuple-element.54.q, bf16[1280,512]{1,0:T(8,128)(2,1)} %get-tuple-element.55.k, bf16[1280,512]{1,0:T(8,128)(2,1)} %get-tuple-element.56.v, bf16[256,512]{1,0:T(8,128)(2,1)} %get-tuple-element.58.kp, ...), custom_call_target="tpu_custom_call" | custom-call | flops 9126805504 | bytes 6000000 | tf_op jit(solution)/shard_map/pallas_call | solution.py:226
  135.7 1.1 constant_dynamic-slice_fusion.3
  136.9 1.7 collective-permute-start.7
  138.5 0.6 stack.107.pos
  139.2 14.7 %collective-permute-done.7.other = bf16[640,512]{1,0:T(8,128)(2,1)S(1)} collective-permute-done((bf16[640,512]{1,0:T(8,128)(2,1)S(1)}, bf16[640,512]{1,0:T(8,128)(2,1)S(1)}, u32[]{:S(2)}, u32[]{:S(2)}) %collective-permute-start.7) | collective-permute-done | bytes 655392 | tf_op jit(solution)/shard_map/ppermute | solution.py:974
  153.9 0.8 copy-done.7
  155.1 35.8 %shard_map.164 = (bf16[640,1024]{1,0:T(8,128)(2,1)}, bf16[640,1024]{1,0:T(8,128)(2,1)}, bf16[4096,640]{1,0:T(8,128)(2,1)}, bf16[640,4096]{1,0:T(8,128)(2,1)}, bf...) custom-call(s32[9]{0:T(128)} %stack.94.info, ...), custom_call_target="tpu_custom_call" | custom-call | flops 12079595520 | bytes 60000000 | tf_op jit(solution)/shard_map/pallas_call | solution.py:441
  190.9 22.9 %shard_map.166 = (bf16[2,1024,1024]{2,1,0:T(8,128)(2,1)}, bf16[2,1024,1024]{2,1,0:T(8,128)(2,1)}, f32[640,1024]{1,0:T(8,128)}) custom-call(s32[9]{0:T(128)} %stack.94.info, bf16[640,1024]{1,0:T(8,128)(2,1)} %get-tuple-element.63.g_feed, bf16[1024,640]{1,0:T(8,128)(2,1)} %get-tuple-element.64.n_t, bf16[4096,640]{1,0:T(8,128)(2,1)} %get-tuple-element.65.act_t, ...), custom_call_target="tpu_custom_call" | custom-call | flops 10737418240 | bytes 40000000 | tf_op jit(solution)/shard_map/pallas_call | solution.py:540
  213.7 22.6 %shard_map.165 = (bf16[2,1024,1024]{2,1,0:T(8,128)(2,1)}, bf16[2,1024,1024]{2,1,0:T(8,128)(2,1)}, f32[640,1024]{1,0:T(8,128)}) custom-call(s32[9]{0:T(128)} %stack.94.info, bf16[640,1024]{1,0:T(8,128)(2,1)} %get-tuple-element.63.g_feed, bf16[1024,640]{1,0:T(8,128)(2,1)} %get-tuple-element.64.n_t, bf16[4096,640]{1,0:T(8,128)(2,1)} %get-tuple-element.65.act_t, ...), custom_call_target="tpu_custom_call" | custom-call | flops 10737418240 | bytes 40000000 | tf_op jit(solution)/shard_map/pallas_call | solution.py:540
  236.4 15.2 %shard_map.167 = (f32[640,1024]{1,0:T(8,128)}, bf16[640,512]{1,0:T(8,128)(2,1)}, bf16[640,512]{1,0:T(8,128)(2,1)}, bf16[2,256,1024]{2,1,0:T(8,128)(2,1)}, bf16[2...) custom-call(s32[9]{0:T(128)} %stack.94.info, f32[640,1024]{1,0:T(8,128)} %get-tuple-element.69.ga, ...), custom_call_target="tpu_custom_call" | custom-call | flops 2684354560 | bytes 22000000 | tf_op jit(solution)/shard_map/pallas_call | solution.py:600
  251.6 1.6 collective-permute-start.23
  253.3 0.9 fusion.3
  254.2 13.9 %collective-permute-done.23.d_other = bf16[640,512]{1,0:T(8,128)(2,1)S(1)} collective-permute-done((bf16[640,512]{1,0:T(8,128)(2,1)}, bf16[640,512]{1,0:T(8,128)(2,1)S(1)}, u32[]{:S(2)}, u32[]{:S(2)}) %collective-permute-start.23) | collective-permute-done | bytes 655392 | tf_op jit(solution)/shard_map/ppermute | solution.py:974
  268.1 0.8 copy-done.19
  268.9 44.9 %shard_map.168 = (bf16[1280,512]{1,0:T(8,128)(2,1)}, bf16[1280,512]{1,0:T(8,128)(2,1)}, bf16[1280,512]{1,0:T(8,128)(2,1)}, bf16[256,512]{1,0:T(8,128)(2,1)}, bf16[256,512]{1,0:T(8,128)(2,1)}) custom-call(s32[9]{0:T(128)} %stack.94.info, bf16[1280,512]{1,0:T(8,128)(2,1)} %get-tuple-element.54.q, bf16[1280,512]{1,0:T(8,128)(2,1)} %get-tuple-element.55.k, ...), custom_call_target="tpu_custom_call" | custom-call | flops 22817013760 | bytes 14000000 | tf_op jit(solution)/shard_map/pallas_call | solution.py:326
  313.8 19.5 %shard_map.169 = (f32[640,1024]{1,0:T(8,128)}, bf16[640,1024]{1,0:T(8,128)(2,1)}, bf16[256,1024]{1,0:T(8,128)(2,1)}, bf16[2,256,1536]{2,1,0:T(8,128)(2,1)}, bf16...) custom-call(s32[9]{0:T(128)} %stack.94.info, bf16[640,1024]{1,0:T(8,128)(2,1)} %bitcast.52, bf16[256,1024]{1,0:T(8,128)(2,1)} %copy-done.9, ...), custom_call_target="tpu_custom_call" | custom-call | flops 8053063680 | bytes 24000000 | tf_op jit(solution)/shard_map/pallas_call | solution.py:666
  333.3 3.1 collective-permute-start.26
  336.5 2.1 collective-permute-start.25
  338.6 174.9 %shard_map.171 = (bf16[9,256,1024]{2,1,0:T(8,128)(2,1)}, bf16[3,256,512]{2,1,0:T(8,128)(2,1)}) custom-call(bf16[2,1024,1024]{2,1,0:T(8,128)(2,1)} %get-tuple-element.87.refs_0_, bf16[2,1024,1024]{2,1,0:T(8,128)(2,1)} %get-tuple-element.88.refs_1_, bf16[2,256,1024]{2,1,0:T(8,128)(2,1)} %get-tuple-element.89.refs_2_, ...), custom_call_target="tpu_custom_call" | custom-call | flops 100000000 | bytes 500000000 | tf_op jit(solution)/shard_map/pallas_call | solution.py:955
  513.4 2.3 bitcast_convert_fusion
  515.7 2.8 fusion
  518.5 1.8 fusion.1
  520.3 0.9 slice_bitcast_fusion.4
  521.3 1.1 pad_maximum_fusion.1
  522.5 2.0 collective-permute-start.24
  524.5 0.9 slice_dynamic-update-slice_fusion.21
  525.4 0.9 slice_dynamic-update-slice_fusion.20
  526.4 1.0 slice_dynamic-update-slice_fusion.17
  527.4 0.9 slice_dynamic-update-slice_fusion.16
  528.4 0.9 slice_dynamic-update-slice_fusion.13
  529.3 0.9 slice_dynamic-update-slice_fusion.12
  530.3 0.9 slice_dynamic-update-slice_fusion.9
  531.3 0.9 slice_dynamic-update-slice_fusion.8
  532.2 3.0 collective-permute-done.29
  535.2 3.9 collective-permute-done.30
  539.2 32.0 %collective-permute-done.31 = f32[8,1024]{1,0:T(8,128)S(1)} collective-permute-done((f32[8,1024]{1,0:T(8,128)S(1)}, f32[8,1024]{1,0:T(8,128)S(1)}, u32[]{:S(2)}, u32[]{:S(2)}) %collective-permute-start.31) | collective-permute-done | bytes 32800 | tf_op jit(solution)/shard_map/ppermute | solution.py:974
  571.2 3.2 collective-permute-start.32
  574.4 2.5 maximum_convert_fusion
  576.8 2.5 convert_element_type.18
  580.5 2.0 convert_element_type.15
  582.5 7.8 %shard_map.170 = bf16[640,1024]{1,0:T(8,128)(2,1)} custom-call(s32[9]{0:T(128)} %stack.94.info, bf16[640,1024]{1,0:T(8,128)(2,1)} %bitcast.53, f32[640,1024]{1,0:T(8,128)} %get-tuple-element.83.g_own, bf16[640,1024]{1,0:T(8,128)(2,1)} %collective-permute-done.24.g_other, bf16[256,1024]{1,0:T(8,128)(2,1)} %collective-permute-done.25.pad_a, ...), custom_call_target="tpu_custom_call" | custom-call | flops 10000000 | bytes 12000000 | tf_op jit(solution)/shard_map/pallas_call | solution.py:698
  (117 shorter events, 8.2 us)
Async XLA Ops:
  0.6 5.2 copy-start.1
  0.6 20.9 %collective-permute-start.8 = (bf16[256,1024]{1,0:T(8,128)(2,1)}, bf16[256,1024]{1,0:T(8,128)(2,1)}, u32[]{:S(2)}, u32[]{:S(2)}) collective-permute-start(bf16[256,1024]{1,0:T(8,128)(2,1)} %refs_0_.1), channel_id=1, source_target_pairs={{0,8},{8,0},{16,24},{24,16},{1,9},{9,1},{17,25},{25,17},{2,10},{10... | collective-permute-start | bytes 1572872 | tf_op jit(solution)/shard_map/ppermute | solution.py:974
  1.8 8.8 %collective-permute-start.9 = (bf16[128,1024]{1,0:T(8,128)(2,1)S(1)}, bf16[128,1024]{1,0:T(8,128)(2,1)}, u32[]{:S(2)}, u32[]{:S(2)}) collective-permute-start(bf16[128,1024]{1,0:T(8,128)(2,1)S(1)} %constant_dynamic-slice_fusion.2), channel_id=1, source_target_pairs={{0,16},{8,24},{16,0},{24,8},{1,17},{9,25},{17,1},{25,9},{2,18},{10... | collective-permute-start | bytes 786440 | tf_op jit(solution)/shard_map/ppermute | solution.py:974
  4.2 16.5 %collective-permute-start = (bf16[256,1024]{1,0:T(8,128)(2,1)}, bf16[256,1024]{1,0:T(8,128)(2,1)S(1)}, u32[]{:S(2)}, u32[]{:S(2)}) collective-permute-start(bf16[256,1024]{1,0:T(8,128)(2,1)} %slice_bitcast_fusion.1), channel_id=1, source_target_pairs={{0,1},{1,0},{2,3},{3,2},{4,5},{5,4},{6,7},{7,6},{8,9},{9,8},{10,11... | collective-permute-start | bytes 1572872 | tf_op jit(solution)/shard_map/ppermute | solution.py:974
  5.9 29.5 %collective-permute-start.1 = (bf16[384,1024]{1,0:T(8,128)(2,1)S(1)}, bf16[384,1024]{1,0:T(8,128)(2,1)}, u32[]{:S(2)}, u32[]{:S(2)}) collective-permute-start(bf16[384,1024]{1,0:T(8,128)(2,1)S(1)} %slice_bitcast_fusion), channel_id=1, source_target_pairs={{0,1},{1,0},{2,3},{3,2},{4,5},{5,4},{6,7},{7,6},{8,9},{9,8},{10,11... | collective-permute-start | bytes 2359304 | tf_op jit(solution)/shard_map/ppermute | solution.py:974
  6.4 5.7 copy-start.10
  7.8 13.0 %copy-start.8 = (bf16[256,4096]{1,0:T(8,128)(2,1)S(1)}, bf16[256,4096]{1,0:T(8,128)(2,1)}, u32[]{:S(2)}) copy-start(bf16[256,4096]{1,0:T(8,128)(2,1)} %refs_6_.1) | copy-start | bytes 6291460
  10.6 8.1 %collective-permute-start.11 = (bf16[128,1024]{1,0:T(8,128)(2,1)}, bf16[128,1024]{1,0:T(8,128)(2,1)S(1)}, u32[]{:S(2)}, u32[]{:S(2)}) collective-permute-start(bf16[128,1024]{1,0:T(8,128)(2,1)} %collective-permute-done.9.refs_2_), channel_id=1, source_target_pairs={{0,4},{4,0},{1,5},{5,1},{2,6},{6,2},{3,7},{7,3},{8,12},{12,8},{9,1... | collective-permute-start | bytes 786440 | tf_op jit(solution)/shard_map/ppermute | solution.py:974
  12.1 7.1 %collective-permute-start.10 = (bf16[128,1024]{1,0:T(8,128)(2,1)}, bf16[128,1024]{1,0:T(8,128)(2,1)S(1)}, u32[]{:S(2)}, u32[]{:S(2)}) collective-permute-start(bf16[128,1024]{1,0:T(8,128)(2,1)} %collective-permute-done.9.refs_2_), channel_id=1, source_target_pairs={{0,8},{8,0},{16,24},{24,16},{1,9},{9,1},{17,25},{25,17},{2,10},{10... | collective-permute-start | bytes 786440 | tf_op jit(solution)/shard_map/ppermute | solution.py:974
  12.2 8.7 %copy-start.13 = (s32[1,2]{1,0:T(1,128)S(1)}, s32[1,2]{1,0:T(1,128)}, u32[]{:S(2)}) copy-start(s32[1,2]{1,0:T(1,128)} %param.18) | copy-start | bytes 28
  12.2 82.2 %copy-start.5 = (bf16[256,1536]{1,0:T(8,128)(2,1)}, bf16[256,1536]{1,0:T(8,128)(2,1)S(1)}, u32[]{:S(2)}) copy-start(bf16[256,1536]{1,0:T(8,128)(2,1)S(1)} %pad_maximum_fusion.refs_0_) | copy-start | bytes 2359300
  12.3 71.2 %copy-start.14 = (s32[1,2]{1,0:T(1,128)S(1)}, s32[1,2]{1,0:T(1,128)}, u32[]{:S(2)}) copy-start(s32[1,2]{1,0:T(1,128)} %param.17) | copy-start | bytes 28
  18.7 63.2 %copy-start.20 = (bf16[128,1024]{1,0:T(8,128)(2,1)}, bf16[128,1024]{1,0:T(8,128)(2,1)S(1)}, u32[]{:S(2)}) copy-start(bf16[128,1024]{1,0:T(8,128)(2,1)S(1)} %collective-permute-done.11.refs_4_) | copy-start | bytes 786436
  18.7 20.6 %collective-permute-start.3 = (bf16[256,1536]{1,0:T(8,128)(2,1)S(1)}, bf16[256,1536]{1,0:T(8,128)(2,1)}, u32[]{:S(2)}, u32[]{:S(2)}) collective-permute-start(bf16[256,1536]{1,0:T(8,128)(2,1)S(1)} %pad_maximum_fusion.refs_0_), channel_id=1, source_target_pairs={{0,16},{8,24},{16,0},{24,8},{1,17},{9,25},{17,1},{25,9},{2,18},{10... | collective-permute-start | bytes 2359304 | tf_op jit(solution)/shard_map/ppermute | solution.py:974
  19.2 1.5 copy-start.21
  19.2 42.5 %collective-permute-start.19 = (bf16[512,1024]{1,0:T(8,128)(2,1)S(1)}, bf16[512,1024]{1,0:T(8,128)(2,1)}, u32[]{:S(2)}, u32[]{:S(2)}) collective-permute-start(bf16[512,1024]{1,0:T(8,128)(2,1)S(1)} %constant_dynamic-slice_fusion), channel_id=1, source_target_pairs={{0,16},{8,24},{16,0},{24,8},{1,17},{9,25},{17,1},{25,9},{2,18},{10... | collective-permute-start | bytes 3145736 | tf_op jit(solution)/shard_map/ppermute | solution.py:974
  20.7 73.8 %copy-start.9 = (bf16[256,1024]{1,0:T(8,128)(2,1)}, bf16[256,1024]{1,0:T(8,128)(2,1)S(1)}, u32[]{:S(2)}) copy-start(bf16[256,1024]{1,0:T(8,128)(2,1)S(1)} %collective-permute-done.head) | copy-start | bytes 1572868
  20.7 2.1 collective-permute-start.12
  21.5 60.4 %collective-permute-start.14 = (bf16[128,4096]{1,0:T(8,128)(2,1)S(1)}, bf16[128,4096]{1,0:T(8,128)(2,1)}, u32[]{:S(2)}, u32[]{:S(2)}) collective-permute-start(bf16[128,4096]{1,0:T(8,128)(2,1)S(1)} %constant_dynamic-slice_fusion.1), channel_id=1, source_target_pairs={{0,16},{8,24},{16,0},{24,8},{1,17},{9,25},{17,1},{25,9},{2,18},{10... | collective-permute-start | bytes 3145736 | tf_op jit(solution)/shard_map/ppermute | solution.py:974
  22.8 59.1 %copy-start.22 = (bf16[128,1024]{1,0:T(8,128)(2,1)}, bf16[128,1024]{1,0:T(8,128)(2,1)S(1)}, u32[]{:S(2)}) copy-start(bf16[128,1024]{1,0:T(8,128)(2,1)S(1)} %collective-permute-done.12.refs_5_) | copy-start | bytes 786436
  22.8 43.9 %collective-permute-start.2 = (bf16[256,1536]{1,0:T(8,128)(2,1)S(1)}, bf16[256,1536]{1,0:T(8,128)(2,1)S(1)}, u32[]{:S(2)}, u32[]{:S(2)}) collective-permute-start(bf16[256,1536]{1,0:T(8,128)(2,1)S(1)} %pad_maximum_fusion.refs_0_), channel_id=1, source_target_pairs={{0,8},{8,0},{16,24},{24,16},{1,9},{9,1},{17,25},{25,17},{2,10},{10... | collective-permute-start | bytes 2359304 | tf_op jit(solution)/shard_map/ppermute | solution.py:974
  35.4 27.8 %collective-permute-start.5 = (bf16[256,1024]{1,0:T(8,128)(2,1)S(1)}, bf16[256,1024]{1,0:T(8,128)(2,1)S(1)}, u32[]{:S(2)}, u32[]{:S(2)}) collective-permute-start(bf16[256,1024]{1,0:T(8,128)(2,1)S(1)} %bitcast_select_fusion), channel_id=1, source_target_pairs={{1,2},{5,6},{9,10},{13,14},{17,18},{21,22},{25,26},{29,30}} | collective-permute-start | bytes 1572872 | tf_op jit(solution)/shard_map/ppermute | solution.py:1051
  39.3 53.8 %collective-permute-start.4 = (bf16[256,1536]{1,0:T(8,128)(2,1)}, bf16[256,1536]{1,0:T(8,128)(2,1)S(1)}, u32[]{:S(2)}, u32[]{:S(2)}) collective-permute-start(bf16[256,1536]{1,0:T(8,128)(2,1)} %collective-permute-done.3.refs_2_), channel_id=1, source_target_pairs={{0,8},{8,0},{16,24},{24,16},{1,9},{9,1},{17,25},{25,17},{2,10},{10... | collective-permute-start | bytes 2359304 | tf_op jit(solution)/shard_map/ppermute | solution.py:974
  61.7 32.8 %collective-permute-start.21 = (bf16[512,1024]{1,0:T(8,128)(2,1)}, bf16[512,1024]{1,0:T(8,128)(2,1)}, u32[]{:S(2)}, u32[]{:S(2)}) collective-permute-start(bf16[512,1024]{1,0:T(8,128)(2,1)} %collective-permute-done.19.refs_14_), channel_id=1, source_target_pairs={{0,4},{4,0},{1,5},{5,1},{2,6},{6,2},{3,7},{7,3},{8,12},{12,8},{9,1... | collective-permute-start | bytes 3145736 | tf_op jit(solution)/shard_map/ppermute | solution.py:974
  63.2 29.9 %collective-permute-start.6 = (bf16[256,1024]{1,0:T(8,128)(2,1)S(1)}, bf16[256,1024]{1,0:T(8,128)(2,1)S(1)}, u32[]{:S(2)}, u32[]{:S(2)}) collective-permute-start(bf16[256,1024]{1,0:T(8,128)(2,1)S(1)} %collective-permute-done.5), channel_id=1, source_target_pairs={{2,3},{6,7},{10,11},{14,15},{18,19},{22,23},{26,27},{30,31}} | collective-permute-start | bytes 1572872 | tf_op jit(solution)/shard_map/ppermute | solution.py:1052
  66.7 15.2 %copy-start.17 = (bf16[256,1536]{1,0:T(8,128)(2,1)}, bf16[256,1536]{1,0:T(8,128)(2,1)S(1)}, u32[]{:S(2)}) copy-start(bf16[256,1536]{1,0:T(8,128)(2,1)S(1)} %collective-permute-done.2.refs_1_) | copy-start | bytes 2359300
  66.7 44.2 %collective-permute-start.20 = (bf16[512,1024]{1,0:T(8,128)(2,1)}, bf16[512,1024]{1,0:T(8,128)(2,1)}, u32[]{:S(2)}, u32[]{:S(2)}) collective-permute-start(bf16[512,1024]{1,0:T(8,128)(2,1)} %collective-permute-done.19.refs_14_), channel_id=1, source_target_pairs={{0,8},{8,0},{16,24},{24,16},{1,9},{9,1},{17,25},{25,17},{2,10},{10... | collective-permute-start | bytes 3145736 | tf_op jit(solution)/shard_map/ppermute | solution.py:974
  81.9 29.3 %collective-permute-start.16 = (bf16[128,4096]{1,0:T(8,128)(2,1)}, bf16[128,4096]{1,0:T(8,128)(2,1)}, u32[]{:S(2)}, u32[]{:S(2)}) collective-permute-start(bf16[128,4096]{1,0:T(8,128)(2,1)} %collective-permute-done.14.refs_8_), channel_id=1, source_target_pairs={{0,4},{4,0},{1,5},{5,1},{2,6},{6,2},{3,7},{7,3},{8,12},{12,8},{9,1... | collective-permute-start | bytes 3145736 | tf_op jit(solution)/shard_map/ppermute | solution.py:974
  93.1 46.1 %collective-permute-start.13 = (bf16[256,4096]{1,0:T(8,128)(2,1)}, bf16[256,4096]{1,0:T(8,128)(2,1)}, u32[]{:S(2)}, u32[]{:S(2)}) collective-permute-start(bf16[256,4096]{1,0:T(8,128)(2,1)} %refs_6_.1), channel_id=1, source_target_pairs={{0,8},{8,0},{16,24},{24,16},{1,9},{9,1},{17,25},{25,17},{2,10},{10... | collective-permute-start | bytes 6291464 | tf_op jit(solution)/shard_map/ppermute | solution.py:974
  93.1 1.7 copy-start.18
  93.1 46.1 %collective-permute-start.18 = (bf16[1024,1024]{1,0:T(8,128)(2,1)}, bf16[1024,1024]{1,0:T(8,128)(2,1)}, u32[]{:S(2)}, u32[]{:S(2)}) collective-permute-start(bf16[1024,1024]{1,0:T(8,128)(2,1)} %refs_12_.1), channel_id=1, source_target_pairs={{0,8},{8,0},{16,24},{24,16},{1,9},{9,1},{17,25},{25,17},{2,10},{10... | collective-permute-start | bytes 6291464 | tf_op jit(solution)/shard_map/ppermute | solution.py:974
  94.5 42.4 %collective-permute-start.15 = (bf16[128,4096]{1,0:T(8,128)(2,1)}, bf16[128,4096]{1,0:T(8,128)(2,1)S(1)}, u32[]{:S(2)}, u32[]{:S(2)}) collective-permute-start(bf16[128,4096]{1,0:T(8,128)(2,1)} %collective-permute-done.14.refs_8_), channel_id=1, source_target_pairs={{0,8},{8,0},{16,24},{24,16},{1,9},{9,1},{17,25},{25,17},{2,10},{10... | collective-permute-start | bytes 3145736 | tf_op jit(solution)/shard_map/ppermute | solution.py:974
  110.9 43.0 %collective-permute-start.22 = (bf16[512,1024]{1,0:T(8,128)(2,1)}, bf16[512,1024]{1,0:T(8,128)(2,1)S(1)}, u32[]{:S(2)}, u32[]{:S(2)}) collective-permute-start(bf16[512,1024]{1,0:T(8,128)(2,1)} %collective-permute-done.21.refs_16_), channel_id=1, source_target_pairs={{0,8},{8,0},{16,24},{24,16},{1,9},{9,1},{17,25},{25,17},{2,10},{10... | collective-permute-start | bytes 3145736 | tf_op jit(solution)/shard_map/ppermute | solution.py:974
  111.2 42.7 %collective-permute-start.17 = (bf16[128,4096]{1,0:T(8,128)(2,1)}, bf16[128,4096]{1,0:T(8,128)(2,1)}, u32[]{:S(2)}, u32[]{:S(2)}) collective-permute-start(bf16[128,4096]{1,0:T(8,128)(2,1)} %collective-permute-done.16.refs_10_), channel_id=1, source_target_pairs={{0,8},{8,0},{16,24},{24,16},{1,9},{9,1},{17,25},{25,17},{2,10},{10... | collective-permute-start | bytes 3145736 | tf_op jit(solution)/shard_map/ppermute | solution.py:974
  136.9 17.1 %copy-start.15 = (bf16[128,4096]{1,0:T(8,128)(2,1)}, bf16[128,4096]{1,0:T(8,128)(2,1)S(1)}, u32[]{:S(2)}) copy-start(bf16[128,4096]{1,0:T(8,128)(2,1)S(1)} %collective-permute-done.15.refs_9_) | copy-start | bytes 3145732
  136.9 17.0 %collective-permute-start.7 = (bf16[640,512]{1,0:T(8,128)(2,1)S(1)}, bf16[640,512]{1,0:T(8,128)(2,1)S(1)}, u32[]{:S(2)}, u32[]{:S(2)}) collective-permute-start(bf16[640,512]{1,0:T(8,128)(2,1)S(1)} %constant_dynamic-slice_fusion.3), channel_id=1, source_target_pairs={{0,1},{1,0},{2,3},{3,2},{4,5},{5,4},{6,7},{7,6},{8,9},{9,8},{10,11... | collective-permute-start | bytes 1966088 | tf_op jit(solution)/shard_map/ppermute | solution.py:974
  153.9 0.9 copy-start.7
  153.9 1.2 copy-start.16
  236.4 16.9 %copy-start.12 = (f32[2,1024]{1,0:T(2,128)S(1)}, f32[2,1024]{1,0:T(2,128)}, u32[]{:S(2)}) copy-start(f32[2,1024]{1,0:T(2,128)} %get-tuple-element.99) | copy-start | bytes 24580
  251.6 16.4 %collective-permute-start.23 = (bf16[640,512]{1,0:T(8,128)(2,1)}, bf16[640,512]{1,0:T(8,128)(2,1)S(1)}, u32[]{:S(2)}, u32[]{:S(2)}) collective-permute-start(bf16[640,512]{1,0:T(8,128)(2,1)} %get-tuple-element.75), channel_id=1, source_target_pairs={{0,1},{1,0},{2,3},{3,2},{4,5},{5,4},{6,7},{7,6},{8,9},{9,8},{10,11... | collective-permute-start | bytes 1966088 | tf_op jit(solution)/shard_map/ppermute | solution.py:974
  268.1 0.8 copy-start.19
  333.3 249.2 %collective-permute-start.26 = (bf16[256,1024]{1,0:T(8,128)(2,1)}, bf16[256,1024]{1,0:T(8,128)(2,1)}, u32[]{:S(2)}, u32[]{:S(2)}) collective-permute-start(bf16[256,1024]{1,0:T(8,128)(2,1)} %get-tuple-element.85), channel_id=1, source_target_pairs={{2,1},{3,0},{6,5},{7,4},{10,9},{11,8},{14,13},{15,12},{18,17},{19,... | collective-permute-start | bytes 1572872 | tf_op jit(solution)/shard_map/ppermute | solution.py:1101
  336.5 246.1 %collective-permute-start.25 = (bf16[256,1024]{1,0:T(8,128)(2,1)}, bf16[256,1024]{1,0:T(8,128)(2,1)}, u32[]{:S(2)}, u32[]{:S(2)}) collective-permute-start(bf16[256,1024]{1,0:T(8,128)(2,1)} %get-tuple-element.85), channel_id=1, source_target_pairs={{2,0},{3,1},{6,4},{7,5},{10,8},{11,9},{14,12},{15,13},{18,16},{19,... | collective-permute-start | bytes 1572872 | tf_op jit(solution)/shard_map/ppermute | solution.py:1100
  513.4 5.1 copy-start
  518.5 1.8 copy-start.6
  518.5 2.7 copy-start.11
  521.2 10.0 %collective-permute-start.28 = (f32[8,1024]{1,0:T(8,128)S(1)}, f32[8,1024]{1,0:T(8,128)S(1)}, u32[]{:S(2)}, u32[]{:S(2)}) collective-permute-start(f32[8,1024]{1,0:T(8,128)S(1)} %stack.111), channel_id=1, source_target_pairs={{0,8},{8,0},{16,24},{24,16},{1,9},{9,1},{17,25},{25,17},{2,10},{10... | collective-permute-start | bytes 98312 | tf_op jit(solution)/shard_map/ppermute | solution.py:974
  522.4 57.6 %collective-permute-start.27 = (bf16[256,1536]{1,0:T(8,128)(2,1)S(1)}, bf16[256,1536]{1,0:T(8,128)(2,1)S(1)}, u32[]{:S(2)}, u32[]{:S(2)}) collective-permute-start(bf16[256,1536]{1,0:T(8,128)(2,1)S(1)} %pad_maximum_fusion.1), channel_id=1, source_target_pairs={{0,1},{1,0},{2,3},{3,2},{4,5},{5,4},{6,7},{7,6},{8,9},{9,8},{10,11... | collective-permute-start | bytes 2359304 | tf_op jit(solution)/shard_map/ppermute | solution.py:974
  522.5 60.0 %collective-permute-start.24 = (bf16[640,1024]{1,0:T(8,128)(2,1)}, bf16[640,1024]{1,0:T(8,128)(2,1)}, u32[]{:S(2)}, u32[]{:S(2)}) collective-permute-start(bf16[640,1024]{1,0:T(8,128)(2,1)} %get-tuple-element.84), channel_id=1, source_target_pairs={{0,1},{1,0},{2,3},{3,2},{4,5},{5,4},{6,7},{7,6},{8,9},{9,8},{10,11... | collective-permute-start | bytes 3932168 | tf_op jit(solution)/shard_map/ppermute | solution.py:974
  526.3 48.0 %copy-start.2 = (bf16[2,256,1024]{2,1,0:T(8,128)(2,1)S(1)}, bf16[2,256,1024]{2,1,0:T(8,128)(2,1)}, u32[]{:S(2)}) copy-start(bf16[2,256,1024]{2,1,0:T(8,128)(2,1)} %get-tuple-element.101) | copy-start | bytes 3145732
  531.2 4.0 collective-permute-start.29
  535.2 3.9 collective-permute-start.30
  539.1 32.1 %collective-permute-start.31 = (f32[8,1024]{1,0:T(8,128)S(1)}, f32[8,1024]{1,0:T(8,128)S(1)}, u32[]{:S(2)}, u32[]{:S(2)}) collective-permute-start(f32[8,1024]{1,0:T(8,128)S(1)} %add.107), channel_id=1, source_target_pairs={{0,1},{1,0},{2,3},{3,2},{4,5},{5,4},{6,7},{7,6},{8,9},{9,8},{10,11... | collective-permute-start | bytes 98312 | tf_op jit(solution)/shard_map/ppermute | solution.py:974
  571.2 8.1 %collective-permute-start.32 = (f32[8,1024]{1,0:T(8,128)S(1)}, f32[8,1024]{1,0:T(8,128)S(1)}, u32[]{:S(2)}, u32[]{:S(2)}) collective-permute-start(f32[8,1024]{1,0:T(8,128)S(1)} %add.108), channel_id=1, source_target_pairs={{0,2},{1,3},{2,0},{3,1},{4,6},{5,7},{6,4},{7,5},{8,10},{9,11},{10,... | collective-permute-start | bytes 98312 | tf_op jit(solution)/shard_map/ppermute | solution.py:974
  576.8 3.2 copy-start.3
  576.8 3.2 copy-start.4

commit v3 on v2

--- a/solution.py
+++ b/solution.py
@@ -76,98 +76,8 @@
     return jax.ShapeDtypeStruct(dims, dtype)
 
 
-def project_body(info, pos, own, head, rest, gain, bias, *refs, pieces):
-    parts = refs[:pieces]
-    q, k, v, n_t, w, sems = refs[pieces:]
-    step = pl.program_id(0)
-    half = q.shape[1]
-
-    def copies():
-        return [
-            pltpu.make_async_copy(
-                parts[i], w.at[pl.ds(pl.multiple_of(pos[i], 16), parts[i].shape[0])], sems.at[i]
-            )
-            for i in range(pieces)
-        ]
-
-    @pl.when(step == 0)
-    def _():
-        for c in copies():
-            c.start()
-
-    def rows(x):
-        hat, _ = normalise(x.astype(F32))
-        return (hat * gain[...] + bias[...]).astype(BF16)
-
-    def emit(normed):
-        n_t[...] = normed.T
-        out = nn(normed, w[...])
-        q[...] = out[:, :half].astype(BF16)
-        k[...] = out[:, half : 2 * half].astype(BF16)
-        v[...] = out[:, 2 * half :].astype(BF16)
-
-    @pl.when(step == 0)
-    def _():
-        normed = rows(own[...])
-        for c in copies():
-            c.wait()
-        emit(normed)
-
-    @pl.when(step == 1)
-    def _():
-        emit(rows(jnp.concatenate([head[...], rest[...]], axis=0)))
-
-
-def project(info, pos, own, head, rest, gain, bias, parts):
-    local, d = own.shape
-    wide = parts[0].shape[1]
-    half = wide // 3
-    block = lambda i, info, pos: ((info[1] + i) % 2, 0)
-    return call(
-        functools.partial(project_body, pieces=len(parts)),
-        (2,),
-        2,
-        [full(own.shape), full(head.shape), full(rest.shape), full((1, d)), full((1, d))]
-        + [hbm()] * len(parts),
-        [pl.BlockSpec((local, half), block)] * 3
-        + [
-            pl.BlockSpec((d, local), lambda i, info, pos: (0, (info[1] + i) % 2)),
-            full((d, wide)),
-        ],
-        [shape((2 * local, half), BF16)] * 3 + [shape((d, 2 * local), BF16), shape((d, wide), BF16)],
-        [pltpu.SemaphoreType.DMA((len(parts),))],
-        flops=4 * local * d * wide,
-        moved=16e6,
-    )(info, pos, own, head, rest, gain, bias, *parts)
-
-
-def pad_body(x, gain, bias, w, k, v, n_t):
-    hat, _ = normalise(x[...].astype(F32))
-    normed = (hat * gain[...] + bias[...]).astype(BF16)
-    n_t[...] = normed.T
-    half = k.shape[1]
-    out = nn(normed, w[:, half:])
-    k[...] = out[:, :half].astype(BF16)
-    v[...] = out[:, half:].astype(BF16)
-
-
-def pad_project(x, gain, bias, w):
-    rows, d = x.shape
-    half = w.shape[1] // 3
-    return call(
-        pad_body,
-        (1,),
-        0,
-        [full(x.shape), full((1, d)), full((1, d)), full(w.shape)],
-        [full((rows, half)), full((rows, half)), full((d, rows))],
-        [shape((rows, half), BF16)] * 2 + [shape((d, rows), BF16)],
-        flops=4 * rows * d * half,
-        moved=5e6,
-    )(x, gain, bias, w)
-
-
-def attend_body(info, q, k, v, kp, vp, o, lse):
-    start, stop, pad_a, pad_b = info[2], info[3], info[4], info[5]
+def attend_pair(bounds, q, k, v, kp, vp, o, lse):
+    start, stop, pad_a, pad_b = bounds
     lane = lax.broadcasted_iota(jnp.int32, (1, 2 * HD), 1)
     row = lax.broadcasted_iota(jnp.int32, (BLK, 1), 0)
     col = lax.broadcasted_iota(jnp.int32, (1, BLK), 1)
@@ -176,7 +86,7 @@
     count = SLOT // BLK
     for i in range(count):
         n = (i + 1) * BLK
-        qi = q[i * BLK : n, :]
+        qi = q(slice(i * BLK, n))
         edge = i in (0, count - 1)
         pos_q = row + i * BLK
         in_q = (pos_q >= start) & (pos_q < stop)
@@ -197,42 +107,25 @@
             qh = jnp.where(lane // HD == h, qi, jnp.zeros_like(qi))
             blocks = []
             for j in range(i + 1):
-                s = nt(qh, k[j * BLK : (j + 1) * BLK, :]) * SCALE
+                s = nt(qh, k(slice(j * BLK, (j + 1) * BLK))) * SCALE
                 if masks[j] is not None:
                     s = jnp.where(masks[j], s, NEG)
                 blocks.append(s)
             if edge:
-                s = nt(qh, kp[...]) * SCALE
+                s = nt(qh, kp(slice(None))) * SCALE
                 blocks.append(jnp.where(~in_q & pad_col, s, NEG))
             top = functools.reduce(jnp.maximum, blocks)
             top = jnp.max(top, axis=1, keepdims=True)
             probs = [jnp.exp2(s - top) for s in blocks]
             total = jnp.sum(functools.reduce(jnp.add, probs), axis=1, keepdims=True)
             probs = [x.astype(BF16) for x in probs]
-            mixed = nn(jnp.concatenate(probs[: i + 1], axis=1), v[0:n, :])
+            mixed = nn(jnp.concatenate(probs[: i + 1], axis=1), v(slice(0, n)))
             if edge:
-                mixed = mixed + nn(probs[-1], vp[...])
+                mixed = mixed + nn(probs[-1], vp(slice(None)))
             outs.append(mixed * (1.0 / total))
             level = jnp.broadcast_to(top + jnp.log2(total), (BLK, 128))
-            lse[0, h : h + 1, i * BLK : n] = level.T[0:1, :]
-        o[i * BLK : n, :] = jnp.where(lane < HD, outs[0], outs[1]).astype(BF16)
-
-
-def attend(info, q, k, v, kp, vp):
-    rows, half = q.shape
-    pairs = half // (2 * HD)
-    pair = pl.BlockSpec((rows, 2 * HD), lambda i, info: (0, i))
-    pad = pl.BlockSpec((kp.shape[0], 2 * HD), lambda i, info: (0, i))
-    return call(
-        attend_body,
-        (pairs,),
-        1,
-        [pair, pair, pair, pad, pad],
-        [pair, pl.BlockSpec((1, 2, rows), lambda i, info: (i, 0, 0))],
-        [shape((rows, half), BF16), shape((pairs, 2, rows), F32)],
-        flops=pairs * 34 * BLK * BLK * 256 * 4,
-        moved=6e6,
-    )(info, q, k, v, kp, vp)
+            lse(h, slice(i * BLK, n), level.T[0:1, :])
+        o(slice(i * BLK, n), jnp.where(lane < HD, outs[0], outs[1]).astype(BF16))
 
 
 def attend_back_body(
@@ -342,43 +235,382 @@
     )(info, q, k, v, kp, vp, o, lse, d_own, d_other)
 
 
-def forward_body(info, pos, own, other, x, up, gains, biases, *refs, counts):
-    total = sum(counts)
-    parts = refs[:total]
-    (out, g_feed, act_t, slope, n_t, branch, middle, edges, wo_out, wu_out, wd_out) = refs[total : total + 11]
-    wo, wu, wd, normed, feed, sems, out_sems = refs[total + 11 :]
+def peer(axis, mask):
+    return {axis: lax.axis_index(axis) ^ mask}
+
+
+def greet(partners):
+    barrier = pltpu.get_barrier_semaphore()
+    for p in partners:
+        pl.semaphore_signal(barrier, inc=1, device_id=p, device_id_type=pl.DeviceIdType.MESH)
+    pl.semaphore_wait(barrier, len(partners))
+
+
+def remote(src, dst, send, recv, to):
+    return pltpu.make_async_remote_copy(
+        src_ref=src, dst_ref=dst, send_sem=send, recv_sem=recv, device_id=to, device_id_type=pl.DeviceIdType.MESH
+    )
+
+
+def front_body(
+    info, tokens, wqkv, wo, wu, wd, gain, bias,
+    q_out, k_out, v_out, n_out, np_out, kp_out, vp_out, w_out, mix_out, lse_out, other, tok_out, pad_out, wo_all, wu_all, wd_all,
+    mine, theirs, pads, made, w, normed, n_t, np_t, q, k, v, kp, vp, mixed, held_o, held_u, held_d, lse,
+    tok_l, tok_s, tok_r, pad_s, pad_r, q_l, q_cs, q_cr, q_ys, q_yr, q_fs, q_fr,
+    h_l, s_l, s_cs, s_cr, y_s, y_r, x_s, x_r, fy_s, fy_r, fx_s, fx_r, o_s, o_r, out_l,
+    *, fsdp, dp
+):
+    f, x, s = lax.axis_index("fsdp"), lax.axis_index("dp"), lax.axis_index("seq")
+    parity = s % 2
+    local, d = tokens.shape
+    half = d // 2
+    ys = fsdp // 2
+    bounds = tuple(info[i] for i in range(2, 6))
+    core, mate = peer("fsdp", 1), peer("seq", 1)
+    greet(
+        [core]
+        + [peer("fsdp", 2 * r) for r in range(1, ys)]
+        + [peer("dp", r) for r in range(1, dp)]
+        + [mate, peer("seq", 3)]
+    )
+
+    cuts = ((0, BLK), (BLK, local - BLK))
+
+    def token(i):
+        at = pl.ds(*cuts[i])
+        return remote(tokens.at[at], theirs.at[at], tok_s.at[i], tok_r.at[i], mate)
+
+    load = pltpu.make_async_copy(tokens, mine, tok_l.at[0])
+    load.start()
+    token(0).start()
+    token(1).start()
+
+    rows = wqkv.shape[0]
+
+    def band(r):
+        return pl.ds(pl.multiple_of((f ^ r) * rows, 16), rows)
+
+    def source(c):
+        return wqkv.at[:, pl.ds(pl.multiple_of(c * d + parity * half, 128), half)]
+
+    def cols(c):
+        return pl.ds(c * half, half)
+
+    def q_local(c):
+        return pltpu.make_async_copy(source(c), w.at[band(0), cols(c)], q_l.at[c])
+
+    def q_core(c):
+        return remote(source(c), w.at[band(0), cols(c)], q_cs.at[c], q_cr.at[c], core)
+
+    def q_y(c, r):
+        at = (c, r - 1)
+        return remote(source(c), w.at[band(0), cols(c)], q_ys.at[at], q_yr.at[at], peer("fsdp", 2 * r))
+
+    def q_far(c, r):
+        at = (c, r - 1)
+        here = w.at[band(2 * r), cols(c)]
+        return remote(here, here, q_fs.at[at], q_fr.at[at], core)
+
+    for c in range(3):
+        for r in range(1, ys):
+            q_y(c, r).start()
+        q_core(c).start()
+        q_local(c).start()
+
+    shards, wholes = (held_o, held_u, held_d), (wo_all, wu_all, wd_all)
+
+    def hold(i):
+        return pltpu.make_async_copy((wo, wu, wd)[i], shards[i], h_l.at[i])
+
+    def whole_shard(i):
+        n = shards[i].shape[0]
+        return wholes[i].at[pl.ds(pl.multiple_of(f * n, 16), n)]
+
+    def s_local(i):
+        return pltpu.make_async_copy(shards[i], whole_shard(i), s_l.at[i])
+
+    def s_core(i):
+        return remote(shards[i], whole_shard(i), s_cs.at[i], s_cr.at[i], core)
+
+    units = [(0, 0)] + [(1, j) for j in range(4)] + [(2, j) for j in range(4)]
+
+    def piece(u, owner, part, shard=False):
+        which, j = units[u]
+        n = shards[which].shape[0]
+        sub = n // dp
+        base = part * sub if shard else owner * n + part * sub
+        ref = shards[which] if shard else wholes[which]
+        if which == 0:
+            return ref.at[pl.ds(pl.multiple_of(base, 16), sub)]
+        if which == 1:
+            wide = ref.shape[1] // 4
+            return ref.at[pl.ds(pl.multiple_of(base, 16), sub), pl.ds(j * wide, wide)]
+        return ref.at[pl.ds(pl.multiple_of(base + j * (sub // 4), 16), sub // 4)]
+
+    def w_y(u, r):
+        at = (u, r - 1)
+        return remote(piece(u, f, x, True), piece(u, f, x), y_s.at[at], y_r.at[at], peer("fsdp", 2 * r))
+
+    def w_x(u, r, t):
+        at = (u, r - 1, t - 1)
+        here = piece(u, f ^ (2 * r), x)
+        return remote(here, here, x_s.at[at], x_r.at[at], peer("dp", t))
+
+    def w_fy(u, r):
+        at = (u, r - 1)
+        here = piece(u, f ^ (2 * r), x)
+        return remote(here, here, fy_s.at[at], fy_r.at[at], core)
+
+    def w_fx(u, r, t):
+        at = (u, r - 1, t - 1)
+        here = piece(u, f ^ (2 * r), x ^ t)
+        return remote(here, here, fx_s.at[at], fx_r.at[at], core)
+
+    def issue(u):
+        if u < len(units):
+            for r in range(1, ys):
+                w_y(u, r).start()
+
+    def came_y(u):
+        for r in range(1, ys):
+            w_y(u, r).wait_recv()
+        issue(u + 3)
+        for r in range(1, ys):
+            for t in range(1, dp):
+                w_x(u, r, t).start()
+            w_fy(u, r).start()
+
+    def came_x(u):
+        for r in range(1, ys):
+            for t in range(1, dp):
+                w_x(u, r, t).wait_recv()
+                w_fx(u, r, t).start()
+
+    def normalise_rows(src, at, count):
+        def body(i, carry):
+            here = pl.ds(pl.multiple_of(i * 128, 128), 128)
+            there = pl.ds(pl.multiple_of(at + i * 128, 128), 128)
+            hat, _ = normalise(src[here, :].astype(F32))
+            value = (hat * gain[...] + bias[...]).astype(BF16)
+            normed[there, :] = value
+            n_t[:, there] = value.T
+            return carry
+
+        lax.fori_loop(count[0], count[1], body, 0)
+
+    def project(at, c):
+        here = pl.ds(pl.multiple_of(at, 128), local)
+        (q, k, v)[c][here, :] = nn(normed[here, :], w[:, c * half : (c + 1) * half]).astype(BF16)
+
+    for i in range(3):
+        hold(i).start()
+    load.wait()
+    normalise_rows(mine, parity * local, (0, local // 128))
+    for c in range(3):
+        q_local(c).wait()
+        q_core(c).wait_recv()
+        for r in range(1, ys):
+            q_y(c, r).wait_recv()
+            q_far(c, r).start()
+        if c == 0:
+            for i in range(3):
+                hold(i).wait()
+            issue(0)
+            for i in range(3):
+                s_local(i).start()
+                s_core(i).start()
+        elif c == 1:
+            issue(1)
+        else:
+            issue(2)
+        for r in range(1, ys):
+            q_far(c, r).wait_recv()
+        if c == 0:
+            token(0).wait_recv()
+            index = lax.broadcasted_iota(jnp.int32, (BLK, 1), 0)
+            made[...] = jnp.where(
+                index < info[7], theirs[0:BLK, :].astype(F32), mine[local - BLK : local, :].astype(F32)
+            ).astype(BF16)
+
+            @pl.when(s < 2)
+            def _():
+                pads[...] = made[...]
+
+        project(parity * local, c)
+        if c == 0:
+
+            @pl.when(s == 1)
+            def _():
+                remote(made, pads, pad_s.at[0], pad_r.at[0], peer("seq", 3)).start()
+
+    w_store = pltpu.make_async_copy(w, w_out, out_l.at[0])
+    w_store.start()
+    forward_pads = remote(pads, pads, pad_s.at[1], pad_r.at[1], mate)
+
+    @pl.when(s == 2)
+    def _():
+        remote(made, pads, pad_s.at[0], pad_r.at[0], peer("seq", 3)).wait_recv()
+        forward_pads.start()
+
+    away = (1 - parity) * local
+    normalise_rows(theirs, away, (0, BLK // 128))
+    came_y(0)
+    token(1).wait_recv()
+    normalise_rows(theirs, away, (BLK // 128, local // 128))
+    for c in range(3):
+        project(away, c)
+    stores = [
+        pltpu.make_async_copy(a, b, out_l.at[1 + i])
+        for i, (a, b) in enumerate(((q, q_out), (k, k_out), (v, v_out), (n_t, n_out), (theirs, tok_out)))
+    ]
+    for copy in stores:
+        copy.start()
+    came_y(1)
+    came_x(0)
+
+    @pl.when(s == 3)
+    def _():
+        forward_pads.wait_recv()
+
+    hat, _ = normalise(pads[...].astype(F32))
+    value = (hat * gain[...] + bias[...]).astype(BF16)
+    np_t[...] = value.T
+    kp[...] = nn(value, w[:, half : 2 * half]).astype(BF16)
+    vp[...] = nn(value, w[:, 2 * half :]).astype(BF16)
+    late = [
+        pltpu.make_async_copy(a, b, out_l.at[6 + i])
+        for i, (a, b) in enumerate(((np_t, np_out), (kp, kp_out), (vp, vp_out), (pads, pad_out)))
+    ]
+    for copy in late:
+        copy.start()
+    came_y(2)
+    came_x(1)
+
+    def give(i):
+        lanes = pl.ds(pl.multiple_of(i * 2 * HD, 128), 2 * HD)
+        return remote(
+            mixed.at[pl.ds(pl.multiple_of(away, 16), local), lanes], other.at[:, lanes], o_s.at[i], o_r.at[i], mate
+        )
+
+    pairs = half // (2 * HD)
+    done_y, done_x = 3, 2
+    for i in range(pairs):
+        lanes = slice(i * 2 * HD, (i + 1) * 2 * HD)
+
+        def put(at, value):
+            mixed[at, lanes] = value
+
+        def put_lse(h, at, value):
+            lse[i, h : h + 1, at] = value
+
+        attend_pair(
+            bounds,
+            lambda at: q[at, lanes],
+            lambda at: k[at, lanes],
+            lambda at: v[at, lanes],
+            lambda at: kp[at, lanes],
+            lambda at: vp[at, lanes],
+            put,
+            put_lse,
+        )
+        give(i).start()
+        came_y(done_y)
+        came_x(done_x)
+        done_y, done_x = done_y + 1, done_x + 1
+    last = [
+        pltpu.make_async_copy(mixed, mix_out, out_l.at[10]),
+        pltpu.make_async_copy(lse, lse_out, out_l.at[11]),
+    ]
+    for copy in last:
+        copy.start()
+    for u in range(done_y, len(units)):
+        came_y(u)
+        came_x(u - 1)
+    came_x(len(units) - 1)
+
+    for i in range(pairs):
+        give(i).wait()
+    for i in range(3):
+        s_local(i).wait()
+        s_core(i).wait()
+    for u in range(len(units)):
+        for r in range(1, ys):
+            w_y(u, r).wait_send()
+            w_fy(u, r).wait()
+            for t in range(1, dp):
+                w_x(u, r, t).wait_send()
+                w_fx(u, r, t).wait()
+    for c in range(3):
+        q_core(c).wait_send()
+        for r in range(1, ys):
+            q_y(c, r).wait_send()
+            q_far(c, r).wait_send()
+    token(0).wait_send()
+    token(1).wait_send()
+
+    @pl.when(s == 1)
+    def _():
+        remote(made, pads, pad_s.at[0], pad_r.at[0], peer("seq", 3)).wait_send()
+
+    @pl.when(s == 2)
+    def _():
+        forward_pads.wait_send()
+
+    for copy in [w_store] + stores + late + last:
+        copy.wait()
+
+
+def front(info, tokens, wqkv, wo, wu, wd, gain, bias, fsdp, dp):
+    local, d = tokens.shape
+    half, ff = d // 2, wu.shape[1]
+    pairs = half // (2 * HD)
+    y, px, n = max(fsdp // 2 - 1, 1), max(dp - 1, 1), 9
+    dma = pltpu.SemaphoreType.DMA
+    outs = [((2 * local, half), BF16)] * 3 + [
+        ((d, 2 * local), BF16),
+        ((d, BLK), BF16),
+        ((BLK, half), BF16),
+        ((BLK, half), BF16),
+        ((d, 3 * half), BF16),
+        ((2 * local, half), BF16),
+        ((pairs, 2, 2 * local), F32),
+        ((local, half), BF16),
+        ((local, d), BF16),
+        ((BLK, d), BF16),
+        ((d, d), BF16),
+        ((d, ff), BF16),
+        ((ff, d), BF16),
+    ]
+    buffers = [
+        (local, d), (local, d), (BLK, d), (BLK, d), (d, 3 * half), (2 * local, d), (d, 2 * local), (d, BLK),
+        (2 * local, half), (2 * local, half), (2 * local, half), (BLK, half), (BLK, half), (2 * local, half),
+        wo.shape, wu.shape, wd.shape,
+    ]
+    sems = [(1,), (2,), (2,), (2,), (2,), (3,), (3,), (3,), (3, y), (3, y), (3, y), (3, y)]
+    sems += [(3,)] * 4 + [(n, y)] * 2 + [(n, y, px)] * 2 + [(n, y)] * 2 + [(n, y, px)] * 2 + [(pairs,)] * 2 + [(12,)]
+    return pl.pallas_call(
+        functools.partial(front_body, fsdp=fsdp, dp=dp),
+        in_specs=[pl.BlockSpec(memory_space=pltpu.SMEM)] + [hbm()] * 5 + [pl.BlockSpec(memory_space=pltpu.VMEM)] * 2,
+        out_specs=[hbm()] * len(outs),
+        out_shape=[shape(*o) for o in outs],
+        scratch_shapes=[pltpu.VMEM(b, BF16) for b in buffers]
+        + [pltpu.VMEM((pairs, 2, 2 * local), F32)]
+        + [dma(s) for s in sems],
+        compiler_params=pltpu.CompilerParams(vmem_limit_bytes=VMEM_LIMIT, collective_id=1, has_side_effects=True),
+        cost_estimate=pl.CostEstimate(flops=10**10, bytes_accessed=10**8, transcendentals=0),
+    )(info, tokens, wqkv, wo, wu, wd, gain, bias)
+
+
+def forward_body(
+    info, own, other, x, up, gains, biases, wo, wu, wd, out, g_feed, act_t, slope, n_t, branch, middle, edges, normed, feed
+):
     parity = info[1]
     step, last = pl.program_id(0), pl.num_programs(0) - 1
-    local = x.shape[0]
     half = own.shape[1]
-    tile = slope.shape[1]
-    blocks = local // 128
-
-    def copies(which):
-        first = sum(counts[:which])
-        target = (wo, wu, wd)[which]
-        return [
-            pltpu.make_async_copy(
-                parts[i],
-                target.at[pl.ds(pl.multiple_of(pos[i], 16), parts[i].shape[0])],
-                sems.at[i],
-            )
-            for i in range(first, first + counts[which])
-        ]
-
-    def store(which):
-        return pltpu.make_async_copy(
-            (wo, wu, wd)[which], (wo_out, wu_out, wd_out)[which], out_sems.at[which]
-        )
+    blocks = x.shape[0] // 128
 
     @pl.when(step == 0)
     def _():
-        for which in range(3):
-            for c in copies(which):
-                c.start()
-        for c in copies(0):
-            c.wait()
-        store(0).start()
         w_own = wo[pl.ds(pl.multiple_of(parity * half, 128), half), :]
         w_other = wo[pl.ds(pl.multiple_of((1 - parity) * half, 128), half), :]
         branch[...] = nn(own[...], w_own) + nn(other[...], w_other)
@@ -396,20 +628,15 @@
 
         lax.fori_loop(0, blocks, rows, 0)
         feed[...] = jnp.zeros_like(feed)
-        for which in (1, 2):
-            for c in copies(which):
-                c.wait()
-            store(which).start()
-
-    cols = pl.ds(pl.multiple_of(step * tile, 128), tile)
-    u = nn(normed[...], wu[:, cols])
+
+    u = nn(normed[...], wu[...])
     th = jnp.tanh(0.7978845608 * (u + 0.044715 * (u * u * u)))
     act = (0.5 * u * (1.0 + th)).astype(BF16)
     slope[...] = (
         0.5 * (1.0 + th) + 0.5 * u * (1.0 - th * th) * (0.7978845608 + (3 * 0.044715 * 0.7978845608) * (u * u))
     ).astype(BF16)
     act_t[...] = act.T
-    feed[...] += nn(act, wd[cols, :])
+    feed[...] += nn(act, wd[...])
 
     @pl.when(step == last)
     def _():
@@ -429,40 +656,37 @@
         a, b = lax.fori_loop(0, blocks, rows, (zero, zero))
         edges[0:1, :] = a
         edges[1:2, :] = b
-        for which in range(3):
-            store(which).wait()
-
-
-def forward(info, pos, own, other, x, up, gains, biases, parts, counts, ff):
-    attn, half, parity = own
+
+
+def forward(info, mixed, other, x, up, gains, biases, wo, wu, wd):
     local, d = x.shape
+    half, ff = mixed.shape[1], wu.shape[1]
     tile = 512
     once = lambda s: pl.BlockSpec(s, lambda *_: (0,) * len(s), pipeline_mode=pl.Buffered(1))
     return call(
-        functools.partial(forward_body, counts=counts),
+        forward_body,
         (ff // tile,),
-        2,
+        1,
         [
-            pl.BlockSpec((local, half), lambda i, info, pos: (info[1], 0), pipeline_mode=pl.Buffered(1)),
+            pl.BlockSpec((local, half), lambda i, info: (info[1], 0), pipeline_mode=pl.Buffered(1)),
             once(other.shape),
             once(x.shape),
             once(up.shape),
             once(gains.shape),
             once(biases.shape),
-        ]
-        + [hbm()] * len(parts),
+            once(wo.shape),
+            pl.BlockSpec((d, tile), lambda i, info: (0, i)),
+            pl.BlockSpec((tile, d), lambda i, info: (i, 0)),
+        ],
         [
             full((local, d)),
             full((local, d)),
-            pl.BlockSpec((tile, local), lambda i, info, pos: (i, 0)),
-            pl.BlockSpec((local, tile), lambda i, info, pos: (0, i)),
+            pl.BlockSpec((tile, local), lambda i, info: (i, 0)),
+            pl.BlockSpec((local, tile), lambda i, info: (0, i)),
             full((d, local)),
             full((local, d)),
             full((local, d)),
             full((2, d)),
-            hbm(),
-            hbm(),
-            hbm(),
         ],
         [
             shape((local, d), BF16),
@@ -473,22 +697,11 @@
             shape((local, d), F32),
             shape((local, d), F32),
             shape((2, d), F32),
-            shape((d, d), BF16),
-            shape((d, ff), BF16),
-            shape((ff, d), BF16),
         ],
-        [
-            pltpu.VMEM((d, d), BF16),
-            pltpu.VMEM((d, ff), BF16),
-            pltpu.VMEM((ff, d), BF16),
-            pltpu.VMEM((local, d), BF16),
-            pltpu.VMEM((local, d), F32),
-            pltpu.SemaphoreType.DMA((len(parts),)),
-            pltpu.SemaphoreType.DMA((3,)),
-        ],
+        [pltpu.VMEM((local, d), BF16), pltpu.VMEM((local, d), F32)],
         flops=2 * local * d * (d + 2 * ff),
-        moved=60e6,
-    )(info, pos, attn, other, x, up, gains, biases, *parts)
+        moved=40e6,
+    )(info, mixed, other, x, up, gains, biases, wo, wu, wd)
 
 
 def back_body(info, g_feed, n_t, act_t, slope, wd, wu, keep, send, g_two, *, fsdp):
@@ -612,7 +825,7 @@
 
 
 def project_back_body(
-    info, own, head, rest, padx, gains, dq, dk, dv, dkp, dvp, w, n_t, np_t, g_own, g_send, g_pad, keep, send, edges, *, fsdp
+    info, own, theirs, padx, gains, dq, dk, dv, dkp, dvp, w, n_t, np_t, g_own, g_send, g_pad, keep, send, edges, *, fsdp
 ):
     f, parity = info[0], info[1]
     step = pl.program_id(0)
@@ -636,7 +849,7 @@
         edges[1:2, :] = jnp.sum(g, axis=0, keepdims=True)
         g = through(pl.ds(pl.multiple_of((1 - parity) * local, 128), local))
         g_send[...] = g.astype(BF16)
-        hat, _ = normalise(jnp.concatenate([head[...], rest[...]], axis=0).astype(F32))
+        hat, _ = normalise(theirs[...].astype(F32))
         edges[0:1, :] += jnp.sum(g * hat, axis=0, keepdims=True)
         edges[1:2, :] += jnp.sum(g, axis=0, keepdims=True)
 
@@ -657,12 +870,12 @@
             target[r // 2, :, 2 * half :] = (nn(left, dv[...]) + nn(pads, dvp[...])).astype(BF16)
 
 
-def project_back(info, own, head, rest, padx, gains, dq, dk, dv, dkp, dvp, w, n_t, np_t, fsdp):
+def project_back(info, own, theirs, padx, gains, dq, dk, dv, dkp, dvp, w, n_t, np_t, fsdp):
     local, d = own.shape
     wide = w.shape[1]
     pads = padx.shape[0]
     grads = shape((fsdp // 2, d // fsdp, wide), BF16)
-    arrays = (own, head, rest, padx, gains, dq, dk, dv, dkp, dvp, w, n_t, np_t)
+    arrays = (own, theirs, padx, gains, dq, dk, dv, dkp, dvp, w, n_t, np_t)
     return call(
         functools.partial(project_back_body, fsdp=fsdp),
         (2,),
@@ -706,23 +919,6 @@
         flops=1e7,
         moved=12e6,
     )(info, *arrays)
-
-
-def peer(axis, mask):
-    return {axis: lax.axis_index(axis) ^ mask}
-
-
-def greet(partners):
-    barrier = pltpu.get_barrier_semaphore()
-    for p in partners:
-        pl.semaphore_signal(barrier, inc=1, device_id=p, device_id_type=pl.DeviceIdType.MESH)
-    pl.semaphore_wait(barrier, len(partners))
-
-
-def remote(src, dst, send, recv, to):
-    return pltpu.make_async_remote_copy(
-        src_ref=src, dst_ref=dst, send_sem=send, recv_sem=recv, device_id=to, device_id_type=pl.DeviceIdType.MESH
-    )
 
 
 class Lane:
@@ -984,38 +1180,6 @@
     return [jnp.where(bit, b, a) for a, b in zip(low, high)] + [jnp.where(bit, a, b) for a, b in zip(low, high)]
 
 
-def part_of(value, count, index):
-    rows = value.shape[0] // count
-    return lax.dynamic_slice_in_dim(value, index * rows, rows, 0)
-
-
-def gather_weight(w, f, x):
-    fsdp, dp = lax.axis_size("fsdp"), lax.axis_size("dp")
-    rows = w.shape[0]
-    sub = rows // dp
-    pieces, places = [w, hop(w, "fsdp", 1)], [f * rows, (f ^ 1) * rows]
-    mine = part_of(w, dp, x)
-    for ry in range(1, fsdp // 2):
-        first = hop(mine, "fsdp", 2 * ry)
-        for rx in range(dp):
-            got = first if rx == 0 else hop(first, "dp", rx)
-            pieces += [got, hop(got, "fsdp", 1)]
-            place = (x ^ rx) * sub
-            places += [(f ^ (2 * ry)) * rows + place, (f ^ (2 * ry + 1)) * rows + place]
-    return pieces, places
-
-
-def gather_half(w, f):
-    fsdp = lax.axis_size("fsdp")
-    rows = w.shape[0]
-    pieces, places = [], []
-    for ry in range(fsdp // 2):
-        got = w if ry == 0 else hop(w, "fsdp", 2 * ry)
-        pieces += [got, hop(got, "fsdp", 1)]
-        places += [(f ^ (2 * ry)) * rows, (f ^ (2 * ry + 1)) * rows]
-    return pieces, places
-
-
 def sum_all(value):
     for axis in ("fsdp", "dp", "seq"):
         m = 1
@@ -1033,7 +1197,7 @@
     fsdp = lax.axis_size("fsdp")
     ff = up_weight.shape[1]
     half = d // 2
-    f, x, s = lax.axis_index("fsdp"), lax.axis_index("dp"), lax.axis_index("seq")
+    f, s = lax.axis_index("fsdp"), lax.axis_index("seq")
     parity, slot = s % 2, s // 2
     caps, starts = caption_len[0], item_start[0]
     start = jnp.where(slot == 0, starts[0], starts[1] - SLOT)
@@ -1044,44 +1208,12 @@
         [f, parity, start, stop, pad_a, pad_b, s, starts[0], starts[0] + caps[0]]
     ).astype(jnp.int32)
 
-    head = hop(x_tok[:BLK], "seq", 1)
-    rest = hop(x_tok[BLK:], "seq", 1)
-    index = lax.broadcasted_iota(jnp.int32, (BLK, 1), 0)
-    pads = jnp.where(index < starts[0], head, x_tok[local_rows - BLK :])
-    pads = lax.ppermute(pads, "seq", [(1, 2)])
-    pads = jnp.where(s == 3, lax.ppermute(pads, "seq", [(2, 3)]), pads)
-
-    w_half = jnp.concatenate(
-        [lax.dynamic_slice_in_dim(qkv_weight, c * d + parity * half, half, 1) for c in range(3)], axis=1
+    dp = lax.axis_size("dp")
+    (q, k, v, n_t, np_t, kp, vp, w_qkv, mixed, lse, other, theirs, pads, wo, wu, wd) = front(
+        info, x_tok, qkv_weight, out_weight, up_weight, down_weight, norm_gain[0:1], norm_bias[0:1], fsdp, dp
     )
-    parts, places = gather_half(w_half, f)
-    gain0, bias0 = norm_gain[0:1], norm_bias[0:1]
-    q, k, v, n_t, w_qkv = project(
-        info, jnp.stack(places).astype(jnp.int32), x_tok, head, rest, gain0, bias0, parts
-    )
-    kp, vp, np_t = pad_project(pads, gain0, bias0, w_qkv)
-    mixed, lse = attend(info, q, k, v, kp, vp)
-    to_send = lax.dynamic_slice_in_dim(mixed, (1 - parity) * local_rows, local_rows, 0)
-    other = hop(to_send, "seq", 1)
-
-    parts, places, counts = [], [], []
-    for w in (out_weight, up_weight, down_weight):
-        got, at = gather_weight(w, f, x)
-        parts += got
-        places += at
-        counts.append(len(got))
-    (out, g_feed, act_t, slope, two_t, branch, middle, edges3, wo, wu, wd) = forward(
-        info,
-        jnp.stack(places).astype(jnp.int32),
-        (mixed, half, parity),
-        other,
-        x_tok,
-        up,
-        norm_gain,
-        norm_bias,
-        parts,
-        tuple(counts),
-        ff,
+    (out, g_feed, act_t, slope, two_t, branch, middle, edges3) = forward(
+        info, mixed, other, x_tok, up, norm_gain, norm_bias, wo, wu, wd
     )
     keeps, g_twos = [], []
     for g in range(GROUPS):
@@ -1094,7 +1226,7 @@
     d_other = hop(d_send, "seq", 1)
     dq, dk, dv, dkp, dvp = attend_back(info, q, k, v, kp, vp, mixed, lse, d_own, d_other)
     g_own, g_send, g_pad, keep_q, send_q, edges0 = project_back(
-        info, x_tok, head, rest, pads, norm_gain, dq, dk, dv, dkp, dvp, w_qkv, n_t, np_t, fsdp
+        info, x_tok, theirs, pads, norm_gain, dq, dk, dv, dkp, dvp, w_qkv, n_t, np_t, fsdp
     )
     g_other = hop(g_send, "seq", 1)
     back_a = lax.ppermute(g_pad, "seq", [(2, 0), (3, 1)])
@@ -1107,7 +1239,6 @@
         )
     )
 
-    dp = lax.axis_size("dp")
     done, done_q = reduce_all(keeps + [(keep_o, send_o), (keep_q, send_q)], fsdp, dp)
     rows = d // fsdp
     per = (done.shape[0] - 1) // GROUPS

time: 601 us -> 540 us (0.90)
  the two profiles are of different devices: /device:TPU:20 before, /device:TPU:0 now
where the time goes in v3:
time: 540 us; the launch traced here: 537 us
  Pallas kernels  437 us (81%)
  waiting for transfers between devices  53.2 us (10%)
  local copies, waits for them, and re-layouts  22.1 us (4%)
  other arithmetic  10.7 us (2%)
  starting transfers between devices  8.5 us (2%)
  between operations  5.74 us (1%)
    pallas_call x1, Pallas kernels, reduce_all(): pl.pallas_call(functools.partial(reduce_body, fsdp=fsdp, dp=dp, layout=la...  181 us
    pallas_call x1, Pallas kernels, front(): pl.pallas_call(functools.partial(front_body, fsdp=fsdp, dp=dp), in_specs=...  88.9 us
    ppermute x8, waiting for transfers between devices, hop(): lax.ppermute(value, axis, [(i, i ^ mask) for i in range(lax.axis_size(axi...  53.2 us
    pallas_call x2, Pallas kernels, back_group(): call(functools.partial(back_body, fsdp=fsdp), (fsdp,), 1, [full((local, d...  45.4 us
    pallas_call x1, Pallas kernels, attend_back(): call(attend_back_body, (pairs,), 1, [pair, pair, pair, pad, pad, pair, pl...  44.8 us
    pallas_call x1, Pallas kernels, forward(): call(forward_body, (ff // tile,), 1, [pl.BlockSpec((local, half), lambda...  33.9 us
    pallas_call x1, Pallas kernels, project_back(): call(functools.partial(project_back_body, fsdp=fsdp), (2,), 1, [pl.BlockS...  19.5 us
    pallas_call x1, Pallas kernels, middle_back(): call(functools.partial(middle_body, fsdp=fsdp), (local // rows,), 1, [blo...  15.3 us
  transfers between devices with their start and end apart: 10, of which 4 were waited for; matrix products, arithmetic and copies ran while one was open for 5% of the time, Pallas kernels for 34%

profile of v3, /device:TPU:0, one launch (start us, length us, event | category | flops | bytes accessed | tf_op | source)
XLA Modules:
  0.0 537.1 jit_solution(6954644365764947122)
XLA Ops:
  0.7 1.3 fusion.6
  2.0 1.3 fusion.7
  7.8 1.3 slice.164.bias
  9.1 1.3 slice.163.gain
  10.4 1.3 stack.38.info
  11.7 88.9 %shard_map.161 = (bf16[1280,512]{1,0:T(8,128)(2,1)}, bf16[1280,512]{1,0:T(8,128)(2,1)}, bf16[1280,512]{1,0:T(8,128)(2,1)}, bf16[1024,1280]{1,0:T(8,128)(2,1)}, b...) custom-call(s32[9]{0:T(128)} %stack.38.info, ...), custom_call_target="tpu_custom_call" | custom-call | flops 10000000000 | bytes 100000000 | tf_op jit(solution)/shard_map/pallas_call | solution.py:591
  100.6 33.9 %shard_map.162 = (bf16[640,1024]{1,0:T(8,128)(2,1)}, bf16[640,1024]{1,0:T(8,128)(2,1)}, bf16[4096,640]{1,0:T(8,128)(2,1)}, bf16[640,4096]{1,0:T(8,128)(2,1)}, bf...) custom-call(s32[9]{0:T(128)} %stack.38.info, ...), custom_call_target="tpu_custom_call" | custom-call | flops 12079595520 | bytes 40000000 | tf_op jit(solution)/shard_map/pallas_call | solution.py:666
  134.5 22.8 %shard_map.164 = (bf16[2,1024,1024]{2,1,0:T(8,128)(2,1)}, bf16[2,1024,1024]{2,1,0:T(8,128)(2,1)}, f32[640,1024]{1,0:T(8,128)}) custom-call(s32[9]{0:T(128)} %stack.38.info, bf16[640,1024]{1,0:T(8,128)(2,1)} %get-tuple-element.71.g_feed, bf16[1024,640]{1,0:T(8,128)(2,1)} %get-tuple-element.72.n_t, bf16[4096,640]{1,0:T(8,128)(2,1)} %get-tuple-element.73.act_t, ...), custom_call_target="tpu_custom_call" | custom-call | flops 10737418240 | bytes 40000000 | tf_op jit(solution)/shard_map/pallas_call | solution.py:753
  157.3 22.6 %shard_map.163 = (bf16[2,1024,1024]{2,1,0:T(8,128)(2,1)}, bf16[2,1024,1024]{2,1,0:T(8,128)(2,1)}, f32[640,1024]{1,0:T(8,128)}) custom-call(s32[9]{0:T(128)} %stack.38.info, bf16[640,1024]{1,0:T(8,128)(2,1)} %get-tuple-element.71.g_feed, bf16[1024,640]{1,0:T(8,128)(2,1)} %get-tuple-element.72.n_t, bf16[4096,640]{1,0:T(8,128)(2,1)} %get-tuple-element.73.act_t, ...), custom_call_target="tpu_custom_call" | custom-call | flops 10737418240 | bytes 40000000 | tf_op jit(solution)/shard_map/pallas_call | solution.py:753
  179.9 15.3 %shard_map.165 = (f32[640,1024]{1,0:T(8,128)}, bf16[640,512]{1,0:T(8,128)(2,1)}, bf16[640,512]{1,0:T(8,128)(2,1)}, bf16[2,256,1024]{2,1,0:T(8,128)(2,1)}, bf16[2...) custom-call(s32[9]{0:T(128)} %stack.38.info, f32[640,1024]{1,0:T(8,128)} %get-tuple-element.75.ga, ...), custom_call_target="tpu_custom_call" | custom-call | flops 2684354560 | bytes 22000000 | tf_op jit(solution)/shard_map/pallas_call | solution.py:813
  195.2 3.4 collective-permute-start
  198.6 0.0 copy-done.6
  198.6 0.9 fusion.3
  199.5 14.6 %collective-permute-done.d_other = bf16[640,512]{1,0:T(8,128)(2,1)S(1)} collective-permute-done((bf16[640,512]{1,0:T(8,128)(2,1)}, bf16[640,512]{1,0:T(8,128)(2,1)S(1)}, u32[]{:S(2)}, u32[]{:S(2)}) %collective-permute-start) | collective-permute-done | bytes 655392 | tf_op jit(solution)/shard_map/ppermute | solution.py:1170
  214.0 0.8 copy-done.7
  214.9 44.8 %shard_map.166 = (bf16[1280,512]{1,0:T(8,128)(2,1)}, bf16[1280,512]{1,0:T(8,128)(2,1)}, bf16[1280,512]{1,0:T(8,128)(2,1)}, bf16[256,512]{1,0:T(8,128)(2,1)}, bf16[256,512]{1,0:T(8,128)(2,1)}) custom-call(s32[9]{0:T(128)} %stack.38.info, bf16[1280,512]{1,0:T(8,128)(2,1)} %get-tuple-element.65.q, bf16[1280,512]{1,0:T(8,128)(2,1)} %get-tuple-element.66.k, ...), custom_call_target="tpu_custom_call" | custom-call | flops 22817013760 | bytes 14000000 | tf_op jit(solution)/shard_map/pallas_call | solution.py:219
  259.7 19.5 %shard_map.167 = (f32[640,1024]{1,0:T(8,128)}, bf16[640,1024]{1,0:T(8,128)(2,1)}, bf16[256,1024]{1,0:T(8,128)(2,1)}, bf16[2,256,1536]{2,1,0:T(8,128)(2,1)}, bf16...) custom-call(s32[9]{0:T(128)} %stack.38.info, bf16[640,1024]{1,0:T(8,128)(2,1)} %bitcast.50, ...), custom_call_target="tpu_custom_call" | custom-call | flops 8053063680 | bytes 24000000 | tf_op jit(solution)/shard_map/pallas_call | solution.py:879
  279.2 1.3 collective-permute-start.3
  280.5 1.3 collective-permute-start.2
  281.8 181.3 %shard_map.169 = (bf16[9,256,1024]{2,1,0:T(8,128)(2,1)}, bf16[3,256,512]{2,1,0:T(8,128)(2,1)}) custom-call(bf16[2,1024,1024]{2,1,0:T(8,128)(2,1)} %get-tuple-element.93.refs_0_, bf16[2,1024,1024]{2,1,0:T(8,128)(2,1)} %get-tuple-element.94.refs_1_, bf16[2,256,1024]{2,1,0:T(8,128)(2,1)} %get-tuple-element.95.refs_2_, ...), custom_call_target="tpu_custom_call" | custom-call | flops 100000000 | bytes 500000000 | tf_op jit(solution)/shard_map/pallas_call | solution.py:1151
  463.1 0.0 copy-start
  463.1 2.3 bitcast_convert_fusion
  465.4 2.8 fusion
  468.1 0.0 copy-done
  468.1 1.8 fusion.1
  470.0 0.0 copy-done.4
  470.0 0.9 slice_bitcast_fusion.2
  470.8 0.0 copy-done.5
  470.8 0.1 stack.39
  470.9 0.1 collective-permute-start.5
  471.0 1.1 pad_maximum_fusion
  472.1 0.1 collective-permute-start.4
  472.1 2.0 collective-permute-start.1
  474.2 0.9 slice_dynamic-update-slice_fusion.21
  475.1 0.9 slice_dynamic-update-slice_fusion.20
  476.0 0.0 copy-start.1
  476.1 1.0 slice_dynamic-update-slice_fusion.17
  477.1 0.9 slice_dynamic-update-slice_fusion.16
  478.0 0.9 slice_dynamic-update-slice_fusion.13
  479.0 0.9 slice_dynamic-update-slice_fusion.12
  479.9 0.9 slice_dynamic-update-slice_fusion.9
  480.9 0.0 collective-permute-done.5
  480.9 0.3 collective-permute-start.6
  481.2 0.9 slice_dynamic-update-slice_fusion.8
  482.1 2.8 collective-permute-done.6
  484.9 0.0 collective-permute-start.7
  484.9 3.9 collective-permute-done.7
  488.8 0.1 collective-permute-start.8
  488.9 32.0 %collective-permute-done.8 = f32[8,1024]{1,0:T(8,128)S(1)} collective-permute-done((f32[8,1024]{1,0:T(8,128)S(1)}, f32[8,1024]{1,0:T(8,128)S(1)}, u32[]{:S(2)}, u32[]{:S(2)}) %collective-permute-start.8) | collective-permute-done | bytes 32800 | tf_op jit(solution)/shard_map/ppermute | solution.py:1170
  520.9 0.0 collective-permute-start.9
  520.9 0.0 copy-done.1
  520.9 2.5 maximum_convert_fusion
  523.4 2.5 convert_element_type.18
  525.9 0.0 collective-permute-done.9
  525.9 0.6 fusion.2
  526.5 0.0 collective-permute-done.4
  526.5 0.0 copy-done.2
  526.5 0.0 copy-done.3
  526.5 0.3 broadcast_select_fusion
  527.0 2.0 convert_element_type.15
  529.0 0.0 collective-permute-done.3.pad_b
  529.0 0.0 collective-permute-done.2.pad_a
  529.0 0.0 collective-permute-done.1.g_other
  529.1 7.8 %shard_map.168 = bf16[640,1024]{1,0:T(8,128)(2,1)} custom-call(s32[9]{0:T(128)} %stack.38.info, bf16[640,1024]{1,0:T(8,128)(2,1)} %bitcast.51, f32[640,1024]{1,0:T(8,128)} %get-tuple-element.89.g_own, bf16[640,1024]{1,0:T(8,128)(2,1)} %collective-permute-done.1.g_other, bf16[256,1024]{1,0:T(8,128)(2,1)} %collective-permute-done.2.pad_a, ...), custom_call_target="tpu_custom_call" | custom-call | flops 10000000 | bytes 12000000 | tf_op jit(solution)/shard_map/pallas_call | solution.py:911
  (26 shorter events, 0.4 us)
Async XLA Ops:
  179.9 18.6 %copy-start.6 = (f32[2,1024]{1,0:T(2,128)S(1)}, f32[2,1024]{1,0:T(2,128)}, u32[]{:S(2)}) copy-start(f32[2,1024]{1,0:T(2,128)} %get-tuple-element.105) | copy-start | bytes 24580
  195.2 18.8 %collective-permute-start = (bf16[640,512]{1,0:T(8,128)(2,1)}, bf16[640,512]{1,0:T(8,128)(2,1)S(1)}, u32[]{:S(2)}, u32[]{:S(2)}) collective-permute-start(bf16[640,512]{1,0:T(8,128)(2,1)} %get-tuple-element.80), channel_id=1, source_target_pairs={{0,1},{1,0},{2,3},{3,2},{4,5},{5,4},{6,7},{7,6},{8,9},{9,8},{10,11... | collective-permute-start | bytes 1966088 | tf_op jit(solution)/shard_map/ppermute | solution.py:1170
  214.0 0.8 copy-start.7
  279.2 249.9 %collective-permute-start.3 = (bf16[256,1024]{1,0:T(8,128)(2,1)}, bf16[256,1024]{1,0:T(8,128)(2,1)}, u32[]{:S(2)}, u32[]{:S(2)}) collective-permute-start(bf16[256,1024]{1,0:T(8,128)(2,1)} %get-tuple-element.91), channel_id=1, source_target_pairs={{2,1},{3,0},{6,5},{7,4},{10,9},{11,8},{14,13},{15,12},{18,17},{19,... | collective-permute-start | bytes 1572872 | tf_op jit(solution)/shard_map/ppermute | solution.py:1233
  280.5 248.6 %collective-permute-start.2 = (bf16[256,1024]{1,0:T(8,128)(2,1)}, bf16[256,1024]{1,0:T(8,128)(2,1)}, u32[]{:S(2)}, u32[]{:S(2)}) collective-permute-start(bf16[256,1024]{1,0:T(8,128)(2,1)} %get-tuple-element.91), channel_id=1, source_target_pairs={{2,0},{3,1},{6,4},{7,5},{10,8},{11,9},{14,12},{15,13},{18,16},{19,... | collective-permute-start | bytes 1572872 | tf_op jit(solution)/shard_map/ppermute | solution.py:1232
  463.1 5.1 copy-start
  468.1 1.8 copy-start.4
  468.1 2.7 copy-start.5
  470.9 10.0 %collective-permute-start.5 = (f32[8,1024]{1,0:T(8,128)S(1)}, f32[8,1024]{1,0:T(8,128)S(1)}, u32[]{:S(2)}, u32[]{:S(2)}) collective-permute-start(f32[8,1024]{1,0:T(8,128)S(1)} %stack.39), channel_id=1, source_target_pairs={{0,8},{8,0},{16,24},{24,16},{1,9},{9,1},{17,25},{25,17},{2,10},{10... | collective-permute-start | bytes 98312 | tf_op jit(solution)/shard_map/ppermute | solution.py:1170
  472.1 54.4 %collective-permute-start.4 = (bf16[256,1536]{1,0:T(8,128)(2,1)S(1)}, bf16[256,1536]{1,0:T(8,128)(2,1)S(1)}, u32[]{:S(2)}, u32[]{:S(2)}) collective-permute-start(bf16[256,1536]{1,0:T(8,128)(2,1)S(1)} %pad_maximum_fusion), channel_id=1, source_target_pairs={{0,1},{1,0},{2,3},{3,2},{4,5},{5,4},{6,7},{7,6},{8,9},{9,8},{10,11... | collective-permute-start | bytes 2359304 | tf_op jit(solution)/shard_map/ppermute | solution.py:1170
  472.1 56.9 %collective-permute-start.1 = (bf16[640,1024]{1,0:T(8,128)(2,1)}, bf16[640,1024]{1,0:T(8,128)(2,1)}, u32[]{:S(2)}, u32[]{:S(2)}) collective-permute-start(bf16[640,1024]{1,0:T(8,128)(2,1)} %get-tuple-element.90), channel_id=1, source_target_pairs={{0,1},{1,0},{2,3},{3,2},{4,5},{5,4},{6,7},{7,6},{8,9},{9,8},{10,11... | collective-permute-start | bytes 3932168 | tf_op jit(solution)/shard_map/ppermute | solution.py:1170
  476.0 44.9 %copy-start.1 = (bf16[2,256,1024]{2,1,0:T(8,128)(2,1)S(1)}, bf16[2,256,1024]{2,1,0:T(8,128)(2,1)}, u32[]{:S(2)}) copy-start(bf16[2,256,1024]{2,1,0:T(8,128)(2,1)} %get-tuple-element.107) | copy-start | bytes 3145732
  480.9 4.0 collective-permute-start.6
  484.9 3.9 collective-permute-start.7
  488.8 32.1 %collective-permute-start.8 = (f32[8,1024]{1,0:T(8,128)S(1)}, f32[8,1024]{1,0:T(8,128)S(1)}, u32[]{:S(2)}, u32[]{:S(2)}) collective-permute-start(f32[8,1024]{1,0:T(8,128)S(1)} %add.38), channel_id=1, source_target_pairs={{0,1},{1,0},{2,3},{3,2},{4,5},{5,4},{6,7},{7,6},{8,9},{9,8},{10,11... | collective-permute-start | bytes 98312 | tf_op jit(solution)/shard_map/ppermute | solution.py:1170
  520.9 5.0 collective-permute-start.9
  523.4 3.2 copy-start.2
  523.4 3.2 copy-start.3

commit v4 on v3

--- a/solution.py
+++ b/solution.py
@@ -17,7 +17,7 @@
 F32 = jnp.float32
 BF16 = jnp.bfloat16
 VMEM_LIMIT = 60 * 1024 * 1024
-GROUPS = 2
+PIECES = 4
 
 
 def nn(a, b):
@@ -128,25 +128,13 @@
         o(slice(i * BLK, n), jnp.where(lane < HD, outs[0], outs[1]).astype(BF16))
 
 
-def attend_back_body(
-    info, q, k, v, kp, vp, o, lse, d_own, d_other, dq, dk, dv, dkp, dvp, do, dk_sum, dv_sum, dkp_sum, dvp_sum
-):
-    parity, start, stop, pad_a, pad_b = info[1], info[2], info[3], info[4], info[5]
-    local = d_own.shape[0]
-    do[pl.ds(pl.multiple_of(parity * local, 128), local), :] = d_own[...]
-    do[pl.ds(pl.multiple_of((1 - parity) * local, 128), local), :] = d_other[...]
+def attend_back_pair(bounds, q, k, v, kp, vp, o, lse, do, dq, dk_sum, dv_sum, dkp_sum, dvp_sum):
+    start, stop, pad_a, pad_b = bounds
     lane = lax.broadcasted_iota(jnp.int32, (1, 2 * HD), 1)
     pick = (
         lax.broadcasted_iota(jnp.int32, (8, 2 * HD), 1) // HD
         == lax.broadcasted_iota(jnp.int32, (8, 2 * HD), 0)
     ).astype(F32)
-    inner = lax.dot_general(
-        pick,
-        do[...].astype(F32) * o[...].astype(F32),
-        (((1,), (1,)), ((), ())),
-        precision=lax.Precision.HIGHEST,
-        preferred_element_type=F32,
-    )
     row = lax.broadcasted_iota(jnp.int32, (BLK, 1), 0)
     col = lax.broadcasted_iota(jnp.int32, (1, 2 * BLK), 1) % BLK
     causal = row <= col
@@ -163,10 +151,18 @@
 
     for i in range(count):
         rows = slice(i * BLK, (i + 1) * BLK)
-        qs = jnp.concatenate(split(q[rows, :]), axis=0)
-        ds = jnp.concatenate(split(do[rows, :]), axis=0)
-        level = jnp.concatenate([lse[0, 0:1, rows], lse[0, 1:2, rows]], axis=1)
-        inner_i = jnp.concatenate([inner[0:1, rows], inner[1:2, rows]], axis=1)
+        do_i = do(rows)
+        qs = jnp.concatenate(split(q(rows)), axis=0)
+        ds = jnp.concatenate(split(do_i), axis=0)
+        level = jnp.concatenate([lse(0, rows), lse(1, rows)], axis=1)
+        inner = lax.dot_general(
+            pick,
+            do_i.astype(F32) * o(rows).astype(F32),
+            (((1,), (1,)), ((), ())),
+            precision=lax.Precision.HIGHEST,
+            preferred_element_type=F32,
+        )
+        inner = jnp.concatenate([inner[0:1, :], inner[1:2, :]], axis=1)
         edge = i in (0, count - 1)
         pos_q = col + i * BLK
         in_q = (pos_q >= start) & (pos_q < stop)
@@ -177,7 +173,7 @@
             if mask is not None:
                 s = jnp.where(mask, s, NEG)
             p = jnp.exp2(s)
-            g = p * (nt(vj, ds) - inner_i)
+            g = p * (nt(vj, ds) - inner)
             p, g = p.astype(BF16), g.astype(BF16)
             halves = split(kj)
             part = tn(g[:, :BLK], halves[0]) + tn(g[:, BLK:], halves[1])
@@ -194,45 +190,16 @@
                 mask = jnp.broadcast_to(pos_k >= start, (BLK, 2 * BLK))
             if j == i:
                 mask = causal if mask is None else mask & causal
-            gk, gv, part = block(k[keys, :], v[keys, :], mask)
+            gk, gv, part = block(k(keys), v(keys), mask)
             dk_sum[keys, :] += gk
             dv_sum[keys, :] += gv
             dq_sum = dq_sum + part
         if edge:
-            gk, gv, part = block(kp[...], vp[...], ~in_q & pad_row)
+            gk, gv, part = block(kp(slice(None)), vp(slice(None)), ~in_q & pad_row)
             dkp_sum[...] += gk
             dvp_sum[...] += gv
             dq_sum = dq_sum + part
-        dq[rows, :] = (dq_sum * 0.125).astype(BF16)
-    dk[...] = (dk_sum[...] * 0.125).astype(BF16)
-    dv[...] = dv_sum[...].astype(BF16)
-    dkp[...] = (dkp_sum[...] * 0.125).astype(BF16)
-    dvp[...] = dvp_sum[...].astype(BF16)
-
-
-def attend_back(info, q, k, v, kp, vp, o, lse, d_own, d_other):
-    rows, half = q.shape
-    pads = kp.shape[0]
-    pairs = half // (2 * HD)
-    pick = lambda n: pl.BlockSpec((n, 2 * HD), lambda i, info: (0, i))
-    pair, pad, part = pick(rows), pick(pads), pick(d_own.shape[0])
-    return call(
-        attend_back_body,
-        (pairs,),
-        1,
-        [pair, pair, pair, pad, pad, pair, pl.BlockSpec((1, 2, rows), lambda i, info: (i, 0, 0)), part, part],
-        [pair, pair, pair, pad, pad],
-        [shape((rows, half), BF16)] * 3 + [shape((pads, half), BF16)] * 2,
-        [
-            pltpu.VMEM((rows, 2 * HD), BF16),
-            pltpu.VMEM((rows, 2 * HD), F32),
-            pltpu.VMEM((rows, 2 * HD), F32),
-            pltpu.VMEM((pads, 2 * HD), F32),
-            pltpu.VMEM((pads, 2 * HD), F32),
-        ],
-        flops=pairs * 34 * BLK * BLK * 256 * 10,
-        moved=14e6,
-    )(info, q, k, v, kp, vp, o, lse, d_own, d_other)
+        dq(rows, (dq_sum * 0.125).astype(BF16))
 
 
 def peer(axis, mask):
@@ -704,34 +671,12 @@
     )(info, mixed, other, x, up, gains, biases, wo, wu, wd)
 
 
-def back_body(info, g_feed, n_t, act_t, slope, wd, wu, keep, send, g_two, *, fsdp):
+def back_body(info, g_feed, slope, wd, wu, hid_out, g_two):
     r = pl.program_id(0)
-    f = info[0]
-    tile = wd.shape[0]
-    rows = n_t.shape[0] // fsdp
-    width = keep.shape[2]
-    piece = width // fsdp
-    here = r ^ f
-    g = g_feed[...]
-    hid = (nt(g, wd[...]) * slope[...].astype(F32)).astype(BF16)
-    down = nn(act_t[...], g).astype(BF16)
-    even = r % 2 == 0
-
-    @pl.when(even)
-    def _():
-        keep[r // 2, 0:tile, :] = down
-
-    @pl.when(~even)
-    def _():
-        send[r // 2, 0:tile, :] = down
-
-    lanes = pl.ds(pl.multiple_of(here * piece, 128), piece)
-    for other in range(fsdp):
-        shard = other ^ f
-        up = nn(n_t[pl.ds(pl.multiple_of(shard * rows, 128), rows), :], hid).astype(BF16)
-        target = (keep, send)[other % 2]
-        for c in range(tile // piece):
-            target[other // 2, tile + c * rows : tile + (c + 1) * rows, lanes] = up[:, c * piece : (c + 1) * piece]
+    hid = (nt(g_feed[...], wd[...]) * slope[...].astype(F32)).astype(BF16)
+    pieces, _, width = hid_out.shape
+    for c in range(pieces):
+        hid_out[c] = hid[:, c * width : (c + 1) * width]
     part = nt(hid, wu[...])
 
     @pl.when(r == 0)
@@ -743,46 +688,37 @@
         g_two[...] += part
 
 
-def back_group(info, g, g_feed, n_t, act_t, slope, wd, wu, fsdp):
+def back(info, g_feed, slope, wd, wu, fsdp):
     local, d = g_feed.shape
     ff = wd.shape[0]
-    tile = ff // fsdp // GROUPS
-    extra = (d // fsdp) * (fsdp * tile // d)
-    block = lambda i, info: (i ^ info[0]) * GROUPS + g
-    grads = shape((fsdp // 2, tile + extra, d), BF16)
+    tile = ff // fsdp
     return call(
-        functools.partial(back_body, fsdp=fsdp),
+        back_body,
         (fsdp,),
         1,
         [
             full((local, d)),
-            full((d, local)),
-            pl.BlockSpec((tile, local), lambda i, info: (block(i, info), 0)),
-            pl.BlockSpec((local, tile), lambda i, info: (0, block(i, info))),
-            pl.BlockSpec((tile, d), lambda i, info: (block(i, info), 0)),
-            pl.BlockSpec((d, tile), lambda i, info: (0, block(i, info))),
+            pl.BlockSpec((local, tile), lambda i, info: (0, i)),
+            pl.BlockSpec((tile, d), lambda i, info: (i, 0)),
+            pl.BlockSpec((d, tile), lambda i, info: (0, i)),
         ],
-        [full(grads.shape), full(grads.shape), full((local, d))],
-        [grads, grads, shape((local, d), F32)],
-        flops=8 * local * d * tile * fsdp,
-        moved=40e6,
-    )(info, g_feed, n_t, act_t, slope, wd, wu)
-
-
-def middle_body(
-    info, ga, gb, middle, branch, up, gains, wo, own, other, g_mid, d_own, d_send, keep, send, edges, att, gbr, *, fsdp
-):
-    f, parity = info[0], info[1]
+        [pl.BlockSpec((PIECES, local, tile // PIECES), lambda i, info: (0, 0, i)), full((local, d))],
+        [shape((PIECES, local, ff // PIECES), BF16), shape((local, d), F32)],
+        flops=4 * local * d * ff,
+        moved=35e6,
+    )(info, g_feed, slope, wd, wu)
+
+
+def middle_body(info, g, middle, branch, up, gains, wo, g_mid, d_own, d_send, gbr, edges):
+    parity = info[1]
     step, last = pl.program_id(0), pl.num_programs(0) - 1
-    half = own.shape[1]
+    half = d_own.shape[1]
 
     @pl.when(step == 0)
     def _():
         edges[...] = jnp.zeros_like(edges)
-        att[:, pl.ds(pl.multiple_of(parity * half, 128), half)] = own[...]
-        att[:, pl.ds(pl.multiple_of((1 - parity) * half, 128), half)] = other[...]
-
-    g = ga[...] + gb[...]
+
+    g = g[...]
     hat, rstd = normalise(middle[...])
     edges[2:3, :] += jnp.sum(g * hat, axis=0, keepdims=True)
     edges[3:4, :] += jnp.sum(g, axis=0, keepdims=True)
@@ -799,126 +735,28 @@
         grad = gbr[...]
         d_send[...] = nt(grad, wo[pl.ds(pl.multiple_of((1 - parity) * half, 128), half), :]).astype(BF16)
         d_own[...] = nt(grad, wo[pl.ds(pl.multiple_of(parity * half, 128), half), :]).astype(BF16)
-        rows = keep.shape[1]
-        for r in range(fsdp):
-            cols = pl.ds(pl.multiple_of((r ^ f) * rows, 128), rows)
-            (keep, send)[r % 2][r // 2] = tn(att[:, cols], grad).astype(BF16)
-
-
-def middle_back(info, ga, gb, middle, branch, up, gains, wo, attn, half, other, fsdp):
-    local, d = ga.shape
-    rows = 128
+
+
+def middle_back(info, g, middle, branch, up, gains, wo):
+    local, d = g.shape
+    rows, half = 128, d // 2
     block = pl.BlockSpec((rows, d), lambda i, info: (i, 0))
-    grads = shape((fsdp // 2, d // fsdp, d), BF16)
     return call(
-        functools.partial(middle_body, fsdp=fsdp),
+        middle_body,
         (local // rows,),
         1,
-        [block, block, block, block, block, full(gains.shape), full(wo.shape)]
-        + [pl.BlockSpec((local, half), lambda i, info: (info[1], 0)), full(other.shape)],
-        [block, full((local, half)), full((local, half)), full(grads.shape), full(grads.shape), full((4, d))],
-        [shape((local, d), F32), shape((local, half), BF16), shape((local, half), BF16), grads, grads, shape((4, d), F32)],
-        [pltpu.VMEM((local, d), BF16), pltpu.VMEM((local, d), BF16)],
-        flops=4 * local * d * d,
-        moved=22e6,
-    )(info, ga, gb, middle, branch, up, gains, wo, attn, other)
-
-
-def project_back_body(
-    info, own, theirs, padx, gains, dq, dk, dv, dkp, dvp, w, n_t, np_t, g_own, g_send, g_pad, keep, send, edges, *, fsdp
-):
-    f, parity = info[0], info[1]
-    step = pl.program_id(0)
-    local = own.shape[0]
-    half = dq.shape[1]
-    gain = gains[0:1, :]
-
-    def through(at):
-        return (
-            nt(dq[at, :], w[:, 0:half])
-            + nt(dk[at, :], w[:, half : 2 * half])
-            + nt(dv[at, :], w[:, 2 * half :])
-        )
-
-    @pl.when(step == 0)
-    def _():
-        g = nt(dkp[...], w[:, half : 2 * half]) + nt(dvp[...], w[:, 2 * half :])
-        g_pad[...] = g.astype(BF16)
-        hat, _ = normalise(padx[...].astype(F32))
-        edges[0:1, :] = jnp.sum(g * hat, axis=0, keepdims=True)
-        edges[1:2, :] = jnp.sum(g, axis=0, keepdims=True)
-        g = through(pl.ds(pl.multiple_of((1 - parity) * local, 128), local))
-        g_send[...] = g.astype(BF16)
-        hat, _ = normalise(theirs[...].astype(F32))
-        edges[0:1, :] += jnp.sum(g * hat, axis=0, keepdims=True)
-        edges[1:2, :] += jnp.sum(g, axis=0, keepdims=True)
-
-    @pl.when(step == 1)
-    def _():
-        g = through(pl.ds(pl.multiple_of(parity * local, 128), local))
-        g_own[...] = g
-        hat, _ = normalise(own[...].astype(F32))
-        edges[0:1, :] += jnp.sum(g * hat, axis=0, keepdims=True)
-        edges[1:2, :] += jnp.sum(g, axis=0, keepdims=True)
-        rows = keep.shape[1]
-        for r in range(fsdp):
-            at = pl.ds(pl.multiple_of((r ^ f) * rows, 128), rows)
-            target = (keep, send)[r % 2]
-            left, pads = n_t[at, :], np_t[at, :]
-            target[r // 2, :, 0:half] = nn(left, dq[...]).astype(BF16)
-            target[r // 2, :, half : 2 * half] = (nn(left, dk[...]) + nn(pads, dkp[...])).astype(BF16)
-            target[r // 2, :, 2 * half :] = (nn(left, dv[...]) + nn(pads, dvp[...])).astype(BF16)
-
-
-def project_back(info, own, theirs, padx, gains, dq, dk, dv, dkp, dvp, w, n_t, np_t, fsdp):
-    local, d = own.shape
-    wide = w.shape[1]
-    pads = padx.shape[0]
-    grads = shape((fsdp // 2, d // fsdp, wide), BF16)
-    arrays = (own, theirs, padx, gains, dq, dk, dv, dkp, dvp, w, n_t, np_t)
-    return call(
-        functools.partial(project_back_body, fsdp=fsdp),
-        (2,),
-        1,
-        [pl.BlockSpec(a.shape, lambda *_: (0, 0), pipeline_mode=pl.Buffered(1)) for a in arrays],
-        [full((local, d)), full((local, d)), full((pads, d)), full(grads.shape), full(grads.shape), full((2, d))],
-        [shape((local, d), F32), shape((local, d), BF16), shape((pads, d), BF16), grads, grads, shape((2, d), F32)],
-        flops=8 * local * d * wide,
-        moved=24e6,
-    )(info, *arrays)
-
-
-def finish_body(info, x, g_own, g_other, pad_a, pad_b, g_mid, gains, out, total):
-    s, start, cut = info[6], info[7], info[8]
-    row = lax.broadcasted_iota(jnp.int32, (pad_a.shape[0], 1), 0)
-    mine = ((s == 0) & (row < start)) | ((s == 1) & (row >= cut))
-    extra = jnp.where(mine, pad_a[...].astype(F32) + pad_b[...].astype(F32), 0.0)
-    total[...] = g_own[...] + g_other[...].astype(F32)
-    at = pl.ds(pl.multiple_of(jnp.where(s == 0, 0, total.shape[0] - pad_a.shape[0]), 128), pad_a.shape[0])
-    total[at, :] += extra
-
-    def rows(i, carry):
-        at = pl.ds(pl.multiple_of(i * 128, 128), 128)
-        hat, rstd = normalise(x[at, :].astype(F32))
-        out[at, :] = (g_mid[at, :] + norm_back(total[at, :], hat, rstd, gains[0:1, :])).astype(BF16)
-        return carry
-
-    lax.fori_loop(0, x.shape[0] // 128, rows, 0)
-
-
-def finish(info, x, g_own, g_other, pad_a, pad_b, g_mid, gains):
-    arrays = (x, g_own, g_other, pad_a, pad_b, g_mid, gains)
-    return call(
-        finish_body,
-        (1,),
-        1,
-        [full(a.shape) for a in arrays],
-        full(x.shape),
-        shape(x.shape, BF16),
-        [pltpu.VMEM(x.shape, F32)],
-        flops=1e7,
-        moved=12e6,
-    )(info, *arrays)
+        [block, block, block, block, full(gains.shape), full(wo.shape)],
+        [block, full((local, half)), full((local, half)), full((local, d)), full((4, d))],
+        [
+            shape((local, d), F32),
+            shape((local, half), BF16),
+            shape((local, half), BF16),
+            shape((local, d), BF16),
+            shape((4, d), F32),
+        ],
+        flops=2 * local * d * d,
+        moved=18e6,
+    )(info, g, middle, branch, up, gains, wo)
 
 
 class Lane:
@@ -1023,10 +861,7 @@
 
         lax.fori_loop(0, rows // step, body, 0)
 
-    def one(self, u, keep):
-        self.core(u, keep).wait_recv()
-        for ry in range(self.ys):
-            self.add(self.acc.at[u, ry], [keep.at[ry]])
+    def start_y(self, u):
         for ry in range(1, self.ys):
             self.over_y(u, ry).start()
 
@@ -1065,8 +900,7 @@
         for rx in range(1, self.dp):
             self.back_x(u, rx).wait_recv()
 
-    def drain(self, u, src):
-        self.core(u, src).wait_send()
+    def drain(self, u):
         for ry in range(1, self.ys):
             self.over_y(u, ry).wait_send()
         for rx in range(1, self.dp):
@@ -1086,107 +920,415 @@
     )
 
 
-def reduce_body(*refs, fsdp, dp, layout):
-    n_in = len(layout)
-    keeps, sends = refs[:n_in], refs[n_in : 2 * n_in]
-    final_a, final_b = refs[2 * n_in : 2 * n_in + 2]
-    rest = refs[2 * n_in + 2 :]
-    held_a, held_b, load_a, load_b = rest[:4]
-    a = Lane(rest[4 : 4 + Lane.size], final_a, fsdp, dp, (1, 2, 3), 1)
-    b = Lane(rest[4 + Lane.size :], final_b, fsdp, dp, (2,), 2)
+def doublings(fsdp, dp, seq):
+    steps = []
+    for axis, size in (("fsdp", fsdp), ("dp", dp), ("seq", seq)):
+        m = 1
+        while m < size:
+            steps.append((axis, m))
+            m *= 2
+    return steps
+
+
+def rear_body(
+    info, d_send, d_own, act_t, hid, g_feed, two_t, mixed_rows, other, gbr, q, k, v, mixed, kp, vp, lse,
+    w, n_t, np_t, tokens, theirs, padx, g_mid, gains, edges3, edges12,
+    final_a, final_b, grad_in, sums,
+    *rest, fsdp, dp, seq
+):
+    a = Lane(rest[: Lane.size], final_a, fsdp, dp, (1, 2, 3), 1)
+    rest = rest[Lane.size :]
+    parity = lax.axis_index("seq") % 2
+    b = Lane(rest[: Lane.size], final_b.at[parity], fsdp, dp, (2,), 2)
+    (
+        ring, ring_b, do, dq, dk, dv, dkp, dvp, dk_sum, dv_sum, dkp_sum, dvp_sum,
+        g_out, g_in, gp_out, gp_in, run, got, load, d_s, d_r, gs_s, gs_r, gp_s, gp_r, e_s, e_r, p_s, p_r,
+    ) = rest[Lane.size :]
+    f, s = lax.axis_index("fsdp"), lax.axis_index("seq")
+    local, half = d_own.shape
+    d = 2 * half
+    ys = fsdp // 2
+    rows = a.rows
+    mate = peer("seq", 1)
+    bounds = tuple(info[i] for i in range(2, 6))
     greet(partners(fsdp, dp))
 
-    def views(lane, held, load):
-        u = 0
-        for i, (kind, cuts) in enumerate(layout):
-            if kind != (lane is b):
-                continue
-            for cut in range(cuts):
-                if kind:
-                    at = (slice(None), slice(None), pl.ds(cut * lane.cols, lane.cols))
-                else:
-                    at = (slice(None), pl.ds(cut * lane.rows, lane.rows))
-                yield u, sends[i].at[at], functools.partial(
-                    pltpu.make_async_copy, keeps[i].at[at], held.at[u], load.at[u]
-                )
-                u += 1
-
-    lanes = ((a, held_a, load_a), (b, held_b, load_b))
-    for lane, held, load in lanes:
-        for u, src, copy in views(lane, held, load):
-            lane.core(u, src).start()
-            copy().start()
-    for lane, held, load in lanes:
-        for u, src, copy in views(lane, held, load):
-            copy().wait()
-    total = a.count + b.count
-
-    def tick(t, carry):
-        for offset, name in ((0, "one"), (2, "two"), (3, "three"), (4, "four"), (5, "five"), (6, "six")):
-            for lane, held, first in ((a, held_a, 0), (b, held_b, a.count)):
+    my_rows = pl.ds(pl.multiple_of(parity * local, 128), local)
+    mate_rows = pl.ds(pl.multiple_of((1 - parity) * local, 128), local)
+    give = remote(d_send, do.at[my_rows], d_s.at[0], d_r.at[0], mate)
+    give.start()
+    take = pltpu.make_async_copy(d_own, do.at[my_rows], load.at[0])
+    take.start()
+
+    def shard(r):
+        return r ^ f
+
+    def band(r):
+        return pl.ds(pl.multiple_of(shard(r) * rows, 16), rows)
+
+    def feed_phase(act_v, hid_v, g_v, two_v, att, gbr_v):
+        def fetch(c):
+            return [
+                pltpu.make_async_copy(act_t.at[:, c], act_v.at[c], load.at[1 + c]),
+                pltpu.make_async_copy(hid.at[c], hid_v.at[c], load.at[1 + PIECES + c]),
+            ]
+
+        base = 1 + 2 * PIECES
+        common = [
+            pltpu.make_async_copy(g_feed, g_v, load.at[base]),
+            pltpu.make_async_copy(two_t, two_v, load.at[base + 1]),
+        ]
+        attn = [
+            pltpu.make_async_copy(
+                mixed_rows.at[parity], att.at[:, pl.ds(pl.multiple_of(parity * half, 128), half)], load.at[base + 2]
+            ),
+            pltpu.make_async_copy(
+                other, att.at[:, pl.ds(pl.multiple_of((1 - parity) * half, 128), half)], load.at[base + 3]
+            ),
+            pltpu.make_async_copy(gbr, gbr_v, load.at[base + 4]),
+        ]
+        for copy in common[:1] + fetch(0) + common[1:]:
+            copy.start()
+        for c in range(1, PIECES):
+            for copy in fetch(c):
+                copy.start()
+        for copy in attn:
+            copy.start()
+        for copy in common:
+            copy.wait()
+
+        def down(c, r):
+            return nn(act_v[c, shard(r)], g_v[...])
+
+        def up(c, r):
+            return nn(two_v[band(r), :], hid_v[c])
+
+        def step(c, carry):
+            @pl.when(c < PIECES)
+            def _():
+                for kind in range(2):
+                    pltpu.make_async_copy(
+                        (act_t.at[:, c], hid.at[c])[kind],
+                        (act_v.at[c], hid_v.at[c])[kind],
+                        load.at[1 + kind * PIECES + c],
+                    ).wait()
+                for kind, make in ((0, down), (1, up)):
+                    u = 2 * c + kind
+                    slot = ring.at[u % 4]
+
+                    @pl.when(c >= 2)
+                    def _():
+                        a.core(u - 4, slot).wait_send()
+
+                    for ry in range(ys):
+                        slot[ry] = make(c, 2 * ry + 1).astype(BF16)
+                    a.core(u, slot).start()
+
+            @pl.when(c >= 1)
+            def _():
+                for kind, make in ((0, down), (1, up)):
+                    u = 2 * (c - 1) + kind
+                    a.core(u, ring.at[u % 4]).wait_recv()
+                    for ry in range(ys):
+                        a.acc[u, ry] = (make(c - 1, 2 * ry) + a.acc[u, ry].astype(F32)).astype(BF16)
+
+                    @pl.when(c == 1)
+                    def _():
+                        a.start_y(u)
+
+            return carry
+
+        lax.fori_loop(0, PIECES + 1, step, 0)
+        u = 2 * PIECES
+        a.core(u - 4, ring.at[0]).wait_send()
+        for copy in attn:
+            copy.wait()
+        for ry in range(ys):
+            ring[0, ry] = tn(att[:, band(2 * ry + 1)], gbr_v[...]).astype(BF16)
+        a.core(u, ring.at[0]).start()
+        for ry in range(ys):
+            held = tn(att[:, band(2 * ry)], gbr_v[...])
+            if ry == 0:
+                a.core(u, ring.at[0]).wait_recv()
+            a.acc[u, ry] = (held + a.acc[u, ry].astype(F32)).astype(BF16)
+
+    def tick(t):
+        plan = ((0, "two"), (-2, "start_y"), (1, "three"), (2, "four"), (3, "five"), (4, "six"), (5, "seven"))
+        for offset, name in plan:
+            for lane, first in ((a, 0), (b, a.count)):
                 u = t - offset - first
-
-                @pl.when((u >= 0) & (u < lane.count))
-                def _():
-                    if name == "one":
-                        lane.one(u, held.at[u])
-                    else:
+                if name == "start_y" and lane is a and isinstance(u, int) and u < 2:
+                    continue
+                if name == "seven":
+                    if lane is a or not isinstance(t, int) or not 0 <= u < lane.count:
+                        continue
+                    seven(u).start()
+                    continue
+                if isinstance(u, int):
+                    if 0 <= u < lane.count:
                         getattr(lane, name)(u)
-
-        return carry
-
-    lax.fori_loop(0, total + 6, tick, 0)
-    for lane, held, load in lanes:
-        for u, src, copy in views(lane, held, load):
-            lane.drain(u, src)
-
-
-def reduce_all(pairs, fsdp, dp):
-    d = pairs[0][0].shape[2]
-    rows = d // fsdp
-    layout = tuple((False, k.shape[1] // rows) for k, _ in pairs[:-1]) + ((True, 3),)
-    n_a = sum(c for kind, c in layout if not kind)
-    wide = pairs[-1][0].shape[2] // 3
-    y = fsdp // 2
+                elif lane is a:
+
+                    @pl.when((u >= 0) & (u < lane.count))
+                    def _():
+                        getattr(lane, name)(u)
+
+    def seven(u):
+        here = final_b.at[parity, u]
+        return remote(here, here, p_s.at[u], p_r.at[u], mate)
+
+    def attention_phase(q_v, k_v, v_v, o_v, kp_v, vp_v, lse_v):
+        pairs = ((q, q_v), (k, k_v), (v, v_v), (mixed, o_v), (kp, kp_v), (vp, vp_v), (lse, lse_v))
+        copies = [pltpu.make_async_copy(x, y, load.at[16 + i]) for i, (x, y) in enumerate(pairs)]
+        for copy in copies:
+            copy.start()
+        take.wait()
+        for copy in copies:
+            copy.wait()
+        give.wait_recv()
+
+        def step(i, carry):
+            lanes = pl.ds(pl.multiple_of(i * 2 * HD, 128), 2 * HD)
+
+            def put(at, value):
+                dq[at, lanes] = value
+
+            attend_back_pair(
+                bounds,
+                lambda at: q_v[at, lanes],
+                lambda at: k_v[at, lanes],
+                lambda at: v_v[at, lanes],
+                lambda at: kp_v[at, lanes],
+                lambda at: vp_v[at, lanes],
+                lambda at: o_v[at, lanes],
+                lambda h, at: lse_v[i, h : h + 1, at],
+                lambda at: do[at, lanes],
+                put,
+                dk_sum,
+                dv_sum,
+                dkp_sum,
+                dvp_sum,
+            )
+            dk[:, lanes] = (dk_sum[...] * 0.125).astype(BF16)
+            dv[:, lanes] = dv_sum[...].astype(BF16)
+            dkp[:, lanes] = (dkp_sum[...] * 0.125).astype(BF16)
+            dvp[:, lanes] = dvp_sum[...].astype(BF16)
+            tick(i)
+            return carry
+
+        lax.fori_loop(0, half // (2 * HD), step, 0)
+
+    steps = doublings(fsdp, dp, seq)
+
+    def double(i):
+        axis, m = steps[i]
+        return remote(run.at[i], got.at[i], e_s.at[i], e_r.at[i], peer(axis, m))
+
+    def double_start(i):
+        double(i).start()
+
+    def double_end(i):
+        double(i).wait_recv()
+        run[i + 1] = run[i] + got[i]
+
+    def project_phase(w_v, nt_v, npt_v, x_v, y_v, px_v, mid_v, own, out_v):
+        pairs = (
+            (w, w_v), (n_t, nt_v), (np_t, npt_v), (padx, px_v), (theirs, y_v), (tokens, x_v), (g_mid, mid_v),
+        )
+        copies = [pltpu.make_async_copy(x, y, load.at[16 + i]) for i, (x, y) in enumerate(pairs)]
+        for copy in copies:
+            copy.start()
+        gain = gains[0:1, :]
+        back_rows = (dq, dk, dv)
+        back_pads = (None, dkp, dvp)
+
+        def grad(c, r):
+            total = nn(nt_v[band(r), :], back_rows[c][...])
+            if c:
+                total = total + nn(npt_v[band(r), :], back_pads[c][...])
+            return total
+
+        for copy in copies[:3]:
+            copy.wait()
+        for c in range(3):
+            for ry in range(ys):
+                ring_b[c, ry] = grad(c, 2 * ry + 1).astype(BF16)
+            b.core(c, ring_b.at[c]).start()
+        for c in range(3):
+            for ry in range(ys):
+                held = grad(c, 2 * ry)
+                if ry == 0:
+                    b.core(c, ring_b.at[c]).wait_recv()
+                b.acc[c, ry] = (held + b.acc[c, ry].astype(F32)).astype(BF16)
+        tick(4)
+
+        def weight(c):
+            return w_v[:, c * half : (c + 1) * half]
+
+        def count(g, x):
+            hat, _ = normalise(x.astype(F32))
+            return jnp.sum(g * hat, axis=0, keepdims=True), jnp.sum(g, axis=0, keepdims=True)
+
+        for copy in copies[3:]:
+            copy.wait()
+        g = nt(dkp[...], weight(1)) + nt(dvp[...], weight(2))
+        gp_out[...] = g.astype(BF16)
+        for i in range(2):
+            back_pad = remote(gp_out, gp_in.at[i], gp_s.at[i], gp_r.at[i], peer("seq", 2 + i))
+
+            @pl.when(s >= 2)
+            def _():
+                back_pad.start()
+
+        edge = count(g, px_v[...])
+
+        def through(first, source, store):
+            def body(i, carry):
+                at = pl.ds(pl.multiple_of(first + i * 128, 128), 128)
+                here = pl.ds(pl.multiple_of(i * 128, 128), 128)
+                g = nt(dq[at, :], weight(0)) + nt(dk[at, :], weight(1)) + nt(dv[at, :], weight(2))
+                store(here, g)
+                one, two = count(g, source[here, :])
+                return carry[0] + one, carry[1] + two
+
+            return lax.fori_loop(0, local // 128, body, edge)
+
+        def store_out(at, value):
+            g_out[at, :] = value.astype(BF16)
+
+        def store_own(at, value):
+            own[at, :] = value
+
+        edge = through((1 - parity) * local, y_v, store_out)
+        pass_rows = remote(g_out, g_in, gs_s.at[0], gs_r.at[0], mate)
+        pass_rows.start()
+        edge = through(parity * local, x_v, store_own)
+        order = (edge[0], edges12[0:1, :], edges12[2:3, :], edges3[0:1, :])
+        order += (edge[1], edges12[1:2, :], edges12[3:4, :], edges3[1:2, :])
+        for i, value in enumerate(order):
+            run[0, i : i + 1, :] = value
+        double_start(0)
+        tick(5)
+        pending = 0
+        t = 6
+        while pending < len(steps):
+            for _ in range(2):
+                if pending < len(steps):
+                    double_end(pending)
+                    pending += 1
+                    if pending < len(steps):
+                        double_start(pending)
+            tick(t)
+            t += 1
+        last = pltpu.make_async_copy(run.at[len(steps)], sums, load.at[24])
+        last.start()
+
+        pass_rows.wait_recv()
+        for i in range(2):
+            back_pad = remote(gp_out, gp_in.at[i], gp_s.at[i], gp_r.at[i], peer("seq", 2 + i))
+
+            @pl.when(s < 2)
+            def _():
+                back_pad.wait_recv()
+
+            @pl.when(s >= 2)
+            def _():
+                back_pad.wait_send()
+
+        @pl.when(s < 2)
+        def _():
+            row = lax.broadcasted_iota(jnp.int32, (BLK, 1), 0)
+            mine = ((s == 0) & (row < info[7])) | ((s == 1) & (row >= info[8]))
+            extra = jnp.where(mine, gp_in[0].astype(F32) + gp_in[1].astype(F32), 0.0)
+            at = pl.ds(pl.multiple_of(jnp.where(s == 0, 0, local - BLK), 128), BLK)
+            own[at, :] += extra
+
+        def finish(i, carry):
+            at = pl.ds(pl.multiple_of(i * 128, 128), 128)
+            hat, rstd = normalise(x_v[at, :].astype(F32))
+            g = own[at, :] + g_in[at, :].astype(F32)
+            out_v[at, :] = (mid_v[at, :] + norm_back(g, hat, rstd, gain)).astype(BF16)
+            return carry
+
+        lax.fori_loop(0, local // 128, finish, 0)
+        leave = pltpu.make_async_copy(out_v, grad_in, load.at[25])
+        leave.start()
+        end = a.count + b.count + 5
+        while t <= end:
+            tick(t)
+            t += 1
+        for u in range(b.count):
+            seven(u).wait()
+        pass_rows.wait_send()
+        last.wait()
+        leave.wait()
+
+    dt = lambda s, t=BF16: pltpu.VMEM(s, t)
+    pl.run_scoped(
+        feed_phase,
+        dt((PIECES, fsdp, rows, local)),
+        dt((PIECES, local, d)),
+        dt((local, d)),
+        dt((d, local)),
+        dt((local, d)),
+        dt((local, d)),
+    )
+    pl.run_scoped(
+        attention_phase,
+        dt(q.shape), dt(k.shape), dt(v.shape), dt(mixed.shape), dt(kp.shape), dt(vp.shape), dt(lse.shape, F32),
+    )
+    pl.run_scoped(
+        project_phase,
+        dt(w.shape), dt(n_t.shape), dt(np_t.shape), dt(tokens.shape), dt(theirs.shape), dt(padx.shape),
+        dt(g_mid.shape, F32), dt((local, d), F32), dt((local, d)),
+    )
+    give.wait_send()
+    for u in range(2 * PIECES - 3, 2 * PIECES + 1):
+        a.core(u, ring.at[u % 4]).wait_send()
+    for u in range(b.count):
+        b.core(u, ring_b.at[u]).wait_send()
+    for lane in (a, b):
+        for u in range(lane.count):
+            lane.drain(u)
+    for i in range(len(steps)):
+        double(i).wait_send()
+
+
+def rear(info, arrays, small, sizes):
+    fsdp, dp, seq = sizes
+    local, half = arrays[1].shape
+    d = 2 * half
+    rows, y = d // fsdp, fsdp // 2
+    n = 2 * PIECES + 1
+    steps = len(doublings(fsdp, dp, seq))
+    dma = pltpu.SemaphoreType.DMA
+    vm = pltpu.VMEM
     return pl.pallas_call(
-        functools.partial(reduce_body, fsdp=fsdp, dp=dp, layout=layout),
-        in_specs=[hbm()] * (2 * len(pairs)),
-        out_specs=[hbm(), hbm()],
-        out_shape=[shape((n_a, rows, d), BF16), shape((3, rows, wide), BF16)],
-        scratch_shapes=[
-            pltpu.VMEM((n_a, y, rows, d), BF16),
-            pltpu.VMEM((3, y, rows, wide), BF16),
-            pltpu.SemaphoreType.DMA((n_a,)),
-            pltpu.SemaphoreType.DMA((3,)),
-        ]
-        + Lane.scratch(n_a, rows, d, fsdp, dp, (1, 2, 3))
-        + Lane.scratch(3, rows, wide, fsdp, dp, (2,)),
+        functools.partial(rear_body, fsdp=fsdp, dp=dp, seq=seq),
+        in_specs=[pl.BlockSpec(memory_space=pltpu.SMEM)]
+        + [hbm()] * len(arrays)
+        + [pl.BlockSpec(memory_space=pltpu.VMEM)] * len(small),
+        out_specs=[hbm()] * 4,
+        out_shape=[
+            shape((n, rows, d), BF16),
+            shape((2, 3, rows, half), BF16),
+            shape((local, d), BF16),
+            shape((8, d), F32),
+        ],
+        scratch_shapes=Lane.scratch(n, rows, d, fsdp, dp, (1, 2, 3))
+        + Lane.scratch(3, rows, half, fsdp, dp, (2,))
+        + [vm((4, y, rows, d), BF16), vm((3, y, rows, half), BF16)]
+        + [vm((2 * local, half), BF16)] * 4
+        + [vm((BLK, half), BF16)] * 2
+        + [vm((2 * local, 2 * HD), F32)] * 2
+        + [vm((BLK, 2 * HD), F32)] * 2
+        + [vm((local, d), BF16)] * 2
+        + [vm((BLK, d), BF16), vm((2, BLK, d), BF16), vm((steps + 1, 8, d), F32), vm((steps, 8, d), F32)]
+        + [dma((26,)), dma((1,)), dma((1,)), dma((1,)), dma((1,)), dma((2,)), dma((2,))]
+        + [dma((steps,)), dma((steps,)), dma((3,)), dma((3,))],
         compiler_params=pltpu.CompilerParams(vmem_limit_bytes=VMEM_LIMIT, collective_id=0, has_side_effects=True),
-        cost_estimate=pl.CostEstimate(flops=10**8, bytes_accessed=5 * 10**8, transcendentals=0),
-    )(*[k for k, _ in pairs], *[s for _, s in pairs])
-
-
-def hop(value, axis, mask):
-    return lax.ppermute(value, axis, [(i, i ^ mask) for i in range(lax.axis_size(axis))])
-
-
-def arrange(pieces, index):
-    count = len(pieces)
-    if count == 1:
-        return list(pieces)
-    half = count // 2
-    low, high = arrange(pieces[:half], index), arrange(pieces[half:], index)
-    bit = (index & half) != 0
-    return [jnp.where(bit, b, a) for a, b in zip(low, high)] + [jnp.where(bit, a, b) for a, b in zip(low, high)]
-
-
-def sum_all(value):
-    for axis in ("fsdp", "dp", "seq"):
-        m = 1
-        while m < lax.axis_size(axis):
-            value = value + hop(value, axis, m)
-            m *= 2
-    return value
+        cost_estimate=pl.CostEstimate(flops=10**10, bytes_accessed=10**8, transcendentals=0),
+    )(info, *arrays, *small)
 
 
 def local(
@@ -1215,49 +1357,25 @@
     (out, g_feed, act_t, slope, two_t, branch, middle, edges3) = forward(
         info, mixed, other, x_tok, up, norm_gain, norm_bias, wo, wu, wd
     )
-    keeps, g_twos = [], []
-    for g in range(GROUPS):
-        keep, send, g_two = back_group(info, g, g_feed, two_t, act_t, slope, wd, wu, fsdp)
-        keeps.append((keep, send))
-        g_twos.append(g_two)
-    g_mid, d_own, d_send, keep_o, send_o, edges12 = middle_back(
-        info, g_twos[0], g_twos[1], middle, branch, up, norm_gain, wo, mixed, half, other, fsdp
+    hid, g_two = back(info, g_feed, slope, wd, wu, fsdp)
+    g_mid, d_own, d_send, gbr, edges12 = middle_back(info, g_two, middle, branch, up, norm_gain, wo)
+    rows = d // fsdp
+    done, done_q, grad_in, sums = rear(
+        info,
+        (
+            d_send, d_own, act_t.reshape(fsdp, PIECES, rows, local_rows), hid, g_feed, two_t,
+            mixed.reshape(2, local_rows, half), other, gbr, q, k, v, mixed, kp, vp, lse,
+            w_qkv, n_t, np_t, x_tok, theirs, pads, g_mid,
+        ),
+        (norm_gain, edges3, edges12),
+        (fsdp, dp, lax.axis_size("seq")),
     )
-    d_other = hop(d_send, "seq", 1)
-    dq, dk, dv, dkp, dvp = attend_back(info, q, k, v, kp, vp, mixed, lse, d_own, d_other)
-    g_own, g_send, g_pad, keep_q, send_q, edges0 = project_back(
-        info, x_tok, theirs, pads, norm_gain, dq, dk, dv, dkp, dvp, w_qkv, n_t, np_t, fsdp
-    )
-    g_other = hop(g_send, "seq", 1)
-    back_a = lax.ppermute(g_pad, "seq", [(2, 0), (3, 1)])
-    back_b = lax.ppermute(g_pad, "seq", [(2, 1), (3, 0)])
-    grad_in = finish(info, x_tok, g_own, g_other, back_a, back_b, g_mid, norm_gain)
-
-    sums = sum_all(
-        jnp.stack(
-            [edges0[0], edges12[0], edges12[2], edges3[0], edges0[1], edges12[1], edges12[3], edges3[1]]
-        )
-    )
-
-    done, done_q = reduce_all(keeps + [(keep_o, send_o), (keep_q, send_q)], fsdp, dp)
-    rows = d // fsdp
-    per = (done.shape[0] - 1) // GROUPS
-    reduced = [done[g * per : (g + 1) * per].reshape(per * rows, d) for g in range(GROUPS)]
+    grad_qkv = jnp.concatenate([done_q[h, c] for c in range(3) for h in range(2)], axis=1).astype(F32)
     grad_proj = done[-1].astype(F32)
-    half_q = jnp.concatenate([done_q[0], done_q[1], done_q[2]], axis=1)
-    both = arrange([half_q, hop(half_q, "seq", 1)], parity)
-    grad_qkv = jnp.concatenate(
-        [both[h][:, c * half : (c + 1) * half] for c in range(3) for h in range(2)], axis=1
+    grad_down = jnp.concatenate([done[2 * c] for c in range(PIECES)], axis=0).astype(F32)
+    grad_up = jnp.concatenate(
+        [done[2 * c + 1][:, h * rows : (h + 1) * rows] for h in range(fsdp) for c in range(PIECES)], axis=1
     ).astype(F32)
-    tile = ff // fsdp // GROUPS
-    grad_down = jnp.concatenate([r[:tile] for r in reduced], axis=0).astype(F32)
-    piece = d // fsdp
-    blocks = []
-    for h in range(fsdp):
-        for r in reduced:
-            for c in range(tile // piece):
-                blocks.append(r[tile + c * rows : tile + (c + 1) * rows, h * piece : (h + 1) * piece])
-    grad_up = jnp.concatenate(blocks, axis=1).astype(F32)
     return (out[None], grad_in[None], grad_qkv, grad_proj, grad_up, grad_down, sums[0:4], sums[4:8])
 
 

time: 540 us -> 436 us (0.81)
  waiting for transfers between devices: 53.2 us -> 0 us
  Pallas kernels: 437 us -> 401 us
  starting transfers between devices: 8.5 us -> 0 us
  local copies, waits for them, and re-layouts: 22.1 us -> 16.6 us
    ppermute x10 -> x0, waiting for transfers between devices: 53.2 us -> none  [the longest x8 53.2 us: hop(): lax.ppermute(value, axis, [(i, i ^ mask) for i in range(lax.axis_size(axi...]
    pallas_call x7 -> x3, Pallas kernels: 314 us -> 279 us  [the longest x1 248 us: rear(): pl.pallas_call(functools.partial(rear_body, fsdp=fsdp, dp=dp, seq=seq), i...]
    ppermute x10 -> x0, starting transfers between devices: 8.5 us -> none  [the longest x8 5.92 us: hop(): lax.ppermute(value, axis, [(i, i ^ mask) for i in range(lax.axis_size(axi...]
    slice x4 -> x0, local copies, waits for them, and re-layouts: 5.48 us -> none  [the longest x1 2.77 us: local(): grad_down = jnp.concatenate([r[:tile] for r in reduced], axis=0).astype(F32)]
  transfers between devices with their start and end apart: 10 -> 0, of which waited for: 4 -> 0; matrix products, arithmetic and copies ran while one was open for 5% -> 0% of each run, Pallas kernels for 34% -> 0%
where the time goes in v4:
time: 436 us; the launch traced here: 432 us
  Pallas kernels  401 us (92%)
  local copies, waits for them, and re-layouts  16.6 us (4%)
  other arithmetic  8.75 us (2%)
  between operations  5.65 us (1%)
    pallas_call x1, Pallas kernels, rear(): pl.pallas_call(functools.partial(rear_body, fsdp=fsdp, dp=dp, seq=seq), i...  248 us
    pallas_call x1, Pallas kernels, front(): pl.pallas_call(functools.partial(front_body, fsdp=fsdp, dp=dp), in_specs=...  88.9 us
    pallas_call x1, Pallas kernels, forward(): call(forward_body, (ff // tile,), 1, [pl.BlockSpec((local, half), lambda...  33.9 us
    pallas_call x1, Pallas kernels, back(): call(back_body, (fsdp,), 1, [full((local, d)), pl.BlockSpec((local, tile)...  18.8 us
    pallas_call x1, Pallas kernels, middle_back(): call(middle_body, (local // rows,), 1, [block, block, block, block, full(...  11.9 us

profile of v4, /device:TPU:0, one launch (start us, length us, event | category | flops | bytes accessed | tf_op | source)
XLA Modules:
  0.0 432.2 jit_solution(5189979023862420559)
XLA Ops:
  0.7 1.3 fusion.1
  3.3 1.3 fusion.2
  7.8 1.2 stack.35.info
  9.1 1.3 slice.147.bias
  10.4 1.3 slice.146.gain
  11.7 88.9 %shard_map.161 = (bf16[1280,512]{1,0:T(8,128)(2,1)}, bf16[1280,512]{1,0:T(8,128)(2,1)}, bf16[1280,512]{1,0:T(8,128)(2,1)}, bf16[1024,1280]{1,0:T(8,128)(2,1)}, b...) custom-call(s32[9]{0:T(128)} %stack.35.info, ...), custom_call_target="tpu_custom_call" | custom-call | flops 10000000000 | bytes 100000000 | tf_op jit(solution)/shard_map/pallas_call | solution.py:558
  100.6 33.9 %shard_map.162 = (bf16[640,1024]{1,0:T(8,128)(2,1)}, bf16[640,1024]{1,0:T(8,128)(2,1)}, bf16[4096,640]{1,0:T(8,128)(2,1)}, bf16[640,4096]{1,0:T(8,128)(2,1)}, bf...) custom-call(s32[9]{0:T(128)} %stack.35.info, ...), custom_call_target="tpu_custom_call" | custom-call | flops 12079595520 | bytes 40000000 | tf_op jit(solution)/shard_map/pallas_call | solution.py:633
  134.4 18.8 %shard_map.163 = (bf16[4,640,1024]{2,1,0:T(8,128)(2,1)}, f32[640,1024]{1,0:T(8,128)}) custom-call(s32[9]{0:T(128)} %stack.35.info, bf16[640,1024]{1,0:T(8,128)(2,1)} %get-tuple-element.49.g_feed, bf16[640,4096]{1,0:T(8,128)(2,1)} %get-tuple-element.50.slope, bf16[4096,1024]{1,0:T(8,128)(2,1)} %get-tuple-element.47.wd, bf16[1024,4096]{1,0:T(8,128)(2,1)} %get-tuple-element.46.wu), custom_call_target="tpu_custom_call" | custom-call | flops 10737418240 | bytes 35000000 | tf_op jit(solution)/shard_map/pallas_call | solution.py:695
  153.3 11.9 %shard_map.164 = (f32[640,1024]{1,0:T(8,128)}, bf16[640,512]{1,0:T(8,128)(2,1)}, bf16[640,512]{1,0:T(8,128)(2,1)}, bf16[640,1024]{1,0:T(8,128)(2,1)}, f32[4,1024]{1,0:T(4,128)}) custom-call(s32[9]{0:T(128)} %stack.35.info, f32[640,1024]{1,0:T(8,128)} %get-tuple-element.51.g, f32[640,1024]{1,0:T(8,128)} %get-tuple-element.52.middle, ...), custom_call_target="tpu_custom_call" | custom-call | flops 1342177280 | bytes 18000000 | tf_op jit(solution)/shard_map/pallas_call | solution.py:744
  165.2 247.8 %shard_map.165 = (bf16[9,256,1024]{2,1,0:T(8,128)(2,1)}, bf16[2,3,256,512]{3,2,1,0:T(8,128)(2,1)}, bf16[640,1024]{1,0:T(8,128)(2,1)}, f32[8,1024]{1,0:T(8,128)}) custom-call(s32[9]{0:T(128)} %stack.35.info, bf16[640,512]{1,0:T(8,128)(2,1)} %get-tuple-element.54.d_send, bf16[640,512]{1,0:T(8,128)(2,1)} %get-tuple-element.55.d_own, ...), custom_call_target="tpu_custom_call" | custom-call | flops 10000000000 | bytes 100000000 | tf_op jit(solution)/shard_map/pallas_call | solution.py:1306
  413.0 1.5 fusion
  414.4 1.0 bitcast_dynamic-update-slice_fusion.5
  415.4 1.0 bitcast_dynamic-update-slice_fusion.4
  416.4 1.0 bitcast_dynamic-update-slice_fusion.3
  417.4 1.0 bitcast_dynamic-update-slice_fusion.2
  418.4 1.0 bitcast_dynamic-update-slice_fusion.1
  419.3 1.0 bitcast_dynamic-update-slice_fusion
  420.3 0.0 copy-start
  420.3 2.0 convert_element_type.15
  422.4 1.4 copy-done
  423.8 1.7 slice_bitcast_fusion.3
  425.5 2.5 maximum_convert_fusion
  428.4 0.0 copy-start.1
  428.5 2.5 convert_element_type.18
  431.0 0.0 copy-done.1
  431.0 1.1 copy.39
  (16 shorter events, 0.3 us)
Async XLA Ops:
  420.3 3.5 copy-start
  428.4 2.5 copy-start.1

commit v5 on v4

v5 whole, which is shorter than its diff:
```python
import functools

import jax
import jax.numpy as jnp
from jax import lax
from jax.experimental import pallas as pl
from jax.experimental.pallas import tpu as pltpu
from jax.sharding import PartitionSpec as P

HD = 64
IMAGE = 1024
SLOT = 1280
BLK = 256
LOG2E = 1.4426950408889634
SCALE = LOG2E / 8.0
NEG = -1e30
F32 = jnp.float32
BF16 = jnp.bfloat16
VMEM_LIMIT = 60 * 1024 * 1024
PIECES = 4


def nn(a, b):
    return lax.dot_general(a, b, (((1,), (0,)), ((), ())), preferred_element_type=F32)


def nt(a, b):
    return lax.dot_general(a, b, (((1,), (1,)), ((), ())), preferred_element_type=F32)


def tn(a, b):
    return lax.dot_general(a, b, (((0,), (0,)), ((), ())), preferred_element_type=F32)


def normalise(v):
    mean = jnp.mean(v, axis=-1, keepdims=True)
    centred = v - mean
    var = jnp.mean(centred * centred, axis=-1, keepdims=True)
    rstd = lax.rsqrt(var + 1e-05)
    return centred * rstd, rstd


def norm_back(g, hat, rstd, gain):
    gg = g * gain
    return rstd * (
        gg - jnp.mean(gg, axis=-1, keepdims=True) - hat * jnp.mean(gg * hat, axis=-1, keepdims=True)
    )


def call(body, grid, prefetch, in_specs, out_specs, out_shape, scratch=(), flops=0, moved=0):
    return pl.pallas_call(
        body,
        grid_spec=pltpu.PrefetchScalarGridSpec(
            num_scalar_prefetch=prefetch,
            grid=grid,
            in_specs=in_specs,
            out_specs=out_specs,
            scratch_shapes=list(scratch),
        ),
        out_shape=out_shape,
        compiler_params=pltpu.CompilerParams(vmem_limit_bytes=VMEM_LIMIT),
        cost_estimate=pl.CostEstimate(flops=int(flops), bytes_accessed=int(moved), transcendentals=0),
    )


def full(shape):
    zeros = (0,) * len(shape)
    return pl.BlockSpec(shape, lambda *_: zeros)


def hbm():
    return pl.BlockSpec(memory_space=pl.ANY)


def shape(dims, dtype):
    return jax.ShapeDtypeStruct(dims, dtype)


def attend_pair(bounds, q, k, v, kp, vp, o, lse):
    start, stop, pad_a, pad_b = bounds
    lane = lax.broadcasted_iota(jnp.int32, (1, 2 * HD), 1)
    row = lax.broadcasted_iota(jnp.int32, (BLK, 1), 0)
    col = lax.broadcasted_iota(jnp.int32, (1, BLK), 1)
    causal = col <= row
    pad_col = (col < pad_a) | (col >= pad_b)
    count = SLOT // BLK
    for i in range(count):
        n = (i + 1) * BLK
        qi = q(slice(i * BLK, n))
        edge = i in (0, count - 1)
        pos_q = row + i * BLK
        in_q = (pos_q >= start) & (pos_q < stop)
        masks = []
        for j in range(i + 1):
            pos_k = col + j * BLK
            mask = None
            if edge:
                in_k = (pos_k >= start) & (pos_k < stop)
                mask = (in_q & in_k) | (~in_q & ~in_k)
            elif j == 0:
                mask = jnp.broadcast_to(pos_k >= start, (BLK, BLK))
            if j == i:
                mask = causal if mask is None else mask & causal
            masks.append(mask)
        outs = []
        for h in range(2):
            qh = jnp.where(lane // HD == h, qi, jnp.zeros_like(qi))
            blocks = []
            for j in range(i + 1):
                s = nt(qh, k(slice(j * BLK, (j + 1) * BLK))) * SCALE
                if masks[j] is not None:
                    s = jnp.where(masks[j], s, NEG)
                blocks.append(s)
            if edge:
                s = nt(qh, kp(slice(None))) * SCALE
                blocks.append(jnp.where(~in_q & pad_col, s, NEG))
            top = functools.reduce(jnp.maximum, blocks)
            top = jnp.max(top, axis=1, keepdims=True)
            probs = [jnp.exp2(s - top) for s in blocks]
            total = jnp.sum(functools.reduce(jnp.add, probs), axis=1, keepdims=True)
            probs = [x.astype(BF16) for x in probs]
            mixed = nn(jnp.concatenate(probs[: i + 1], axis=1), v(slice(0, n)))
            if edge:
                mixed = mixed + nn(probs[-1], vp(slice(None)))
            outs.append(mixed * (1.0 / total))
            level = jnp.broadcast_to(top + jnp.log2(total), (BLK, 128))
            lse(h, slice(i * BLK, n), level.T[0:1, :])
        o(slice(i * BLK, n), jnp.where(lane < HD, outs[0], outs[1]).astype(BF16))


def split_heads(x):
    lane = lax.broadcasted_iota(jnp.int32, (1, 2 * HD), 1)
    zero = jnp.zeros_like(x)
    return [jnp.where(lane // HD == h, x, zero) for h in range(2)]


def back_block(i, q, o, lse, do):
    pick = (
        lax.broadcasted_iota(jnp.int32, (8, 2 * HD), 1) // HD
        == lax.broadcasted_iota(jnp.int32, (8, 2 * HD), 0)
    ).astype(F32)
    rows = slice(i * BLK, (i + 1) * BLK)
    do_i = do(rows)
    qs = jnp.concatenate(split_heads(q(rows)), axis=0)
    ds = jnp.concatenate(split_heads(do_i), axis=0)
    level = jnp.concatenate([lse(0, rows), lse(1, rows)], axis=1)
    inner = lax.dot_general(
        pick,
        do_i.astype(F32) * o(rows).astype(F32),
        (((1,), (1,)), ((), ())),
        precision=lax.Precision.HIGHEST,
        preferred_element_type=F32,
    )
    inner = jnp.concatenate([inner[0:1, :], inner[1:2, :]], axis=1)

    def block(kj, vj, mask):
        s = nt(kj, qs) * SCALE - level
        if mask is not None:
            s = jnp.where(mask, s, NEG)
        p = jnp.exp2(s)
        g = p * (nt(vj, ds) - inner)
        p, g = p.astype(BF16), g.astype(BF16)
        halves = split_heads(kj)
        part = tn(g[:, :BLK], halves[0]) + tn(g[:, BLK:], halves[1])
        return nn(g, qs), nn(p, ds), part

    pos_q = lax.broadcasted_iota(jnp.int32, (1, 2 * BLK), 1) % BLK + i * BLK
    return block, pos_q


def attend_back_pads(bounds, q, kp, vp, o, lse, do, dq_pad):
    start, stop, pad_a, pad_b = bounds
    row = lax.broadcasted_iota(jnp.int32, (BLK, 1), 0)
    pad_row = (row < pad_a) | (row >= pad_b)
    gk = gv = 0.0
    for n, i in enumerate((0, SLOT // BLK - 1)):
        block, pos_q = back_block(i, q, o, lse, do)
        one, two, part = block(kp, vp, ~((pos_q >= start) & (pos_q < stop)) & pad_row)
        gk, gv = gk + one, gv + two
        dq_pad(n, part)
    return gk, gv


def attend_back_pair(bounds, q, k, v, o, lse, do, dq_pad, dq, dk_sum, dv_sum):
    start, stop = bounds[:2]
    row = lax.broadcasted_iota(jnp.int32, (BLK, 1), 0)
    causal = row <= lax.broadcasted_iota(jnp.int32, (1, 2 * BLK), 1) % BLK
    dk_sum[...] = jnp.zeros_like(dk_sum)
    dv_sum[...] = jnp.zeros_like(dv_sum)
    count = SLOT // BLK
    for i in range(count):
        block, pos_q = back_block(i, q, o, lse, do)
        edge = i in (0, count - 1)
        in_q = (pos_q >= start) & (pos_q < stop)
        dq_sum = dq_pad(0 if i == 0 else 1) if edge else jnp.zeros((BLK, 2 * HD), F32)
        for j in range(i + 1):
            keys = slice(j * BLK, (j + 1) * BLK)
            pos_k = row + j * BLK
            mask = None
            if edge:
                in_k = (pos_k >= start) & (pos_k < stop)
                mask = (in_q & in_k) | (~in_q & ~in_k)
            elif j == 0:
                mask = jnp.broadcast_to(pos_k >= start, (BLK, 2 * BLK))
            if j == i:
                mask = causal if mask is None else mask & causal
            gk, gv, part = block(k(keys), v(keys), mask)
            dk_sum[keys, :] += gk
            dv_sum[keys, :] += gv
            dq_sum = dq_sum + part
        dq(slice(i * BLK, (i + 1) * BLK), (dq_sum * 0.125).astype(BF16))


def peer(axis, mask):
    return {axis: lax.axis_index(axis) ^ mask}


def greet(partners):
    barrier = pltpu.get_barrier_semaphore()
    for p in partners:
        pl.semaphore_signal(barrier, inc=1, device_id=p, device_id_type=pl.DeviceIdType.MESH)
    pl.semaphore_wait(barrier, len(partners))


def remote(src, dst, send, recv, to):
    return pltpu.make_async_remote_copy(
        src_ref=src, dst_ref=dst, send_sem=send, recv_sem=recv, device_id=to, device_id_type=pl.DeviceIdType.MESH
    )


def slot_bounds(caps, starts):
    s = lax.axis_index("seq")
    late = s >= 2
    start = jnp.where(late, starts[0, 1] - SLOT, starts[0, 0])
    stop = start + jnp.where(late, caps[0, 1], caps[0, 0]) + IMAGE
    pad_a = jnp.where(late, starts[0, 0], 0)
    pad_b = jnp.where(late, starts[0, 0] + caps[0, 0], BLK)
    return start, stop, pad_a, pad_b


def front_body(
    caps, starts, tokens, wqkv, wo, wu, wd, gains, biases,
    q_out, k_out, v_out, n_out, np_out, kp_out, vp_out, w_out, mix_out, own_out, lse_out, other, tok_out, pad_out, wo_all, wu_all, wd_all,
    mine, theirs, pads, made, w, normed, n_t, np_t, q, k, v, kp, vp, mixed, held_o, held_u, held_d, lse,
    tok_l, tok_s, tok_r, pad_s, pad_r, q_l, q_cs, q_cr, q_ys, q_yr, q_fs, q_fr,
    h_l, s_l, s_cs, s_cr, y_s, y_r, x_s, x_r, fy_s, fy_r, fx_s, fx_r, o_s, o_r, out_l,
    *, fsdp, dp
):
    f, x, s = lax.axis_index("fsdp"), lax.axis_index("dp"), lax.axis_index("seq")
    parity = s % 2
    local, d = tokens.shape
    half = d // 2
    ys = fsdp // 2
    bounds = slot_bounds(caps, starts)
    gain, bias = gains[0:1, :], biases[0:1, :]
    core, mate = peer("fsdp", 1), peer("seq", 1)
    greet(
        [core]
        + [peer("fsdp", 2 * r) for r in range(1, ys)]
        + [peer("dp", r) for r in range(1, dp)]
        + [mate, peer("seq", 3)]
    )

    cuts = ((0, BLK), (BLK, local - BLK))

    def token(i):
        at = pl.ds(*cuts[i])
        return remote(tokens.at[at], theirs.at[at], tok_s.at[i], tok_r.at[i], mate)

    load = pltpu.make_async_copy(tokens, mine, tok_l.at[0])
    load.start()
    token(0).start()
    token(1).start()

    rows = wqkv.shape[0]

    def band(r):
        return pl.ds(pl.multiple_of((f ^ r) * rows, 16), rows)

    def source(c):
        return wqkv.at[:, pl.ds(pl.multiple_of(c * d + parity * half, 128), half)]

    def cols(c):
        return pl.ds(c * half, half)

    def q_local(c):
        return pltpu.make_async_copy(source(c), w.at[band(0), cols(c)], q_l.at[c])

    def q_core(c):
        return remote(source(c), w.at[band(0), cols(c)], q_cs.at[c], q_cr.at[c], core)

    def q_y(c, r):
        at = (c, r - 1)
        return remote(source(c), w.at[band(0), cols(c)], q_ys.at[at], q_yr.at[at], peer("fsdp", 2 * r))

    def q_far(c, r):
        at = (c, r - 1)
        here = w.at[band(2 * r), cols(c)]
        return remote(here, here, q_fs.at[at], q_fr.at[at], core)

    for c in range(3):
        for r in range(1, ys):
            q_y(c, r).start()
        q_core(c).start()
        q_local(c).start()

    shards, wholes = (held_o, held_u, held_d), (wo_all, wu_all, wd_all)

    def hold(i):
        return pltpu.make_async_copy((wo, wu, wd)[i], shards[i], h_l.at[i])

    def whole_shard(i):
        n = shards[i].shape[0]
        return wholes[i].at[pl.ds(pl.multiple_of(f * n, 16), n)]

    def s_local(i):
        return pltpu.make_async_copy(shards[i], whole_shard(i), s_l.at[i])

    def s_core(i):
        return remote(shards[i], whole_shard(i), s_cs.at[i], s_cr.at[i], core)

    units = [(0, 0)] + [(1, j) for j in range(4)] + [(2, j) for j in range(4)]

    def piece(u, owner, part, shard=False):
        which, j = units[u]
        n = shards[which].shape[0]
        sub = n // dp
        base = part * sub if shard else owner * n + part * sub
        ref = shards[which] if shard else wholes[which]
        if which == 0:
            return ref.at[pl.ds(pl.multiple_of(base, 16), sub)]
        if which == 1:
            wide = ref.shape[1] // 4
            return ref.at[pl.ds(pl.multiple_of(base, 16), sub), pl.ds(j * wide, wide)]
        return ref.at[pl.ds(pl.multiple_of(base + j * (sub // 4), 16), sub // 4)]

    def w_y(u, r):
        at = (u, r - 1)
        return remote(piece(u, f, x, True), piece(u, f, x), y_s.at[at], y_r.at[at], peer("fsdp", 2 * r))

    def w_x(u, r, t):
        at = (u, r - 1, t - 1)
        here = piece(u, f ^ (2 * r), x)
        return remote(here, here, x_s.at[at], x_r.at[at], peer("dp", t))

    def w_fy(u, r):
        at = (u, r - 1)
        here = piece(u, f ^ (2 * r), x)
        return remote(here, here, fy_s.at[at], fy_r.at[at], core)

    def w_fx(u, r, t):
        at = (u, r - 1, t - 1)
        here = piece(u, f ^ (2 * r), x ^ t)
        return remote(here, here, fx_s.at[at], fx_r.at[at], core)

    def issue(u):
        if u < len(units):
            for r in range(1, ys):
                w_y(u, r).start()

    def came_y(u):
        for r in range(1, ys):
            w_y(u, r).wait_recv()
        issue(u + 3)
        for r in range(1, ys):
            for t in range(1, dp):
                w_x(u, r, t).start()
            w_fy(u, r).start()

    def came_x(u):
        for r in range(1, ys):
            for t in range(1, dp):
                w_x(u, r, t).wait_recv()
                w_fx(u, r, t).start()

    def normalise_rows(src, at, count):
        def body(i, carry):
            here = pl.ds(pl.multiple_of(i * 128, 128), 128)
            there = pl.ds(pl.multiple_of(at + i * 128, 128), 128)
            hat, _ = normalise(src[here, :].astype(F32))
            value = (hat * gain + bias).astype(BF16)
            normed[there, :] = value
            n_t[:, there] = value.T
            return carry

        lax.fori_loop(count[0], count[1], body, 0)

    def project(at, c):
        here = pl.ds(pl.multiple_of(at, 128), local)
        (q, k, v)[c][here, :] = nn(normed[here, :], w[:, c * half : (c + 1) * half]).astype(BF16)

    for i in range(3):
        hold(i).start()
    load.wait()
    normalise_rows(mine, parity * local, (0, local // 128))
    for c in range(3):
        q_local(c).wait()
        q_core(c).wait_recv()
        for r in range(1, ys):
            q_y(c, r).wait_recv()
            q_far(c, r).start()
        if c == 0:
            for i in range(3):
                hold(i).wait()
            issue(0)
            for i in range(3):
                s_local(i).start()
                s_core(i).start()
        elif c == 1:
            issue(1)
        else:
            issue(2)
        for r in range(1, ys):
            q_far(c, r).wait_recv()
        if c == 0:
            token(0).wait_recv()
            index = lax.broadcasted_iota(jnp.int32, (BLK, 1), 0)
            made[...] = jnp.where(
                index < starts[0, 0], theirs[0:BLK, :].astype(F32), mine[local - BLK : local, :].astype(F32)
            ).astype(BF16)

            @pl.when(s < 2)
            def _():
                pads[...] = made[...]

        project(parity * local, c)
        if c == 0:

            @pl.when(s == 1)
            def _():
                remote(made, pads, pad_s.at[0], pad_r.at[0], peer("seq", 3)).start()

    w_store = pltpu.make_async_copy(w, w_out, out_l.at[0])
    w_store.start()
    forward_pads = remote(pads, pads, pad_s.at[1], pad_r.at[1], mate)

    @pl.when(s == 2)
    def _():
        remote(made, pads, pad_s.at[0], pad_r.at[0], peer("seq", 3)).wait_recv()
        forward_pads.start()

    away = (1 - parity) * local
    normalise_rows(theirs, away, (0, BLK // 128))
    came_y(0)
    token(1).wait_recv()
    normalise_rows(theirs, away, (BLK // 128, local // 128))
    for c in range(3):
        project(away, c)
    stores = [
        pltpu.make_async_copy(a, b, out_l.at[1 + i])
        for i, (a, b) in enumerate(((q, q_out), (k, k_out), (v, v_out), (n_t, n_out), (theirs, tok_out)))
    ]
    for copy in stores:
        copy.start()
    came_y(1)
    came_x(0)

    @pl.when(s == 3)
    def _():
        forward_pads.wait_recv()

    hat, _ = normalise(pads[...].astype(F32))
    value = (hat * gain + bias).astype(BF16)
    np_t[...] = value.T
    kp[...] = nn(value, w[:, half : 2 * half]).astype(BF16)
    vp[...] = nn(value, w[:, 2 * half :]).astype(BF16)
    late = [
        pltpu.make_async_copy(a, b, out_l.at[6 + i])
        for i, (a, b) in enumerate(((np_t, np_out), (kp, kp_out), (vp, vp_out), (pads, pad_out)))
    ]
    for copy in late:
        copy.start()
    came_y(2)
    came_x(1)

    def give(i):
        lanes = pl.ds(pl.multiple_of(i * 2 * HD, 128), 2 * HD)
        return remote(
            mixed.at[pl.ds(pl.multiple_of(away, 16), local), lanes], other.at[:, lanes], o_s.at[i], o_r.at[i], mate
        )

    pairs = half // (2 * HD)
    done_y, done_x = 3, 2
    for i in range(pairs):
        lanes = slice(i * 2 * HD, (i + 1) * 2 * HD)

        def put(at, value):
            mixed[at, lanes] = value

        def put_lse(h, at, value):
            lse[i, h : h + 1, at] = value

        attend_pair(
            bounds,
            lambda at: q[at, lanes],
            lambda at: k[at, lanes],
            lambda at: v[at, lanes],
            lambda at: kp[at, lanes],
            lambda at: vp[at, lanes],
            put,
            put_lse,
        )
        give(i).start()
        came_y(done_y)
        came_x(done_x)
        done_y, done_x = done_y + 1, done_x + 1
    last = [
        pltpu.make_async_copy(mixed, mix_out, out_l.at[10]),
        pltpu.make_async_copy(lse, lse_out, out_l.at[11]),
        pltpu.make_async_copy(
            mixed.at[pl.ds(pl.multiple_of(parity * local, 16), local)], own_out, out_l.at[12]
        ),
    ]
    for copy in last:
        copy.start()
    for u in range(done_y, len(units)):
        came_y(u)
        came_x(u - 1)
    came_x(len(units) - 1)

    for i in range(pairs):
        give(i).wait()
    for i in range(3):
        s_local(i).wait()
        s_core(i).wait()
    for u in range(len(units)):
        for r in range(1, ys):
            w_y(u, r).wait_send()
            w_fy(u, r).wait()
            for t in range(1, dp):
                w_x(u, r, t).wait_send()
                w_fx(u, r, t).wait()
    for c in range(3):
        q_core(c).wait_send()
        for r in range(1, ys):
            q_y(c, r).wait_send()
            q_far(c, r).wait_send()
    token(0).wait_send()
    token(1).wait_send()

    @pl.when(s == 1)
    def _():
        remote(made, pads, pad_s.at[0], pad_r.at[0], peer("seq", 3)).wait_send()

    @pl.when(s == 2)
    def _():
        forward_pads.wait_send()

    for copy in [w_store] + stores + late + last:
        copy.wait()


def front(caps, starts, tokens, wqkv, wo, wu, wd, gain, bias, fsdp, dp):
    local, d = tokens.shape
    half, ff = d // 2, wu.shape[1]
    pairs = half // (2 * HD)
    y, px, n = max(fsdp // 2 - 1, 1), max(dp - 1, 1), 9
    dma = pltpu.SemaphoreType.DMA
    outs = [((2 * local, half), BF16)] * 3 + [
        ((d, 2 * local), BF16),
        ((d, BLK), BF16),
        ((BLK, half), BF16),
        ((BLK, half), BF16),
        ((d, 3 * half), BF16),
        ((2 * local, half), BF16),
        ((local, half), BF16),
        ((pairs, 2, 2 * local), F32),
        ((local, half), BF16),
        ((local, d), BF16),
        ((BLK, d), BF16),
        ((d, d), BF16),
        ((d, ff), BF16),
        ((ff, d), BF16),
    ]
    buffers = [
        (local, d), (local, d), (BLK, d), (BLK, d), (d, 3 * half), (2 * local, d), (d, 2 * local), (d, BLK),
        (2 * local, half), (2 * local, half), (2 * local, half), (BLK, half), (BLK, half), (2 * local, half),
        wo.shape, wu.shape, wd.shape,
    ]
    sems = [(1,), (2,), (2,), (2,), (2,), (3,), (3,), (3,), (3, y), (3, y), (3, y), (3, y)]
    sems += [(3,)] * 4 + [(n, y)] * 2 + [(n, y, px)] * 2 + [(n, y)] * 2 + [(n, y, px)] * 2 + [(pairs,)] * 2 + [(13,)]
    return pl.pallas_call(
        functools.partial(front_body, fsdp=fsdp, dp=dp),
        in_specs=[pl.BlockSpec(memory_space=pltpu.SMEM)] * 2 + [hbm()] * 5 + [pl.BlockSpec(memory_space=pltpu.VMEM)] * 2,
        out_specs=[hbm()] * len(outs),
        out_shape=[shape(*o) for o in outs],
        scratch_shapes=[pltpu.VMEM(b, BF16) for b in buffers]
        + [pltpu.VMEM((pairs, 2, 2 * local), F32)]
        + [dma(s) for s in sems],
        compiler_params=pltpu.CompilerParams(vmem_limit_bytes=VMEM_LIMIT, collective_id=1, has_side_effects=True),
        cost_estimate=pl.CostEstimate(flops=10**10, bytes_accessed=10**8, transcendentals=0),
    )(caps, starts, tokens, wqkv, wo, wu, wd, gain, bias)


def forward_body(
    own, other, x, up, gains, biases, wo, wu, wd, out, g_feed, act_t, slope, n_t, branch, middle, edges, normed, feed
):
    parity = lax.axis_index("seq") % 2
    step, last = pl.program_id(0), pl.num_programs(0) - 1
    half = own.shape[1]
    blocks = x.shape[0] // 128

    @pl.when(step == 0)
    def _():
        w_own = wo[pl.ds(pl.multiple_of(parity * half, 128), half), :]
        w_other = wo[pl.ds(pl.multiple_of((1 - parity) * half, 128), half), :]
        branch[...] = nn(own[...], w_own) + nn(other[...], w_other)

        def rows(i, carry):
            at = pl.ds(pl.multiple_of(i * 128, 128), 128)
            hat, _ = normalise(branch[at, :])
            mid = x[at, :].astype(F32) + hat * gains[1:2, :] + biases[1:2, :]
            middle[at, :] = mid
            hat, _ = normalise(mid)
            two = (hat * gains[2:3, :] + biases[2:3, :]).astype(BF16)
            normed[at, :] = two
            n_t[:, at] = two.T
            return carry

        lax.fori_loop(0, blocks, rows, 0)
        feed[...] = jnp.zeros_like(feed)

    u = nn(normed[...], wu[...])
    th = jnp.tanh(0.7978845608 * (u + 0.044715 * (u * u * u)))
    act = (0.5 * u * (1.0 + th)).astype(BF16)
    slope[...] = (
        0.5 * (1.0 + th) + 0.5 * u * (1.0 - th * th) * (0.7978845608 + (3 * 0.044715 * 0.7978845608) * (u * u))
    ).astype(BF16)
    act_t[...] = act.T
    feed[...] += nn(act, wd[...])

    @pl.when(step == last)
    def _():
        def rows(i, carry):
            at = pl.ds(pl.multiple_of(i * 128, 128), 128)
            g = up[at, :].astype(F32)
            hat, rstd = normalise(feed[at, :])
            gain = gains[3:4, :]
            out[at, :] = (middle[at, :] + hat * gain + biases[3:4, :]).astype(BF16)
            g_feed[at, :] = norm_back(g, hat, rstd, gain).astype(BF16)
            return (
                carry[0] + jnp.sum(g * hat, axis=0, keepdims=True),
                carry[1] + jnp.sum(g, axis=0, keepdims=True),
            )

        zero = jnp.zeros((1, x.shape[1]), F32)
        a, b = lax.fori_loop(0, blocks, rows, (zero, zero))
        edges[0:1, :] = a
        edges[1:2, :] = b


def forward(mixed, other, x, up, gains, biases, wo, wu, wd):
    local, d = x.shape
    half, ff = mixed.shape[1], wu.shape[1]
    tile = 512
    once = lambda s: pl.BlockSpec(s, lambda *_: (0,) * len(s), pipeline_mode=pl.Buffered(1))
    return call(
        forward_body,
        (ff // tile,),
        0,
        [
            once(mixed.shape),
            once(other.shape),
            once(x.shape),
            once(up.shape),
            once(gains.shape),
            once(biases.shape),
            once(wo.shape),
            pl.BlockSpec((d, tile), lambda i: (0, i)),
            pl.BlockSpec((tile, d), lambda i: (i, 0)),
        ],
        [
            full((local, d)),
            full((local, d)),
            pl.BlockSpec((tile, local), lambda i: (i, 0)),
            pl.BlockSpec((local, tile), lambda i: (0, i)),
            full((d, local)),
            full((local, d)),
            full((local, d)),
            full((2, d)),
        ],
        [
            shape((local, d), BF16),
            shape((local, d), BF16),
            shape((ff, local), BF16),
            shape((local, ff), BF16),
            shape((d, local), BF16),
            shape((local, d), F32),
            shape((local, d), F32),
            shape((2, d), F32),
        ],
        [pltpu.VMEM((local, d), BF16), pltpu.VMEM((local, d), F32)],
        flops=2 * local * d * (d + 2 * ff),
        moved=40e6,
    )(mixed, other, x, up, gains, biases, wo, wu, wd)


class Lane:
    @staticmethod
    def scratch(count, rows, cols, fsdp, dp, masks):
        y, x, z = max(fsdp // 2 - 1, 1), max(dp - 1, 1), len(masks)
        dma = pltpu.SemaphoreType.DMA
        sems = [(count,)] * 2 + [(count, y)] * 2 + [(count, x)] * 2 + [(count, z)] * 4 + [(count, x)] * 2 + [(count,)] * 3
        return (
            [
                pltpu.VMEM((count, fsdp // 2, rows, cols), BF16),
                pltpu.VMEM((count, y, rows, cols), BF16),
                pltpu.VMEM((count, x, rows // dp, cols), BF16),
            ]
            + [pltpu.VMEM((count, rows // dp, cols >> (i + 1)), BF16) for i in range(z)]
            + [dma(s) for s in sems]
        )

    @staticmethod
    def size(masks):
        return 3 + len(masks) + 15

    def __init__(self, refs, final, fsdp, dp, masks, both=None):
        z = len(masks)
        self.acc, self.y_in, self.x_in = refs[:3]
        self.z_in = refs[3 : 3 + z]
        names = ("core_s", "core_r", "y_s", "y_r", "x_s", "x_r", "z_s", "z_r", "zz_s", "zz_r", "xx_s", "xx_r", "own")
        names += ("pair_s", "pair_r")
        self.both = both
        self.sems = dict(zip(names, refs[3 + z :]))
        self.final = final
        self.ys, self.dp, self.masks = fsdp // 2, dp, masks
        self.count, _, self.rows, self.cols = self.acc.shape
        self.x = lax.axis_index("dp")
        s = lax.axis_index("seq")
        self.bits = [s // m % 2 for m in masks]
        self.stages = [self.from_y, self.from_x]
        self.stages += [functools.partial(self.from_z, i) for i in range(z)]
        self.stages += [functools.partial(self.back_from_z, i) for i in reversed(range(z))]
        self.stages += [self.from_pair] if both is not None else []
        self.stages += [self.back_from_x]

    def place(self, level, away=False):
        at = 0
        for i in range(level):
            bit = self.bits[i]
            if away and i == level - 1:
                bit = 1 - bit
            at = at + bit * (self.cols >> (i + 1))
        if level == 0:
            return pl.ds(0, self.cols)
        return pl.ds(pl.multiple_of(at, 128), self.cols >> level)

    def band(self, mask=0):
        n = self.rows // self.dp
        return pl.ds(pl.multiple_of((self.x ^ mask) * n, 16), n)

    def core(self, u, src):
        return remote(src, self.acc.at[u], self.sems["core_s"].at[u], self.sems["core_r"].at[u], peer("fsdp", 1))

    def over_y(self, u, ry):
        s = self.sems
        return remote(
            self.acc.at[u, ry], self.y_in.at[u, ry - 1], s["y_s"].at[u, ry - 1], s["y_r"].at[u, ry - 1], peer("fsdp", 2 * ry)
        )

    def over_x(self, u, rx):
        s = self.sems
        return remote(
            self.acc.at[u, 0, self.band(rx)],
            self.x_in.at[u, rx - 1],
            s["x_s"].at[u, rx - 1],
            s["x_r"].at[u, rx - 1],
            peer("dp", rx),
        )

    def over_z(self, u, i):
        s = self.sems
        return remote(
            self.acc.at[u, 0, self.band(), self.place(i + 1, True)],
            self.z_in[i].at[u],
            s["z_s"].at[u, i],
            s["z_r"].at[u, i],
            peer("seq", self.masks[i]),
        )

    def back_z(self, u, i):
        s = self.sems
        at = self.final.at[u, self.band(), self.place(i + 1)]
        last = i == len(self.masks) - 1
        src = self.acc.at[u, 0, self.band(), self.place(i + 1)] if last else at
        return remote(src, at, s["zz_s"].at[u, i], s["zz_r"].at[u, i], peer("seq", self.masks[i]))

    def back_x(self, u, rx):
        s = self.sems
        at = self.final.at[u, self.band()] if self.both is None else self.both.at[:, u, self.band()]
        return remote(at, at, s["xx_s"].at[u, rx - 1], s["xx_r"].at[u, rx - 1], peer("dp", rx))

    def keep(self, u):
        at = self.place(len(self.masks))
        return pltpu.make_async_copy(
            self.acc.at[u, 0, self.band(), at], self.final.at[u, self.band(), at], self.sems["own"].at[u]
        )

    def add(self, target, sources):
        rows = target.shape[0]
        step = 64 if rows % 64 == 0 else 16

        def body(i, carry):
            at = pl.ds(pl.multiple_of(i * step, 16), step)
            total = target[at, :].astype(F32)
            for src in sources:
                total = total + src[at, :].astype(F32)
            target[at, :] = total.astype(BF16)
            return carry

        lax.fori_loop(0, rows // step, body, 0)

    def start_y(self, u):
        for ry in range(1, self.ys):
            self.over_y(u, ry).start()

    def from_y(self, u):
        for ry in range(1, self.ys):
            self.over_y(u, ry).wait_recv()
        self.add(self.acc.at[u, 0], [self.y_in.at[u, ry - 1] for ry in range(1, self.ys)])
        for rx in range(1, self.dp):
            self.over_x(u, rx).start()

    def from_x(self, u):
        for rx in range(1, self.dp):
            self.over_x(u, rx).wait_recv()
        self.add(self.acc.at[u, 0, self.band()], [self.x_in.at[u, rx - 1] for rx in range(1, self.dp)])
        self.over_z(u, 0).start()

    def from_z(self, i, u):
        self.over_z(u, i).wait_recv()
        self.add(self.acc.at[u, 0, self.band(), self.place(i + 1)], [self.z_in[i].at[u]])
        if i + 1 < len(self.masks):
            self.over_z(u, i + 1).start()
        else:
            self.keep(u).start()
            self.back_z(u, i).start()

    def back_from_z(self, i, u):
        if i == len(self.masks) - 1:
            self.keep(u).wait()
        self.back_z(u, i).wait_recv()
        if i:
            self.back_z(u, i - 1).start()
        elif self.both is not None:
            self.pair(u).start()
        else:
            for rx in range(1, self.dp):
                self.back_x(u, rx).start()

    def pair(self, u):
        at = self.final.at[u, self.band()]
        return remote(at, at, self.sems["pair_s"].at[u], self.sems["pair_r"].at[u], peer("seq", 1))

    def from_pair(self, u):
        self.pair(u).wait_recv()
        for rx in range(1, self.dp):
            self.back_x(u, rx).start()

    def back_from_x(self, u):
        for rx in range(1, self.dp):
            self.back_x(u, rx).wait_recv()

    def drain(self, u):
        for ry in range(1, self.ys):
            self.over_y(u, ry).wait_send()
        for rx in range(1, self.dp):
            self.over_x(u, rx).wait_send()
            self.back_x(u, rx).wait_send()
        for i in range(len(self.masks)):
            self.over_z(u, i).wait_send()
            self.back_z(u, i).wait_send()
        if self.both is not None:
            self.pair(u).wait_send()


def partners(fsdp, dp):
    return (
        [peer("fsdp", 1)]
        + [peer("fsdp", 2 * ry) for ry in range(1, fsdp // 2)]
        + [peer("dp", rx) for rx in range(1, dp)]
        + [peer("seq", m) for m in (1, 2, 3)]
    )


def doublings(fsdp, dp, seq):
    steps = []
    for axis, size in (("fsdp", fsdp), ("dp", dp), ("seq", seq)):
        m = 1
        while m < size:
            steps.append((axis, m))
            m *= 2
    return steps


def rear_body(
    caps, starts, act_t, g_feed, two_t, slope, wd, wu, wo, middle, branch, upstream, mixed_own, other,
    q, k, v, mixed, kp, vp, lse, w, n_t, np_t, tokens, theirs, padx, gains, edges3,
    final_a, final_b, grad_in, sums, g_mid,
    *rest, fsdp, dp, seq
):
    size_a, size_b = Lane.size((1, 2)), Lane.size((2,))
    a = Lane(rest[:size_a], final_a, fsdp, dp, (1, 2))
    rest = rest[size_a:]
    parity = lax.axis_index("seq") % 2
    b = Lane(rest[:size_b], final_b.at[parity], fsdp, dp, (2,), final_b)
    (
        ring, ring_b, do, dq, dk, dv, dkp, dvp, dk_sum, dv_sum, edges0,
        g_out, g_in, gp_out, gp_in, run, got, d_send, edges12,
        load, tiles_l, blocks_l, mid_s, d_s, d_r, gs_s, gs_r, gp_s, gp_r, e_s, e_r,
    ) = rest[size_b:]
    f, s = lax.axis_index("fsdp"), lax.axis_index("seq")
    local, d = tokens.shape
    half = d // 2
    ys = fsdp // 2
    rows = a.rows
    mate = peer("seq", 1)
    bounds = slot_bounds(caps, starts)
    greet(partners(fsdp, dp))

    my_rows = pl.ds(pl.multiple_of(parity * local, 128), local)
    give = remote(d_send, do.at[my_rows], d_s.at[0], d_r.at[0], mate)

    def shard(r):
        return r ^ f

    def band(r):
        return pl.ds(pl.multiple_of(shard(r) * rows, 16), rows)

    def give_and_take(c, first, make):
        @pl.when(c < PIECES)
        def _():
            u = first + c
            slot = ring.at[u % 4]
            if first:
                a.core(u - 4, slot).wait_send()
            for ry in range(ys):
                slot[ry] = make(c, 2 * ry + 1).astype(BF16)
            a.core(u, slot).start()

        @pl.when(c >= 1)
        def _():
            u = first + c - 1
            a.core(u, ring.at[u % 4]).wait_recv()
            for ry in range(ys):
                a.acc[u, ry] = (make(c - 1, 2 * ry) + a.acc[u, ry].astype(F32)).astype(BF16)

    def feed_phase(g_v, two_v, hid_v, gbr_v):
        common = [
            pltpu.make_async_copy(g_feed, g_v, load.at[0]),
            pltpu.make_async_copy(two_t, two_v, load.at[1]),
        ]

        def down_phase(act_v):
            def fetch(c):
                return pltpu.make_async_copy(act_t.at[:, c], act_v.at[c], load.at[2 + c])

            for copy in (common[0], fetch(0), fetch(1), common[1], fetch(2), fetch(3)):
                copy.start()
            common[0].wait()

            def step(c, carry):
                @pl.when(c < PIECES)
                def _():
                    fetch(c).wait()

                give_and_take(c, 0, lambda c, r: nn(act_v[c, shard(r)], g_v[...]))

                @pl.when((c >= 1) & (c <= 2))
                def _():
                    a.start_y(c - 1)

                return carry

            lax.fori_loop(0, PIECES + 1, step, 0)
            common[1].wait()

        def back_phase(g_two):
            count = 2 * fsdp
            wide = wd.shape[0] // count
            piece = wide // 2

            def tile_phase(wd_v, wu_v, slope_v):
                def fetch(j, slot):
                    at = pl.ds(pl.multiple_of(j * wide, 128), wide)
                    return [
                        pltpu.make_async_copy(wd.at[at], wd_v.at[slot], tiles_l.at[0, slot]),
                        pltpu.make_async_copy(slope.at[:, at], slope_v.at[slot], tiles_l.at[1, slot]),
                        pltpu.make_async_copy(wu.at[:, at], wu_v.at[slot], tiles_l.at[2, slot]),
                    ]

                for copy in fetch(0, 0):
                    copy.start()

                def step(j, carry):
                    slot = j % 2

                    @pl.when(j + 1 < count)
                    def _():
                        for copy in fetch(j + 1, 1 - slot):
                            copy.start()

                    for copy in fetch(j, slot):
                        copy.wait()
                    h = (nt(g_v[...], wd_v[slot]) * slope_v[slot].astype(F32)).astype(BF16)
                    at = pl.ds(pl.multiple_of(j // 2 * piece, 128), piece)
                    for i in range(2):
                        hid_v[j % 2 * 2 + i, :, at] = h[:, i * piece : (i + 1) * piece]
                    part = nt(h, wu_v[slot])

                    @pl.when(j == 0)
                    def _():
                        g_two[...] = part

                    @pl.when(j != 0)
                    def _():
                        g_two[...] += part

                    @pl.when(j == count // 2)
                    def _():
                        tick(0)

                    return carry

                lax.fori_loop(0, count, step, 0)

            pl.run_scoped(tile_phase, dt((2, wide, d)), dt((2, d, wide)), dt((2, local, wide)))

            def middle_phase(mid_v, br_v, up_v, gm_v, wo_v):
                load_wo = pltpu.make_async_copy(wo, wo_v, load.at[6])
                load_wo.start()

                def fetch(i, slot):
                    at = pl.ds(pl.multiple_of(i * 128, 128), 128)
                    return [
                        pltpu.make_async_copy(middle.at[at], mid_v.at[slot], blocks_l.at[0, slot]),
                        pltpu.make_async_copy(branch.at[at], br_v.at[slot], blocks_l.at[1, slot]),
                        pltpu.make_async_copy(upstream.at[at], up_v.at[slot], blocks_l.at[2, slot]),
                    ]

                def leave(i, slot):
                    at = pl.ds(pl.multiple_of(i * 128, 128), 128)
                    return pltpu.make_async_copy(gm_v.at[slot], g_mid.at[at], mid_s.at[slot])

                count = local // 128
                for copy in fetch(0, 0):
                    copy.start()
                edges12[...] = jnp.zeros_like(edges12)
                tick(1)

                def step(i, carry):
                    slot = i % 2

                    @pl.when(i + 1 < count)
                    def _():
                        for copy in fetch(i + 1, 1 - slot):
                            copy.start()

                    for copy in fetch(i, slot):
                        copy.wait()
                    at = pl.ds(pl.multiple_of(i * 128, 128), 128)
                    g = g_two[at, :]
                    hat, rstd = normalise(mid_v[slot])
                    edges12[2:3, :] += jnp.sum(g * hat, axis=0, keepdims=True)
                    edges12[3:4, :] += jnp.sum(g, axis=0, keepdims=True)
                    gm = up_v[slot].astype(F32) + norm_back(g, hat, rstd, gains[2:3, :])

                    @pl.when(i >= 2)
                    def _():
                        leave(i - 2, slot).wait()

                    gm_v[slot] = gm
                    leave(i, slot).start()
                    hat, rstd = normalise(br_v[slot])
                    edges12[0:1, :] += jnp.sum(gm * hat, axis=0, keepdims=True)
                    edges12[1:2, :] += jnp.sum(gm, axis=0, keepdims=True)
                    gbr_v[at, :] = norm_back(gm, hat, rstd, gains[1:2, :]).astype(BF16)
                    return carry

                lax.fori_loop(0, count, step, 0)
                load_wo.wait()
                grad = gbr_v[...]
                d_send[...] = nt(grad, wo_v[pl.ds(pl.multiple_of((1 - parity) * half, 128), half), :]).astype(BF16)
                give.start()
                do[my_rows, :] = nt(grad, wo_v[pl.ds(pl.multiple_of(parity * half, 128), half), :]).astype(BF16)
                for i in (count - 2, count - 1):
                    leave(i, i % 2).wait()

            pl.run_scoped(
                middle_phase,
                dt((2, 128, d), F32), dt((2, 128, d), F32), dt((2, 128, d)), dt((2, 128, d), F32), dt((d, d)),
            )

        def up_phase(att):
            attn = [
                pltpu.make_async_copy(
                    mixed_own, att.at[:, pl.ds(pl.multiple_of(parity * half, 128), half)], load.at[7]
                ),
                pltpu.make_async_copy(
                    other, att.at[:, pl.ds(pl.multiple_of((1 - parity) * half, 128), half)], load.at[8]
                ),
            ]
            for copy in attn:
                copy.start()

            def step(c, carry):
                give_and_take(c, PIECES, lambda c, r: nn(two_v[band(r), :], hid_v[c]))

                @pl.when(c == 1)
                def _():
                    tick(2)

                return carry

            lax.fori_loop(0, PIECES + 1, step, 0)
            u = 2 * PIECES
            slot = ring.at[u % 4]
            a.core(u - 4, slot).wait_send()
            for copy in attn:
                copy.wait()
            for ry in range(ys):
                slot[ry] = tn(att[:, band(2 * ry + 1)], gbr_v[...]).astype(BF16)
            a.core(u, slot).start()
            for ry in range(ys):
                held = tn(att[:, band(2 * ry)], gbr_v[...])
                if ry == 0:
                    a.core(u, slot).wait_recv()
                a.acc[u, ry] = (held + a.acc[u, ry].astype(F32)).astype(BF16)

        pl.run_scoped(down_phase, dt((PIECES, fsdp, rows, local)))
        pl.run_scoped(back_phase, dt((local, d), F32))
        pl.run_scoped(up_phase, dt((local, d)))

    def starts_of(lane, t):
        if lane is b:
            return (2,) if t == a.count - 1 else ()
        if t < 0 or t + 3 >= a.count:
            return ()
        return (t + 2,) if t < 3 else (t + 2, t + 3) if t == 3 else (t + 3,)

    def tick(t):
        for lane, first in ((a, 0), (b, a.count)):
            for k, stage in enumerate(lane.stages):
                u = t - k - first
                if isinstance(t, int):
                    if 0 <= u < lane.count:
                        stage(u)
                    if k == 0:
                        for other in starts_of(lane, t):
                            lane.start_y(other)
                elif lane is a:

                    @pl.when(u >= 0)
                    def _():
                        stage(u)

                    if k == 0:

                        @pl.when(u + 3 < lane.count)
                        def _():
                            lane.start_y(u + 3)

    first = remote(gp_out, gp_in, gp_s.at[0], gp_r.at[0], mate)
    second = remote(gp_out, gp_in, gp_s.at[0], gp_r.at[0], peer("seq", 3))
    third = remote(gp_in, gp_in, gp_s.at[0], gp_r.at[0], mate)

    def count_edges(g, x):
        hat, _ = normalise(x.astype(F32))
        return jnp.sum(g * hat, axis=0, keepdims=True), jnp.sum(g, axis=0, keepdims=True)

    def attention_phase(q_v, k_v, v_v, o_v, kp_v, vp_v, lse_v, wkv_v, px_v, dq_pad):
        pairs = ((q, q_v), (mixed, o_v), (kp, kp_v), (vp, vp_v), (lse, lse_v), (w.at[:, pl.ds(half, 2 * half)], wkv_v))
        pairs += ((padx, px_v), (k, k_v), (v, v_v))
        copies = [pltpu.make_async_copy(x, y, load.at[9 + i]) for i, (x, y) in enumerate(pairs)]
        for copy in copies:
            copy.start()
        tick(3)
        for copy in copies:
            copy.wait()
        give.wait_recv()

        def views(i):
            lanes = pl.ds(pl.multiple_of(i * 2 * HD, 128), 2 * HD)
            return (
                lanes,
                lambda at: q_v[at, lanes],
                lambda at: o_v[at, lanes],
                lambda h, at: lse_v[i, h : h + 1, at],
                lambda at: do[at, lanes],
            )

        def pad_step(i, carry):
            lanes, q_of, o_of, lse_of, do_of = views(i)

            def put_pad(n, value):
                dq_pad[n, :, lanes] = value

            gk, gv = attend_back_pads(bounds, q_of, kp_v[:, lanes], vp_v[:, lanes], o_of, lse_of, do_of, put_pad)
            dkp[:, lanes] = (gk * 0.125).astype(BF16)
            dvp[:, lanes] = gv.astype(BF16)
            return carry

        lax.fori_loop(0, half // (2 * HD), pad_step, 0)
        g = nt(dkp[...], wkv_v[:, 0:half]) + nt(dvp[...], wkv_v[:, half:])
        gp_out[...] = g.astype(BF16)

        @pl.when(s == 3)
        def _():
            first.start()

        one, two = count_edges(g, px_v[...])
        edges0[0:1, :] = one
        edges0[1:2, :] = two

        def step(i, carry):
            lanes, q_of, o_of, lse_of, do_of = views(i)

            def put(at, value):
                dq[at, lanes] = value

            attend_back_pair(
                bounds,
                q_of,
                lambda at: k_v[at, lanes],
                lambda at: v_v[at, lanes],
                o_of,
                lse_of,
                do_of,
                lambda n: dq_pad[n, :, lanes],
                put,
                dk_sum,
                dv_sum,
            )
            dk[:, lanes] = (dk_sum[...] * 0.125).astype(BF16)
            dv[:, lanes] = dv_sum[...].astype(BF16)
            tick(i + 4)

            @pl.when((s == 2) & (i == 1))
            def _():
                first.wait_recv()
                gp_out[...] = (gp_out[...].astype(F32) + gp_in[...].astype(F32)).astype(BF16)
                second.start()

            @pl.when((s == 1) & (i == 3))
            def _():
                second.wait_recv()
                third.start()

            return carry

        lax.fori_loop(0, half // (2 * HD), step, 0)

    steps = doublings(fsdp, dp, seq)

    def double(i):
        axis, m = steps[i]
        return remote(run.at[i], got.at[i], e_s.at[i], e_r.at[i], peer(axis, m))

    def double_start(i):
        double(i).start()

    def double_end(i):
        double(i).wait_recv()
        run[i + 1] = run[i] + got[i]

    def project_phase(w_v, nt_v, npt_v, x_v, y_v, mid_v, own, out_v):
        pairs = ((w, w_v), (theirs, y_v), (n_t, nt_v), (np_t, npt_v), (tokens, x_v), (g_mid, mid_v))
        copies = [pltpu.make_async_copy(x, y, load.at[18 + i]) for i, (x, y) in enumerate(pairs)]
        for copy in copies:
            copy.start()
        gain = gains[0:1, :]
        back_rows = (dq, dk, dv)
        back_pads = (None, dkp, dvp)

        def grad(c, r):
            total = nn(nt_v[band(r), :], back_rows[c][...])
            if c:
                total = total + nn(npt_v[band(r), :], back_pads[c][...])
            return total

        def weight(c):
            return w_v[:, c * half : (c + 1) * half]

        def through(first_row, source, store, edge):
            def body(i, carry):
                at = pl.ds(pl.multiple_of(first_row + i * 128, 128), 128)
                here = pl.ds(pl.multiple_of(i * 128, 128), 128)
                g = nt(dq[at, :], weight(0)) + nt(dk[at, :], weight(1)) + nt(dv[at, :], weight(2))
                store(i, here, g)
                one, two = count_edges(g, source[here, :])
                return carry[0] + one, carry[1] + two

            return lax.fori_loop(0, local // 128, body, edge)

        def pass_rows(i):
            at = pl.ds(pl.multiple_of(i * 128, 128), 128)
            return remote(g_out.at[at], g_in.at[at], gs_s.at[i], gs_r.at[i], mate)

        def store_out(i, at, value):
            g_out[at, :] = value.astype(BF16)
            pass_rows(i).start()

        def store_own(i, at, value):
            own[at, :] = value

        for copy in copies[:2]:
            copy.wait()
        edge = through((1 - parity) * local, y_v, store_out, (edges0[0:1, :], edges0[1:2, :]))
        for copy in copies[2:]:
            copy.wait()
        for c in range(3):
            for ry in range(ys):
                ring_b[c, ry] = grad(c, 2 * ry + 1).astype(BF16)
            b.core(c, ring_b.at[c]).start()
        for c in range(3):
            for ry in range(ys):
                held = grad(c, 2 * ry)
                if ry == 0:
                    b.core(c, ring_b.at[c]).wait_recv()
                b.acc[c, ry] = (held + b.acc[c, ry].astype(F32)).astype(BF16)
        b.start_y(0)
        b.start_y(1)
        tick(8)
        edge = through(parity * local, x_v, store_own, edge)
        order = (edge[0], edges12[0:1, :], edges12[2:3, :], edges3[0:1, :])
        order += (edge[1], edges12[1:2, :], edges12[3:4, :], edges3[1:2, :])
        for i, value in enumerate(order):
            run[0, i : i + 1, :] = value
        leave = pltpu.make_async_copy(out_v, grad_in, load.at[25])

        def finish_rows():
            for i in range(local // 128):
                pass_rows(i).wait_recv()

            @pl.when(s == 1)
            def _():
                third.wait_send()

            @pl.when(s == 0)
            def _():
                third.wait_recv()

            @pl.when(s == 2)
            def _():
                second.wait_send()

            @pl.when(s == 3)
            def _():
                first.wait_send()

            @pl.when(s < 2)
            def _():
                row = lax.broadcasted_iota(jnp.int32, (BLK, 1), 0)
                mine = ((s == 0) & (row < starts[0, 0])) | ((s == 1) & (row >= starts[0, 0] + caps[0, 0]))
                extra = jnp.where(mine, gp_in[...].astype(F32), 0.0)
                at = pl.ds(pl.multiple_of(jnp.where(s == 0, 0, local - BLK), 128), BLK)
                own[at, :] += extra

            def finish(i, carry):
                at = pl.ds(pl.multiple_of(i * 128, 128), 128)
                hat, rstd = normalise(x_v[at, :].astype(F32))
                g = own[at, :] + g_in[at, :].astype(F32)
                out_v[at, :] = (mid_v[at, :] + norm_back(g, hat, rstd, gain)).astype(BF16)
                return carry

            lax.fori_loop(0, local // 128, finish, 0)
            leave.start()

        double_start(0)
        end = max(a.count + len(a.stages), a.count + b.count + len(b.stages))
        pending = 0
        for t in range(9, end):
            tick(t)
            if pending < len(steps):
                double_end(pending)
                pending += 1
                if pending < len(steps):
                    double_start(pending)
            if t == 13:
                finish_rows()
        for i in range(pending, len(steps)):
            double_end(i)
            if i + 1 < len(steps):
                double_start(i + 1)
        last = pltpu.make_async_copy(run.at[len(steps)], sums, load.at[24])
        last.start()

        for i in range(local // 128):
            pass_rows(i).wait_send()
        last.wait()
        leave.wait()

    dt = lambda s, t=BF16: pltpu.VMEM(s, t)
    pl.run_scoped(
        feed_phase,
        dt((local, d)),
        dt((d, local)),
        dt((PIECES, local, d)),
        dt((local, d)),
    )
    pl.run_scoped(
        attention_phase,
        dt(q.shape), dt(k.shape), dt(v.shape), dt(mixed.shape), dt(kp.shape), dt(vp.shape), dt(lse.shape, F32),
        dt((d, 2 * half)), dt(padx.shape), dt((2, BLK, half), F32),
    )
    pl.run_scoped(
        project_phase,
        dt(w.shape), dt(n_t.shape), dt(np_t.shape), dt(tokens.shape), dt(theirs.shape),
        dt(g_mid.shape, F32), dt((local, d), F32), dt((local, d)),
    )
    give.wait_send()
    for u in range(2 * PIECES - 3, 2 * PIECES + 1):
        a.core(u, ring.at[u % 4]).wait_send()
    for u in range(b.count):
        b.core(u, ring_b.at[u]).wait_send()
    for lane in (a, b):
        for u in range(lane.count):
            lane.drain(u)
    for i in range(len(steps)):
        double(i).wait_send()


def rear(caps, starts, arrays, small, sizes):
    fsdp, dp, seq = sizes
    local, d = arrays[1].shape
    half = d // 2
    rows, y = d // fsdp, fsdp // 2
    n = 2 * PIECES + 1
    steps = len(doublings(fsdp, dp, seq))
    dma = pltpu.SemaphoreType.DMA
    vm = pltpu.VMEM
    return pl.pallas_call(
        functools.partial(rear_body, fsdp=fsdp, dp=dp, seq=seq),
        in_specs=[pl.BlockSpec(memory_space=pltpu.SMEM)] * 2
        + [hbm()] * len(arrays)
        + [pl.BlockSpec(memory_space=pltpu.VMEM)] * len(small),
        out_specs=[hbm()] * 5,
        out_shape=[
            shape((n, rows, d), BF16),
            shape((2, 3, rows, half), BF16),
            shape((local, d), BF16),
            shape((8, d), F32),
            shape((local, d), F32),
        ],
        scratch_shapes=Lane.scratch(n, rows, d, fsdp, dp, (1, 2))
        + Lane.scratch(3, rows, half, fsdp, dp, (2,))
        + [vm((4, y, rows, d), BF16), vm((3, y, rows, half), BF16)]
        + [vm((2 * local, half), BF16)] * 4
        + [vm((BLK, half), BF16)] * 2
        + [vm((2 * local, 2 * HD), F32)] * 2
        + [vm((2, d), F32)]
        + [vm((local, d), BF16)] * 2
        + [vm((BLK, d), BF16)] * 2
        + [vm((steps + 1, 8, d), F32), vm((steps, 8, d), F32), vm((local, half), BF16), vm((4, d), F32)]
        + [dma((26,)), dma((3, 2)), dma((3, 2)), dma((2,)), dma((1,)), dma((1,))]
        + [dma((local // 128,))] * 2
        + [dma((1,))] * 2
        + [dma((steps,)), dma((steps,))],
        compiler_params=pltpu.CompilerParams(vmem_limit_bytes=VMEM_LIMIT, collective_id=0, has_side_effects=True),
        cost_estimate=pl.CostEstimate(flops=10**10, bytes_accessed=10**8, transcendentals=0),
    )(caps, starts, *arrays, *small)


def deliver_body(done, done_q, grad_in, sums, qkv, proj, up, down, out, gain, bias, a, b, c_in, s_in, wide, q_wide, load, sem):
    rows, d = a.shape[1:]
    half = b.shape[3]
    loads = [pltpu.make_async_copy(done.at[i], a.at[i], load.at[i]) for i in range(a.shape[0])]
    loads += [
        pltpu.make_async_copy(done_q, b, load.at[9]),
        pltpu.make_async_copy(grad_in, c_in, load.at[10]),
        pltpu.make_async_copy(sums, s_in, load.at[11]),
    ]
    for copy in loads:
        copy.start()
    stores = []

    def store(src, dst):
        copy = pltpu.make_async_copy(src, dst, sem.at[len(stores)])
        copy.start()
        stores.append(copy)

    shards = d // rows
    for i in range(a.shape[0]):
        loads[i].wait()
        wide[i] = a[i].astype(F32)
        if i == 2 * PIECES:
            store(wide.at[i], proj)
        elif i < PIECES:
            store(wide.at[i], down.at[pl.ds(i * rows, rows)])
        else:
            for h in range(shards):
                at = (h * PIECES + i - PIECES) * rows
                store(wide.at[i, :, pl.ds(h * rows, rows)], up.at[:, pl.ds(at, rows)])
    for copy in loads[a.shape[0] :]:
        copy.wait()
    for h in range(2):
        for i in range(3):
            q_wide[h, i] = b[h, i].astype(F32)
            store(q_wide.at[h, i], qkv.at[:, pl.ds((2 * i + h) * half, half)])
    store(c_in, out)
    gain[...] = s_in[0:4, :]
    bias[...] = s_in[4:8, :]
    for copy in stores:
        copy.wait()


def deliver(done, done_q, grad_in, sums, ff):
    n, rows, d = done.shape
    half = done_q.shape[3]
    count = PIECES + PIECES * (d // rows) + 1 + 6 + 1
    vm, dma = pltpu.VMEM, pltpu.SemaphoreType.DMA
    small = pl.BlockSpec(memory_space=pltpu.VMEM)
    return pl.pallas_call(
        deliver_body,
        in_specs=[hbm()] * 4,
        out_specs=[hbm()] * 5 + [small, small],
        out_shape=[
            shape((rows, 6 * half), F32),
            shape((rows, d), F32),
            shape((rows, ff), F32),
            shape((PIECES * rows, d), F32),
            shape(grad_in.shape, BF16),
            shape((4, d), F32),
            shape((4, d), F32),
        ],
        scratch_shapes=[
            vm(done.shape, BF16),
            vm(done_q.shape, BF16),
            vm(grad_in.shape, BF16),
            vm(sums.shape, F32),
            vm(done.shape, F32),
            vm(done_q.shape, F32),
            dma((12,)),
            dma((count,)),
        ],
        compiler_params=pltpu.CompilerParams(vmem_limit_bytes=VMEM_LIMIT),
        cost_estimate=pl.CostEstimate(flops=10**7, bytes_accessed=2 * 10**7, transcendentals=0),
    )(done, done_q, grad_in, sums)


def local(
    tokens, qkv_weight, out_weight, up_weight, down_weight, norm_gain, norm_bias, caption_len, item_start, grad_out
):
    x_tok, up = tokens[0], grad_out[0]
    local_rows, d = x_tok.shape
    fsdp, dp, seq = (lax.axis_size(axis) for axis in ("fsdp", "dp", "seq"))
    ff = up_weight.shape[1]
    (q, k, v, n_t, np_t, kp, vp, w_qkv, mixed, mixed_own, lse, other, theirs, pads, wo, wu, wd) = front(
        caption_len, item_start, x_tok, qkv_weight, out_weight, up_weight, down_weight, norm_gain, norm_bias, fsdp, dp
    )
    (out, g_feed, act_t, slope, two_t, branch, middle, edges3) = forward(
        mixed_own, other, x_tok, up, norm_gain, norm_bias, wo, wu, wd
    )
    done, done_q, grad_in, sums, _ = rear(
        caption_len,
        item_start,
        (
            act_t.reshape(fsdp, PIECES, d // fsdp, local_rows), g_feed, two_t, slope, wd, wu, wo,
            middle, branch, up, mixed_own, other, q, k, v, mixed, kp, vp, lse, w_qkv, n_t, np_t, x_tok, theirs, pads,
        ),
        (norm_gain, edges3),
        (fsdp, dp, seq),
    )
    grad_qkv, grad_proj, grad_up, grad_down, grad_in, grad_gain, grad_bias = deliver(done, done_q, grad_in, sums, ff)
    return (out[None], grad_in[None], grad_qkv, grad_proj, grad_up, grad_down, grad_gain, grad_bias)


def solution(mesh):
    rows = P(("fsdp", "dp"), "seq", None)
    shard = P("fsdp", None)
    items = P(("fsdp", "dp"), None)
    return jax.shard_map(
        local,
        mesh=mesh,
        in_specs=(rows, shard, shard, shard, shard, P(), P(), items, items, rows),
        out_specs=(rows, rows, shard, shard, shard, shard, P(), P()),
        check_vma=False,
    )
```

time: 436 us -> 368 us (0.84)
  Pallas kernels: 401 us -> 364 us
  local copies, waits for them, and re-layouts: 16.6 us -> 0 us
  other arithmetic: 8.75 us -> 0 us
  between operations: 5.65 us -> 0.95 us
    pallas_call x3 -> x2, Pallas kernels: 64.6 us -> 42 us  [the longest x1 33 us: forward(): call(forward_body, (ff // tile,), 0, [once(mixed.shape), once(other.shape...]
    pallas_call x1, Pallas kernels: 248 us -> 232 us  [rear(): pl.pallas_call(functools.partial(rear_body, fsdp=fsdp, dp=dp, seq=seq), i...]
    unnamed x25 -> x0, local copies, waits for them, and re-layouts: 7.65 us -> none
    convert_element_type x3 -> x0, other arithmetic: 7.03 us -> none  [the longest x1 2.5 us: local(): grad_up = jnp.concatenate([done[2 * c + 1][:, h * rows:(h + 1) * rows] fo...]
    slice x5 -> x0, local copies, waits for them, and re-layouts: 6.71 us -> none  [the longest x1 1.45 us: local(): sums[4:8]]
where the time goes in v5:
time: 368 us; the launch traced here: 365 us
  Pallas kernels  364 us (99%)
    pallas_call x1, Pallas kernels, rear(): pl.pallas_call(functools.partial(rear_body, fsdp=fsdp, dp=dp, seq=seq), i...  232 us
    pallas_call x1, Pallas kernels, front(): pl.pallas_call(functools.partial(front_body, fsdp=fsdp, dp=dp), in_specs=...  89.7 us
    pallas_call x1, Pallas kernels, forward(): call(forward_body, (ff // tile,), 0, [once(mixed.shape), once(other.shape...  33 us
    pallas_call x1, Pallas kernels, deliver(): pl.pallas_call(deliver_body, in_specs=[hbm()] * 4, out_specs=[hbm()] * 5...  9.01 us

profile of v5, /device:TPU:0, one launch (start us, length us, event | category | flops | bytes accessed | tf_op | source)
XLA Modules:
  0.0 364.6 jit_solution(6188557110355463766)
XLA Ops:
  0.6 89.7 %shard_map.161 = (bf16[1280,512]{1,0:T(8,128)(2,1)}, bf16[1280,512]{1,0:T(8,128)(2,1)}, bf16[1280,512]{1,0:T(8,128)(2,1)}, bf16[1024,1280]{1,0:T(8,128)(2,1)}, b...) custom-call(s32[1,2]{1,0:T(1,128)} %caps.3, ...), custom_call_target="tpu_custom_call" | custom-call | flops 10000000000 | bytes 100000000 | tf_op jit(solution)/shard_map/pallas_call | solution.py:582
  90.3 33.0 %shard_map.162 = (bf16[640,1024]{1,0:T(8,128)(2,1)}, bf16[640,1024]{1,0:T(8,128)(2,1)}, bf16[4096,640]{1,0:T(8,128)(2,1)}, bf16[640,4096]{1,0:T(8,128)(2,1)}, bf...) custom-call(bf16[640,512]{1,0:T(8,128)(2,1)} %get-tuple-element.44.own.mixed_own, ...), custom_call_target="tpu_custom_call" | custom-call | flops 12079595520 | bytes 40000000 | tf_op jit(solution)/shard_map/pallas_call | solution.py:657
  123.4 231.9 %shard_map.163 = (bf16[9,256,1024]{2,1,0:T(8,128)(2,1)}, bf16[2,3,256,512]{3,2,1,0:T(8,128)(2,1)}, bf16[640,1024]{1,0:T(8,128)(2,1)}, f32[8,1024]{1,0:T(8,128)}, f32[640,1024]{1,0:T(8,128)}) custom-call(s32[1,2]{1,0:T(1,128)} %caps.3, s32[1,2]{1,0:T(1,128)} %starts.3, bf16[4,4,256,640]{3,2,1,0:T(8,128)(2,1)} %bitcast.5, ...), custom_call_target="tpu_custom_call" | custom-call | flops 10000000000 | bytes 100000000 | tf_op jit(solution)/shard_map/pallas_call | solution.py:1433
  355.3 9.0 %shard_map.164 = (f32[256,3072]{1,0:T(8,128)}, f32[256,1024]{1,0:T(8,128)}, f32[256,4096]{1,0:T(8,128)}, f32[1024,1024]{1,0:T(8,128)}, bf16[640,1024]{1,0:T(8,12...) custom-call(bf16[9,256,1024]{2,1,0:T(8,128)(2,1)} %get-tuple-element.69.done, ...), custom_call_target="tpu_custom_call" | custom-call | flops 10000000 | bytes 20000000 | tf_op jit(solution)/shard_map/pallas_call | solution.py:1514

commit v6 on v5

--- a/solution.py
+++ b/solution.py
@@ -652,7 +652,7 @@
 def forward(mixed, other, x, up, gains, biases, wo, wu, wd):
     local, d = x.shape
     half, ff = mixed.shape[1], wu.shape[1]
-    tile = 512
+    tile = 1024
     once = lambda s: pl.BlockSpec(s, lambda *_: (0,) * len(s), pipeline_mode=pl.Buffered(1))
     return call(
         forward_body,
@@ -1299,7 +1299,6 @@
 
         def store_out(i, at, value):
             g_out[at, :] = value.astype(BF16)
-            pass_rows(i).start()
 
         def store_own(i, at, value):
             own[at, :] = value
@@ -1322,6 +1321,7 @@
         b.start_y(0)
         b.start_y(1)
         tick(8)
+        pass_rows(0).start()
         edge = through(parity * local, x_v, store_own, edge)
         order = (edge[0], edges12[0:1, :], edges12[2:3, :], edges3[0:1, :])
         order += (edge[1], edges12[1:2, :], edges12[3:4, :], edges3[1:2, :])
@@ -1372,12 +1372,14 @@
         pending = 0
         for t in range(9, end):
             tick(t)
+            if t - 8 < local // 128:
+                pass_rows(t - 8).start()
             if pending < len(steps):
                 double_end(pending)
                 pending += 1
                 if pending < len(steps):
                     double_start(pending)
-            if t == 13:
+            if t == 15:
                 finish_rows()
         for i in range(pending, len(steps)):
             double_end(i)

time: 368 us -> 357 us (0.970)
  Pallas kernels: 364 us -> 352 us
    pallas_call x1, Pallas kernels: 232 us -> 221 us  [rear(): pl.pallas_call(functools.partial(rear_body, fsdp=fsdp, dp=dp, seq=seq), i...]
where the time goes in v6:
time: 357 us; the launch traced here: 353 us
  Pallas kernels  352 us (99%)
    pallas_call x1, Pallas kernels, rear(): pl.pallas_call(functools.partial(rear_body, fsdp=fsdp, dp=dp, seq=seq), i...  221 us
    pallas_call x1, Pallas kernels, front(): pl.pallas_call(functools.partial(front_body, fsdp=fsdp, dp=dp), in_specs=...  89.7 us
    pallas_call x1, Pallas kernels, forward(): call(forward_body, (ff // tile,), 0, [once(mixed.shape), once(other.shape...  32.5 us
    pallas_call x1, Pallas kernels, deliver(): pl.pallas_call(deliver_body, in_specs=[hbm()] * 4, out_specs=[hbm()] * 5...  9.01 us

profile of v6, /device:TPU:0, one launch (start us, length us, event | category | flops | bytes accessed | tf_op | source)
XLA Modules:
  0.0 353.3 jit_solution(17285202499238360631)
XLA Ops:
  0.6 89.7 %shard_map.161 = (bf16[1280,512]{1,0:T(8,128)(2,1)}, bf16[1280,512]{1,0:T(8,128)(2,1)}, bf16[1280,512]{1,0:T(8,128)(2,1)}, bf16[1024,1280]{1,0:T(8,128)(2,1)}, b...) custom-call(s32[1,2]{1,0:T(1,128)} %caps.3, ...), custom_call_target="tpu_custom_call" | custom-call | flops 10000000000 | bytes 100000000 | tf_op jit(solution)/shard_map/pallas_call | solution.py:582
  90.3 32.5 %shard_map.162 = (bf16[640,1024]{1,0:T(8,128)(2,1)}, bf16[640,1024]{1,0:T(8,128)(2,1)}, bf16[4096,640]{1,0:T(8,128)(2,1)}, bf16[640,4096]{1,0:T(8,128)(2,1)}, bf...) custom-call(bf16[640,512]{1,0:T(8,128)(2,1)} %get-tuple-element.44.own.mixed_own, ...), custom_call_target="tpu_custom_call" | custom-call | flops 12079595520 | bytes 40000000 | tf_op jit(solution)/shard_map/pallas_call | solution.py:657
  122.8 221.2 %shard_map.163 = (bf16[9,256,1024]{2,1,0:T(8,128)(2,1)}, bf16[2,3,256,512]{3,2,1,0:T(8,128)(2,1)}, bf16[640,1024]{1,0:T(8,128)(2,1)}, f32[8,1024]{1,0:T(8,128)}, f32[640,1024]{1,0:T(8,128)}) custom-call(s32[1,2]{1,0:T(1,128)} %caps.3, s32[1,2]{1,0:T(1,128)} %starts.3, bf16[4,4,256,640]{3,2,1,0:T(8,128)(2,1)} %bitcast.5, ...), custom_call_target="tpu_custom_call" | custom-call | flops 10000000000 | bytes 100000000 | tf_op jit(solution)/shard_map/pallas_call | solution.py:1435
  344.0 9.0 %shard_map.164 = (f32[256,3072]{1,0:T(8,128)}, f32[256,1024]{1,0:T(8,128)}, f32[256,4096]{1,0:T(8,128)}, f32[1024,1024]{1,0:T(8,128)}, bf16[640,1024]{1,0:T(8,12...) custom-call(bf16[9,256,1024]{2,1,0:T(8,128)(2,1)} %get-tuple-element.69.done, ...), custom_call_target="tpu_custom_call" | custom-call | flops 10000000 | bytes 20000000 | tf_op jit(solution)/shard_map/pallas_call | solution.py:1516
